TPU v7x, 32 devices: a whole 2x2x4 slice. The times are simulated.
32 devices in a mesh: wide: 8 (over z, y), narrow: 4 (over x, core).
Axes of the slice: x: 2, y: 2, z: 4, core: 2. Of those that a mesh axis runs over, the one named last changes fastest.
Arguments:
- x_lo: bfloat16 [64, 10, 10, 1024], P(('wide', 'narrow')), may hold values from -6 to 6
- x_mid: bfloat16 [64, 14, 14, 1024], P(('wide', 'narrow')), may hold values from -6 to 6
- x_hi: bfloat16 [64, 18, 18, 1024], P(('wide', 'narrow')), may hold values from -6 to 6
- cot_lo: bfloat16 [64, 5, 5, 2048], P(('wide', 'narrow')), may hold values from -6 to 6
- cot_mid: bfloat16 [64, 7, 7, 2048], P(('wide', 'narrow')), may hold values from -6 to 6
- cot_hi: bfloat16 [64, 9, 9, 2048], P(('wide', 'narrow')), may hold values from -6 to 6
- live_counts: int32 [32, 3], P(('wide', 'narrow')), may hold values from 1 to 2, as said below
- slim_master: float32 [12288, 512], P(('wide', 'narrow'))
- broad_master: float32 [2048, 2048], P(('wide', 'narrow'))
- slim_rowstat: float32 [12288], P(('wide', 'narrow')), as said below
- broad_rowstat: float32 [2048], P(('wide', 'narrow')), as said below
- slim_colstat: float32 [4, 512], replicated, as said below
- broad_colstat: float32 [3, 2048], replicated, as said below
- norm_params: float32 [2, 8192], replicated
- norm_moments: float32 [2, 8192], replicated, as said below
Outputs:
- y_lo: bfloat16 [64, 5, 5, 2048], P(('wide', 'narrow'))
- y_mid: bfloat16 [64, 7, 7, 2048], P(('wide', 'narrow'))
- y_hi: bfloat16 [64, 9, 9, 2048], P(('wide', 'narrow'))
- dx_lo: float32 [64, 10, 10, 1024], P(('wide', 'narrow'))
- dx_mid: float32 [64, 14, 14, 1024], P(('wide', 'narrow'))
- dx_hi: float32 [64, 18, 18, 1024], P(('wide', 'narrow'))
- slim_grad: float32 [12288, 512], P(('wide', 'narrow'))
- broad_grad: float32 [2048, 2048], P(('wide', 'narrow'))
- slim_rows_new: float32 [12288], P(('wide', 'narrow'))
- broad_rows_new: float32 [2048], P(('wide', 'narrow'))
- slim_cols_new: float32 [4, 512], replicated
- broad_cols_new: float32 [3, 2048], replicated
- slim_new: float32 [12288, 512], P(('wide', 'narrow'))
- broad_new: float32 [2048, 2048], P(('wide', 'narrow'))
- slim_copy: bfloat16 [12288, 512], P(('wide', 'narrow'))
- broad_copy: bfloat16 [2048, 2048], P(('wide', 'narrow'))
- norm_grad: float32 [2, 8192], replicated
- norm_moments_new: float32 [2, 8192], replicated
- norm_new: float32 [2, 8192], replicated
Inputs may be any that keep to these rules, and one draw needn't show every extreme that they name: Each device uses its first live_counts slots of each resolution; in each column some device has all 2 slots in use. `slim_rowstat`: positive. `broad_rowstat`: positive. `slim_colstat`: positive. `broad_colstat`: positive. `norm_moments`: positive.
All inputs are finite; a program needn't handle non-finite values.
Results may differ from a plain program's by a relative error of at most 0.04.
Values may be sent and summed in bfloat16 or wider, within the bound.
No kernel may reach another device: no remote copies, remote signals or barrier semaphores. Data moves between devices by JAX's collectives and lax.ppermute only.
A program may use at most 256 MiB of HBM per device.

v0:
```python
import jax
import jax.numpy as jnp
from jax import lax
from jax.sharding import PartitionSpec as P

STEP = 10


EPS_NORM = 1e-05
EPS_ONE = 1e-30
EPS_TWO = 0.001
STEP_RATE = 0.3
CLIP_LIMIT = 1.0
PRECISE = lax.Precision.HIGHEST


def contract_rows(first_op, second_op):
    return lax.dot_general(
        first_op, second_op, (((0,), (0,)), ((), ())), preferred_element_type=jnp.float32
    )


def contract_cols(first_op, second_op):
    return lax.dot_general(
        first_op, second_op, (((1,), (1,)), ((), ())), preferred_element_type=jnp.float32
    )


def per_matrix(segment, values):
    return lax.dot_general(
        segment,
        values,
        (((0,), (0,)), ((), ())),
        precision=PRECISE,
        preferred_element_type=jnp.float32,
    )


def silu_slope(argument):
    gate_val = jax.nn.sigmoid(argument)
    return gate_val * (1.0 + argument * (1.0 - gate_val))


def split_flat(flat, images, grid_sizes):
    pieces = []
    offset = 0
    for extent in grid_sizes:
        length = images * extent * extent
        pieces.append(flat[offset : offset + length].reshape(images, extent, extent, flat.shape[1]))
        offset += length
    return pieces


def patches(flat, images, grid_sizes, stride):
    pieces = []
    for block_view in split_flat(flat, images, grid_sizes):
        extent = block_view.shape[1]
        reach = stride * (extent // stride - 1) + 1
        padded = jnp.pad(block_view, ((0, 0), (1, 1), (1, 1), (0, 0)))
        tap_list = [
            padded[:, row_tap : row_tap + reach : stride, col_tap : col_tap + reach : stride, :]
            for row_tap in range(3)
            for col_tap in range(3)
        ]
        joined = jnp.concatenate(tap_list, axis=3)
        pieces.append(joined.reshape(-1, joined.shape[3]))
    return jnp.concatenate(pieces, 0)


def unpatch(flat_grad, images, grid_sizes, stride, channels):
    pieces = []
    offset = 0
    for extent in grid_sizes:
        small_side = extent // stride
        length = images * small_side * small_side
        block_view = flat_grad[offset : offset + length].reshape(
            images, small_side, small_side, 9, channels
        )
        offset += length
        framed = jnp.pad(block_view, ((0, 0), (1, 1), (1, 1), (0, 0), (0, 0)))
        if stride == 1:
            summed = None
            for row_tap in range(3):
                for col_tap in range(3):
                    tap_part = framed[
                        :,
                        2 - row_tap : 2 - row_tap + small_side,
                        2 - col_tap : 2 - col_tap + small_side,
                        3 * row_tap + col_tap,
                        :,
                    ]
                    summed = tap_part if summed is None else summed + tap_part
            pieces.append(summed.reshape(-1, channels))
        else:
            side = small_side + 1
            classes = [[None, None], [None, None]]
            for row_tap in range(3):
                for col_tap in range(3):
                    row_start = 0 if row_tap == 2 else 1
                    col_start = 0 if col_tap == 2 else 1
                    tap_part = framed[
                        :,
                        row_start : row_start + side,
                        col_start : col_start + side,
                        3 * row_tap + col_tap,
                        :,
                    ]
                    row_par = row_tap % 2
                    col_par = col_tap % 2
                    if classes[row_par][col_par] is None:
                        classes[row_par][col_par] = tap_part
                    else:
                        classes[row_par][col_par] = classes[row_par][col_par] + tap_part
            row_sets = [
                jnp.stack([classes[row_par][0], classes[row_par][1]], 3) for row_par in range(2)
            ]
            woven = jnp.stack(row_sets, 2).reshape(images, 2 * side, 2 * side, channels)
            pieces.append(woven[:, 1 : extent + 1, 1 : extent + 1, :].reshape(-1, channels))
    return jnp.concatenate(pieces, 0)


def subsample(flat, images, grid_sizes):
    pieces = [
        block_view[:, ::2, ::2, :].reshape(-1, flat.shape[1])
        for block_view in split_flat(flat, images, grid_sizes)
    ]
    return jnp.concatenate(pieces, 0)


def upsample(flat_grad, images, grids_out):
    pieces = []
    for block_view in split_flat(flat_grad, images, grids_out):
        side = block_view.shape[1]
        empty = jnp.zeros_like(block_view)
        across = jnp.stack([block_view, empty], 3).reshape(
            images, side, 2 * side, flat_grad.shape[1]
        )
        placed = jnp.stack([across, jnp.zeros_like(across)], 2).reshape(
            images, 2 * side, 2 * side, flat_grad.shape[1]
        )
        pieces.append(placed.reshape(-1, flat_grad.shape[1]))
    return jnp.concatenate(pieces, 0)


def group_stats(stacked, mask_in):
    weighted = stacked * mask_in[None, :, None]
    first_sum, second_sum, count_all = (
        lax.psum(jnp.sum(weighted, 1).astype(jnp.bfloat16), "narrow").astype(jnp.float32),
        lax.psum(jnp.sum(weighted * stacked, 1).astype(jnp.bfloat16), "narrow").astype(jnp.float32),
        lax.psum(jnp.sum(mask_in).astype(jnp.bfloat16), "narrow").astype(jnp.float32),
    )
    mean_val = first_sum / count_all
    inv_std = lax.rsqrt(second_sum / count_all - mean_val * mean_val + EPS_NORM)
    return (mean_val[:, None, :], inv_std[:, None, :], count_all)


def norm_backward(gradient, normed, mask_in, inv_std, gain_vec, count_all):
    masked = gradient * mask_in[None, :, None]
    shift_term = jnp.sum(masked, 1)
    gain_term = jnp.sum(masked * normed, 1)
    total_shift, total_gain = (
        lax.psum(shift_term.astype(jnp.bfloat16), "narrow").astype(jnp.float32),
        lax.psum(gain_term.astype(jnp.bfloat16), "narrow").astype(jnp.float32),
    )
    centred = gradient - mask_in[None, :, None] * (
        total_shift[:, None, :] / count_all + normed * total_gain[:, None, :] / count_all
    )
    return ((gain_vec * inv_std * centred).astype(jnp.bfloat16), gain_term, shift_term)


def segment_table(row_count, place, bounds):
    row_index = place * row_count + jnp.arange(row_count)
    return jnp.stack(
        [
            ((row_index >= bounds[level]) & (row_index < bounds[level + 1])).astype(jnp.float32)
            for level in range(len(bounds) - 1)
        ],
        1,
    )


def prepare(gradient, master, rowstat, segment, decay_rate):
    grad_sq = gradient * gradient + EPS_ONE
    rows_new = decay_rate * rowstat + (1.0 - decay_rate) * jnp.mean(grad_sq, 1)
    return (
        rows_new,
        per_matrix(segment, grad_sq),
        per_matrix(segment, rows_new),
        per_matrix(segment, jnp.sum(master * master, 1)),
    )


def renew_columns(col_old, col_sum, row_sum, heights, decay_rate):
    cols_new = decay_rate * col_old + (1.0 - decay_rate) * col_sum / heights[:, None]
    return (cols_new, row_sum / heights)


def direction(gradient, rows_new, segment, cols_new, row_mean):
    second = rows_new[:, None] * jnp.dot(segment, cols_new / row_mean[:, None], precision=PRECISE)
    return gradient * lax.rsqrt(second)


def renew_weights(master, update, segment, update_sq, weight_sum, heights, columns):
    cell_count = heights * columns
    update_rms = jnp.sqrt(update_sq / cell_count)
    weight_rms = jnp.sqrt(weight_sum / cell_count)
    step_size = (
        STEP_RATE * jnp.maximum(EPS_TWO, weight_rms) / jnp.maximum(1.0, update_rms / CLIP_LIMIT)
    )
    return master - jnp.dot(segment, step_size, precision=PRECISE)[:, None] * update


def body(
    x_lo,
    x_mid,
    x_hi,
    cot_lo,
    cot_mid,
    cot_hi,
    live_counts,
    slim_master,
    broad_master,
    slim_rowstat,
    broad_rowstat,
    slim_colstat,
    broad_colstat,
    norm_params,
    norm_moments,
):
    images = x_lo.shape[0]
    grid_sizes = (x_lo.shape[1], x_mid.shape[1], x_hi.shape[1])
    grids_out = tuple((extent // 2 for extent in grid_sizes))
    width_in = x_lo.shape[3]
    width_mid = slim_master.shape[1]
    width_out = broad_master.shape[1]
    slim_full, broad_full = (
        lax.all_gather(slim_master.astype(jnp.bfloat16), ("wide", "narrow"), axis=0, tiled=True),
        lax.all_gather(broad_master.astype(jnp.bfloat16), ("wide", "narrow"), axis=0, tiled=True),
    )
    bound_two = width_in + 9 * width_mid
    bound_three = bound_two + width_out
    w_one = slim_full[:width_in]
    w_two = slim_full[width_in:bound_two]
    w_four = slim_full[bound_two:bound_three]
    w_five = slim_full[bound_three:]
    w_three = broad_full[:width_mid]
    w_side = broad_full[width_mid : width_mid + width_in]
    w_six = broad_full[width_mid + width_in :]
    widths = (width_mid, width_mid, width_out, width_out, width_mid, width_mid, width_out)
    starts = [sum(widths[:level]) for level in range(8)]
    gain_list = [norm_params[0, starts[level] : starts[level + 1]] for level in range(7)]
    shifts = [norm_params[1, starts[level] : starts[level + 1]] for level in range(7)]
    alive_now = live_counts[0]
    alive_list = [(jnp.arange(images) < alive_now[level]).astype(jnp.float32) for level in range(3)]
    mask_in = jnp.concatenate(
        [jnp.repeat(alive_list[level], grid_sizes[level] * grid_sizes[level]) for level in range(3)]
    )
    mask_out = jnp.concatenate(
        [jnp.repeat(alive_list[level], grids_out[level] * grids_out[level]) for level in range(3)]
    )
    x_flat = jnp.concatenate(
        [x_lo.reshape(-1, width_in), x_mid.reshape(-1, width_in), x_hi.reshape(-1, width_in)], 0
    )
    x_sub = subsample(x_flat, images, grid_sizes)
    z_one = jnp.dot(x_flat, w_one, preferred_element_type=jnp.float32)
    mean_one, inv_one, count_in = group_stats(z_one[None], mask_in)
    normed_one = ((z_one[None] - mean_one) * inv_one)[0]
    pre_one = gain_list[0] * normed_one + shifts[0]
    act_one = jax.nn.silu(pre_one).astype(jnp.bfloat16)
    patch_two = patches(act_one, images, grid_sizes, 2)
    z_two = jnp.dot(patch_two, w_two, preferred_element_type=jnp.float32)
    mean_two, inv_two, count_out = group_stats(z_two[None], mask_out)
    normed_two = ((z_two[None] - mean_two) * inv_two)[0]
    pre_two = gain_list[1] * normed_two + shifts[1]
    act_two = jax.nn.silu(pre_two).astype(jnp.bfloat16)
    z_three = jnp.dot(act_two, w_three, preferred_element_type=jnp.float32)
    z_side = jnp.dot(x_sub, w_side, preferred_element_type=jnp.float32)
    stacked = jnp.stack([z_three, z_side])
    mean_pair, inv_pair, unused_count = group_stats(stacked, mask_out)
    normed_pair = (stacked - mean_pair) * inv_pair
    pre_mid = gain_list[2] * normed_pair[0] + shifts[2] + gain_list[3] * normed_pair[1] + shifts[3]
    hidden = jax.nn.silu(pre_mid)
    hidden_low = hidden.astype(jnp.bfloat16)
    z_four = jnp.dot(hidden_low, w_four, preferred_element_type=jnp.float32)
    mean_four, inv_four, unused_four = group_stats(z_four[None], mask_out)
    normed_four = ((z_four[None] - mean_four) * inv_four)[0]
    pre_four = gain_list[4] * normed_four + shifts[4]
    act_four = jax.nn.silu(pre_four).astype(jnp.bfloat16)
    patch_five = patches(act_four, images, grids_out, 1)
    z_five = jnp.dot(patch_five, w_five, preferred_element_type=jnp.float32)
    mean_five, inv_five, unused_five = group_stats(z_five[None], mask_out)
    normed_five = ((z_five[None] - mean_five) * inv_five)[0]
    pre_five = gain_list[5] * normed_five + shifts[5]
    act_five = jax.nn.silu(pre_five).astype(jnp.bfloat16)
    z_six = jnp.dot(act_five, w_six, preferred_element_type=jnp.float32)
    mean_six, inv_six, unused_six = group_stats(z_six[None], mask_out)
    normed_six = ((z_six[None] - mean_six) * inv_six)[0]
    pre_out = gain_list[6] * normed_six + shifts[6] + hidden
    result = jax.nn.silu(pre_out)
    cot_flat = (
        jnp.concatenate(
            [
                cot_lo.reshape(-1, width_out),
                cot_mid.reshape(-1, width_out),
                cot_hi.reshape(-1, width_out),
            ],
            0,
        ).astype(jnp.float32)
        * mask_out[:, None]
    )
    grad_out = cot_flat * silu_slope(pre_out)
    dz_six, dg_six, db_six = norm_backward(
        grad_out[None], normed_six[None], mask_out, inv_six, gain_list[6], count_out
    )
    dz_six = dz_six[0]
    grad_w_six = contract_rows(act_five, dz_six)
    grad_five = contract_cols(dz_six, w_six) * silu_slope(pre_five)
    dz_five, dg_five, db_five = norm_backward(
        grad_five[None], normed_five[None], mask_out, inv_five, gain_list[5], count_out
    )
    dz_five = dz_five[0]
    grad_w_five = contract_rows(patch_five, dz_five)
    grad_four = unpatch(
        contract_cols(dz_five, w_five), images, grids_out, 1, width_mid
    ) * silu_slope(pre_four)
    dz_four, dg_four, db_four = norm_backward(
        grad_four[None], normed_four[None], mask_out, inv_four, gain_list[4], count_out
    )
    dz_four = dz_four[0]
    grad_w_four = contract_rows(hidden_low, dz_four)
    grad_hidden = grad_out + contract_cols(dz_four, w_four)
    grad_mid = grad_hidden * silu_slope(pre_mid)
    gain_pair = jnp.stack([gain_list[2], gain_list[3]])[:, None, :]
    dz_pair, dg_pair, db_pair = norm_backward(
        grad_mid[None], normed_pair, mask_out, inv_pair, gain_pair, count_out
    )
    grad_w_three = contract_rows(act_two, dz_pair[0])
    grad_w_side = contract_rows(x_sub, dz_pair[1])
    grad_two = contract_cols(dz_pair[0], w_three) * silu_slope(pre_two)
    grad_sub = contract_cols(dz_pair[1], w_side)
    dz_two, dg_two, db_two = norm_backward(
        grad_two[None], normed_two[None], mask_out, inv_two, gain_list[1], count_out
    )
    dz_two = dz_two[0]
    grad_w_two = contract_rows(patch_two, dz_two)
    grad_one = unpatch(contract_cols(dz_two, w_two), images, grid_sizes, 2, width_mid) * silu_slope(
        pre_one
    )
    dz_one, dg_one, db_one = norm_backward(
        grad_one[None], normed_one[None], mask_in, inv_one, gain_list[0], count_in
    )
    dz_one = dz_one[0]
    grad_w_one = contract_rows(x_flat, dz_one)
    grad_x = contract_cols(dz_one, w_one) + upsample(grad_sub, images, grids_out)
    y_parts = split_flat(result.astype(jnp.bfloat16), images, grids_out)
    dx_parts = split_flat(grad_x, images, grid_sizes)
    gain_local = jnp.concatenate(
        [dg_one[0], dg_two[0], dg_pair[0], dg_pair[1], dg_four[0], dg_five[0], dg_six[0]]
    )
    shift_local = jnp.concatenate(
        [db_one[0], db_two[0], db_pair[0], db_pair[0], db_four[0], db_five[0], db_six[0]]
    )
    norm_term = jnp.stack([gain_local, shift_local])
    slim_term = jnp.concatenate([grad_w_one, grad_w_two, grad_w_four, grad_w_five], 0)
    broad_term = jnp.concatenate([grad_w_three, grad_w_side, grad_w_six], 0)
    slim_grad, broad_grad = (
        lax.psum_scatter(slim_term, ("wide", "narrow"), scatter_dimension=0, tiled=True),
        lax.psum_scatter(broad_term, ("wide", "narrow"), scatter_dimension=0, tiled=True),
    )
    decay_rate = 1.0 - STEP ** (-0.8)
    place = lax.axis_index(("wide", "narrow"))
    slim_bounds = (0, width_in, bound_two, bound_three, bound_three + 9 * width_mid)
    broad_bounds = (0, width_mid, width_mid + width_in, 2 * width_mid + width_in)
    slim_heights = jnp.array([width_in, 9 * width_mid, width_out, 9 * width_mid], jnp.float32)
    broad_heights = jnp.array([width_mid, width_in, width_mid], jnp.float32)
    slim_segment = segment_table(slim_grad.shape[0], place, slim_bounds)
    broad_segment = segment_table(broad_grad.shape[0], place, broad_bounds)
    slim_rows_new, slim_col_part, slim_row_part, slim_weight_part = prepare(
        slim_grad, slim_master, slim_rowstat, slim_segment, decay_rate
    )
    broad_rows_new, broad_col_part, broad_row_part, broad_weight_part = prepare(
        broad_grad, broad_master, broad_rowstat, broad_segment, decay_rate
    )
    (
        slim_col_sum,
        broad_col_sum,
        slim_row_sum,
        broad_row_sum,
        slim_weight_sum,
        broad_weight_sum,
        norm_grad,
    ) = lax.psum(
        (
            slim_col_part,
            broad_col_part,
            slim_row_part,
            broad_row_part,
            slim_weight_part,
            broad_weight_part,
            norm_term,
        ),
        ("wide", "narrow"),
    )
    slim_cols_new, slim_mean = renew_columns(
        slim_colstat, slim_col_sum, slim_row_sum, slim_heights, decay_rate
    )
    broad_cols_new, broad_mean = renew_columns(
        broad_colstat, broad_col_sum, broad_row_sum, broad_heights, decay_rate
    )
    slim_update = direction(slim_grad, slim_rows_new, slim_segment, slim_cols_new, slim_mean)
    broad_update = direction(broad_grad, broad_rows_new, broad_segment, broad_cols_new, broad_mean)
    slim_update_sq, broad_update_sq = lax.psum(
        (
            per_matrix(slim_segment, jnp.sum(slim_update * slim_update, 1)),
            per_matrix(broad_segment, jnp.sum(broad_update * broad_update, 1)),
        ),
        ("wide", "narrow"),
    )
    slim_new = renew_weights(
        slim_master,
        slim_update,
        slim_segment,
        slim_update_sq,
        slim_weight_sum,
        slim_heights,
        width_mid,
    )
    broad_new = renew_weights(
        broad_master,
        broad_update,
        broad_segment,
        broad_update_sq,
        broad_weight_sum,
        broad_heights,
        width_out,
    )
    norm_moments_new = decay_rate * norm_moments + (1.0 - decay_rate) * (
        norm_grad * norm_grad + EPS_ONE
    )
    norm_update = norm_grad * lax.rsqrt(norm_moments_new)
    update_rms = jnp.sqrt(jnp.mean(norm_update * norm_update, 1))
    weight_rms = jnp.sqrt(jnp.mean(norm_params * norm_params, 1))
    norm_new = (
        norm_params
        - (
            STEP_RATE * jnp.maximum(EPS_TWO, weight_rms) / jnp.maximum(1.0, update_rms / CLIP_LIMIT)
        )[:, None]
        * norm_update
    )
    return (
        y_parts[0],
        y_parts[1],
        y_parts[2],
        dx_parts[0],
        dx_parts[1],
        dx_parts[2],
        slim_grad,
        broad_grad,
        slim_rows_new,
        broad_rows_new,
        slim_cols_new,
        broad_cols_new,
        slim_new,
        broad_new,
        slim_new.astype(jnp.bfloat16),
        broad_new.astype(jnp.bfloat16),
        norm_grad,
        norm_moments_new,
        norm_new,
    )


def solution(mesh):
    in_specs = (
        P(("wide", "narrow"), None, None, None),
        P(("wide", "narrow"), None, None, None),
        P(("wide", "narrow"), None, None, None),
        P(("wide", "narrow"), None, None, None),
        P(("wide", "narrow"), None, None, None),
        P(("wide", "narrow"), None, None, None),
        P(("wide", "narrow"), None),
        P(("wide", "narrow"), None),
        P(("wide", "narrow"), None),
        P(("wide", "narrow")),
        P(("wide", "narrow")),
        P(),
        P(),
        P(),
        P(),
    )
    out_specs = (
        P(("wide", "narrow"), None, None, None),
        P(("wide", "narrow"), None, None, None),
        P(("wide", "narrow"), None, None, None),
        P(("wide", "narrow"), None, None, None),
        P(("wide", "narrow"), None, None, None),
        P(("wide", "narrow"), None, None, None),
        P(("wide", "narrow"), None),
        P(("wide", "narrow"), None),
        P(("wide", "narrow")),
        P(("wide", "narrow")),
        P(),
        P(),
        P(("wide", "narrow"), None),
        P(("wide", "narrow"), None),
        P(("wide", "narrow"), None),
        P(("wide", "narrow"), None),
        P(),
        P(),
        P(),
    )
    return jax.shard_map(body, mesh=mesh, in_specs=in_specs, out_specs=out_specs, check_vma=False)
```

profile of v0, /device:TPU:0, one launch (start us, length us, event | category | flops | bytes accessed | tf_op | source)
XLA Modules:
  0.0 1386.2 jit_solution(10009503388430472186)
XLA Ops:
  52.8 38.9 %all-gather.5.cloned.1.call-done = bf16[2048,2048]{1,0:T(8,128)(2,1)} async-done(((bf16[64,2048]{1,0:T(8,128)(2,1)}), bf16[2048,2048]{1,0:T(8,128)(2,1)}) %all-gather.5.cloned.1.call-update) | async-done | bytes 8388624 | tf_op jit(solution)/shard_map/all_gather | solution.py:238
  95.4 94.3 %all-gather.3.cloned.1.call-done = bf16[12288,512]{1,0:T(8,128)(2,1)} async-done(((bf16[384,512]{1,0:T(8,128)(2,1)}), bf16[12288,512]{1,0:T(8,128)(2,1)}) %all-gather.3.cloned.1.call-update) | async-done | bytes 12582928 | tf_op jit(solution)/shard_map/all_gather | solution.py:237
  194.8 7.8 all-reduce.31
  375.1 6.6 all-reduce.30
  386.6 10.1 all-reduce.29
  404.2 6.1 all-reduce.28
  505.8 6.3 all-reduce.27
  517.2 10.2 all-reduce.26
  527.5 6.6 multiply_reduce_fusion.4
  537.6 10.1 all-reduce.25
  577.0 10.7 fusion.76
  592.7 8.1 fusion.91
  614.9 7.1 all-reduce.23
  624.7 7.3 fusion.148
  633.0 10.4 all-reduce.22
  682.3 12.0 fusion.64
  717.2 6.3 all-reduce.20
  728.9 22.8 %pad_maximum_fusion = f32[12288,512]{1,0:T(8,128)} fusion(f32[4608,512]{1,0:T(8,128)} %fusion.50, f32[2048,512]{1,0:T(8,128)} %fusion.38, f32[4608,512]{1,0:T(8,128)} %fusion.51, f32[1024,512]{1,0:T(8,128)S(1)} %fusion.153), kind=kLoop, calls=%fused_computation | loop fusion | flops 18874368 | bytes 50331648 | tf_op jit(solution)/shard_map/concatenate | solution.py:364
  759.5 6.7 pad_maximum_fusion.1
  812.9 31.9 %all-reduce.34.cloned.1.call-done = f32[2,8192]{1,0:T(2,128)} async-done(((f32[2,8192]{1,0:T(2,128)}), f32[2,8192]{1,0:T(2,128)}) %all-reduce.34.cloned.1.call-update) | async-done | bytes 65552 | tf_op jit(solution)/shard_map/psum | solution.py:392
  847.0 250.9 %reduce-scatter.3.cloned.1.call-done = f32[384,512]{1,0:T(8,128)} async-done(((f32[12288,512]{1,0:T(8,128)}), f32[384,512]{1,0:T(8,128)}) %reduce-scatter.3.cloned.1.call-update) | async-done | bytes 786448 | tf_op jit(solution)/shard_map/reduce_scatter | solution.py:367
  1100.2 182.9 %reduce-scatter.5.cloned.1.call-done = f32[64,2048]{1,0:T(8,128)} async-done(((f32[2048,2048]{1,0:T(8,128)}), f32[64,2048]{1,0:T(8,128)}) %reduce-scatter.5.cloned.1.call-update) | async-done | bytes 524304 | tf_op jit(solution)/shard_map/reduce_scatter | solution.py:368
  1288.1 43.3 %all-reduce.19 = (f32[4,512]{1,0:T(4,128)S(1)}, f32[3,2048]{1,0:T(4,128)}, f32[4]{0:T(128)S(1)}, f32[3]{0:T(128)}) all-reduce(f32[4,512]{1,0:T(4,128)S(1)} %fusion.55, f32[3,2048]{1,0:T(4,128)S(1)} %fusion.60, f32[4]{0:T(128)S(1)} %convolution_bitcast_fusion.6, ...), channel_id=1, replica_groups=mesh['wide'=8,'narrow'=4] {'wide','narrow'}, use_global_device_ids=true, to_apply=%region_60.61 | all-reduce | flops 8199 | bytes 65592 | tf_op jit(solution)/shard_map/psum | solution.py:392
  1336.9 38.6 %all-reduce.18 = (f32[4]{0:T(128)S(1)}, f32[4]{0:T(128)S(1)}, f32[3]{0:T(128)S(1)}, f32[3]{0:T(128)S(1)}) all-reduce(f32[4]{0:T(128)S(1)} %convolution_bitcast_fusion.5, f32[4]{0:T(128)} %convolution_bitcast_fusion.7, f32[3]{0:T(128)S(1)} %convolution_bitcast_fusion.2, ...), channel_id=1, replica_groups=mesh['wide'=8,'narrow'=4] {'wide','narrow'}, use_global_device_ids=true, to_apply=%region_66.67 | all-reduce | flops 14 | bytes 112 | tf_op jit(solution)/shard_map/psum | solution.py:412
  (731 shorter events, 528.2 us)
Async XLA Ops:
  7.2 84.5 %all-gather.5.cloned.1.call-start = ((), (), s32[]{:S(2)}) async-start(), calls=%async_computation.3 | async-start | bytes 8650752 | tf_op jit(solution)/shard_map/all_gather | solution.py:238
  9.9 179.7 %all-gather.3.cloned.1.call-start = ((), (), s32[]{:S(2)}) async-start(), calls=%async_computation.2 | async-start | bytes 12976128 | tf_op jit(solution)/shard_map/all_gather | solution.py:237
  12.9 831.9 %all-reduce.34.cloned.1.call-start = ((), (), s32[]{:S(2)}) async-start(), calls=%async_computation.6 | async-start | bytes 131072 | tf_op jit(solution)/shard_map/psum | solution.py:392
  34.7 56.9 %copy-start.46 = (bf16[50,1024]{1,0:T(8,128)(2,1)}, bf16[50,1024]{1,0:T(8,128)(2,1)S(1)}, u32[]{:S(2)}) copy-start(bf16[50,1024]{1,0:T(8,128)(2,1)S(1)} %reshape.1187) | copy-start | bytes 307204
  48.5 141.2 %copy-start.71 = (f32[1240]{0:T(1024)}, f32[1240]{0:T(1024)S(1)}, u32[]{:S(2)}) copy-start(f32[1240]{0:T(1024)S(1)} %concatenate.131) | copy-start | bytes 14884
  52.1 151.1 %copy-start.94 = (f32[1,512]{1,0:T(1,128)}, f32[1,512]{1,0:T(1,128)S(1)}, u32[]{:S(2)}) copy-start(f32[1,512]{1,0:T(1,128)S(1)} %get-tuple-element.245) | copy-start | bytes 6148
  52.1 151.1 %copy-start.100 = (f32[1,512]{1,0:T(1,128)}, f32[1,512]{1,0:T(1,128)S(1)}, u32[]{:S(2)}) copy-start(f32[1,512]{1,0:T(1,128)S(1)} %get-tuple-element.244) | copy-start | bytes 6148
  52.1 330.3 %copy-start.124 = (f32[1,512]{1,0:T(1,128)}, f32[1,512]{1,0:T(1,128)S(1)}, u32[]{:S(2)}) copy-start(f32[1,512]{1,0:T(1,128)S(1)} %get-tuple-element.246) | copy-start | bytes 6148
  728.8 369.1 %reduce-scatter.3.cloned.1.call-start = ((), (), s32[]{:S(2)}) async-start(), calls=%async_computation.4 | async-start | bytes 25952256 | tf_op jit(solution)/shard_map/reduce_scatter | solution.py:367
  751.8 531.3 %reduce-scatter.5.cloned.1.call-start = ((), (), s32[]{:S(2)}) async-start(), calls=%async_computation.5 | async-start | bytes 17301504 | tf_op jit(solution)/shard_map/reduce_scatter | solution.py:368
  766.9 519.8 %copy-start.140 = (pred[64,3]{0,1:T(4,128)(4,1)}, pred[64,3]{0,1:T(4,128)(4,1)S(1)}, u32[]{:S(2)}) copy-start(pred[64,3]{0,1:T(4,128)(4,1)S(1)} %pad_add_fusion.1) | copy-start | bytes 580
  812.9 518.5 %copy-start.151 = (f32[4]{0:T(128)S(1)}, f32[4]{0:T(128)}, u32[]{:S(2)}) copy-start(f32[4]{0:T(128)} %constant.153) | copy-start | bytes 52
  812.9 518.5 %copy-start.123 = (f32[4,512]{1,0:T(4,128)S(1)}, f32[4,512]{1,0:T(4,128)}, u32[]{:S(2)}) copy-start(f32[4,512]{1,0:T(4,128)} %param.28) | copy-start | bytes 24580
  1097.9 233.5 %copy-start.6 = (f32[384,512]{1,0:T(8,128)S(1)}, f32[384,512]{1,0:T(8,128)}, u32[]{:S(2)}) copy-start(f32[384,512]{1,0:T(8,128)} %reduce-scatter.3.cloned.1.call-done) | copy-start | bytes 2359300
  1099.3 236.0 %copy-start.41 = (f32[2,8192]{1,0:T(2,128)S(1)}, f32[2,8192]{1,0:T(2,128)}, u32[]{:S(2)}) copy-start(f32[2,8192]{1,0:T(2,128)} %all-reduce.34.cloned.1.call-done) | copy-start | bytes 196612
  1099.3 236.0 %copy-start.44 = (f32[2,8192]{1,0:T(2,128)S(1)}, f32[2,8192]{1,0:T(2,128)}, u32[]{:S(2)}) copy-start(f32[2,8192]{1,0:T(2,128)} %param.30) | copy-start | bytes 196612
  1099.3 276.9 %copy-start.13 = (f32[384,512]{1,0:T(8,128)S(1)}, f32[384,512]{1,0:T(8,128)}, u32[]{:S(2)}) copy-start(f32[384,512]{1,0:T(8,128)} %param.24) | copy-start | bytes 2359300
  1100.1 277.3 %copy-start.109 = (f32[384]{0:T(512)}, f32[384]{0:T(512)S(1)}, u32[]{:S(2)}) copy-start(f32[384]{0:T(512)S(1)} %multiply_add_fusion.12) | copy-start | bytes 4612
  1283.1 50.8 %copy-start.11 = (f32[64,2048]{1,0:T(8,128)S(1)}, f32[64,2048]{1,0:T(8,128)}, u32[]{:S(2)}) copy-start(f32[64,2048]{1,0:T(8,128)} %reduce-scatter.5.cloned.1.call-done) | copy-start | bytes 1572868
  1285.0 46.4 %copy-start.150 = (f32[64]{0:T(128)}, f32[64]{0:T(128)S(1)}, u32[]{:S(2)}) copy-start(f32[64]{0:T(128)S(1)} %multiply_add_fusion.13) | copy-start | bytes 772
  1331.5 45.9 %copy-start.93 = (f32[4,512]{1,0:T(4,128)}, f32[4,512]{1,0:T(4,128)S(1)}, u32[]{:S(2)}) copy-start(f32[4,512]{1,0:T(4,128)S(1)} %multiply_add_fusion.11) | copy-start | bytes 24580
  1331.5 46.1 %copy-start.15 = (f32[64,2048]{1,0:T(8,128)S(1)}, f32[64,2048]{1,0:T(8,128)}, u32[]{:S(2)}) copy-start(f32[64,2048]{1,0:T(8,128)} %param.25) | copy-start | bytes 1572868
  1332.2 45.3 %copy-start.142 = (pred[64,3]{0,1:T(4,128)(4,1)S(1)}, pred[64,3]{0,1:T(4,128)(4,1)}, u32[]{:S(2)}) copy-start(pred[64,3]{0,1:T(4,128)(4,1)} %copy-done.140) | copy-start | bytes 580
  1332.2 45.3 %copy-start.155 = (f32[3]{0:T(128)S(1)}, f32[3]{0:T(128)}, u32[]{:S(2)}) copy-start(f32[3]{0:T(128)} %constant.161) | copy-start | bytes 40
  (143 other events, 953.3 us)
Sparse Core Ops, SparseCore 0:
  11.5 80.1 all-gather.4
  95.1 94.4 all-gather.2
  728.9 115.7 all-reduce.33
  851.6 246.2 reduce-scatter.2
  1100.7 182.2 reduce-scatter.4
where the time goes:
time: 1400 us; the launch traced here: 1390 us
  waiting for transfers between devices  599 us (43%)
  local copies, waits for them, and re-layouts  360 us (26%)
  blocking collectives  174 us (12%)
  other arithmetic  138 us (10%)
  matrix products  92.5 us (7%)
  between operations  22 us (2%)
    reduce_scatter x1, waiting for transfers between devices, body(): lax.psum_scatter(slim_term, ('wide', 'narrow'), scatter_dimension=0, tile...  251 us
    reduce_scatter x1, waiting for transfers between devices, body(): lax.psum_scatter(broad_term, ('wide', 'narrow'), scatter_dimension=0, til...  183 us
    slice x30, local copies, waits for them, and re-layouts, patches(): padded[:, row_tap:row_tap + reach:stride, col_tap:col_tap + reach:stride, :]  127 us
    all_gather x1, waiting for transfers between devices, body(): lax.all_gather(slim_master.astype(jnp.bfloat16), ('wide', 'narrow'), axis...  94.3 us
    unnamed x398, local copies, waits for them, and re-layouts  90.2 us
    psum x6, blocking collectives, group_stats(): lax.psum(jnp.sum(weighted, 1).astype(jnp.bfloat16), 'narrow')  47.1 us
    psum x6, blocking collectives, norm_backward(): lax.psum(gain_term.astype(jnp.bfloat16), 'narrow').astype(jnp.float32)  45.4 us
    psum x1, blocking collectives, body(): lax.psum((slim_col_part, broad_col_part, slim_row_part, broad_row_part, s...  43.3 us
  transfers between devices with their start and end apart: 5, of which 5 were waited for; matrix products, arithmetic and copies ran while one was open for 9% of the time, Pallas kernels for 0%

commit v1 on v0

v1 whole, which is shorter than its diff:
```python
import jax
import jax.numpy as jnp
import numpy as np
from jax import lax
from jax.experimental import pallas as pl
from jax.experimental.pallas import tpu as pltpu
from jax.sharding import PartitionSpec as P

STEP = 10
EPS_NORM = 1e-05
EPS_ONE = 1e-30
EPS_TWO = 0.001
STEP_RATE = 0.3
DECAY = 1.0 - STEP ** (-0.8)
AXES = ("wide", "narrow")
BF16 = jnp.bfloat16
F32 = jnp.float32
VMEM_LIMIT = 48 * 1024 * 1024


def shape_of(dims, dtype):
    return jax.ShapeDtypeStruct(dims, dtype)


def whole(dims):
    return pl.BlockSpec(dims, lambda *step: (0,) * len(dims))


def block(dims, place):
    return pl.BlockSpec(dims, place)


def kernel_call(body, name, grid, in_specs, out_specs, out_shape, flops, scratch=(), aliases=None):
    return pl.pallas_call(
        body,
        grid=grid,
        in_specs=in_specs,
        out_specs=out_specs,
        out_shape=out_shape,
        scratch_shapes=list(scratch),
        input_output_aliases=aliases or {},
        cost_estimate=pl.CostEstimate(flops=flops, bytes_accessed=flops // 200, transcendentals=0),
        compiler_params=pltpu.CompilerParams(vmem_limit_bytes=VMEM_LIMIT),
        name=name,
    )


def dot_nn(first, second):
    return jnp.dot(first, second, preferred_element_type=F32)


def dot_nt(first, second):
    return lax.dot_general(first, second, (((1,), (1,)), ((), ())), preferred_element_type=F32)


def dot_tn(first, second):
    return lax.dot_general(first, second, (((0,), (0,)), ((), ())), preferred_element_type=F32)


def sigmoid(value):
    return 1.0 / (1.0 + jnp.exp(-value))


def slope(value):
    gate = sigmoid(value)
    return gate * (1.0 + value * (1.0 - gate))


def tree_sum(values):
    values = list(values)
    while len(values) > 1:
        values = [values[i] + values[i + 1] for i in range(0, len(values), 2)]
    return values[0]


def moments(parts, recip):
    total = tree_sum([part[...] for part in parts]) * recip
    mean = total[0:1]
    return mean, lax.rsqrt(total[1:2] - mean * mean + EPS_NORM)


def column_sum(value):
    return jnp.sum(value, axis=0, keepdims=True)


def stat_rows(value, mask):
    kept = value * mask
    return jnp.concatenate([column_sum(kept), column_sum(kept * value)], 0)


def grid_rows(images, sides):
    return sum(images * side * side for side in sides)


def class_table(images, sides_out, padded):
    table = -np.ones((4, padded), np.int32)
    base_in, base_out = 0, 0
    for side in sides_out:
        extent = 2 * side
        for image in range(images):
            for row in range(side):
                for col in range(side):
                    for kind in range(4):
                        row_in, col_in = 2 * row + kind // 2, 2 * col + kind % 2
                        table[kind, base_out + row * side + col] = (
                            base_in + row_in * extent + col_in
                        )
            base_in += extent * extent
            base_out += side * side
    return table


def shift_table(images, sides_out, padded):
    table = -np.ones((9, padded), np.int32)
    base = 0
    for side in sides_out:
        for _ in range(images):
            for row in range(side):
                for col in range(side):
                    for which in range(9):
                        row_to, col_to = row + which // 3 - 1, col + which % 3 - 1
                        if 0 <= row_to < side and 0 <= col_to < side:
                            table[which, base + row * side + col] = base + row_to * side + col_to
            base += side * side
    return table


def one_hot(table, width):
    return (jnp.asarray(table)[..., None] == jnp.arange(width, dtype=jnp.int32)).astype(BF16)


def first_kernel(x_ref, w_ref, mask_ref, z_ref, stat_ref):
    z = dot_nn(x_ref[0], w_ref[...])
    z_ref[0] = z
    rows = stat_rows(z, mask_ref[...])

    @pl.when(pl.program_id(0) == 0)
    def _():
        stat_ref[...] = rows

    @pl.when(pl.program_id(0) > 0)
    def _():
        stat_ref[...] += rows


def side_kernel(x_ref, w_ref, mask_ref, z_ref, stat_ref):
    z = dot_nn(x_ref[0], w_ref[...])
    z_ref[...] = z
    stat_ref[...] = stat_rows(z, mask_ref[...])


def tap_forward(tap, stride):
    if stride == 1:
        return 0, tap
    row_tap, col_tap = tap // 3, tap % 3
    kind = jnp.where(row_tap == 1, 0, 2) + jnp.where(col_tap == 1, 0, 1)
    shift = jnp.where(row_tap == 0, 0, 3) + jnp.where(col_tap == 0, 0, 1)
    return kind, shift


def tap_backward(tap, stride):
    if stride == 1:
        return 0, 8 - tap
    row_tap, col_tap = tap // 3, tap % 3
    kind = jnp.where(row_tap == 1, 0, 2) + jnp.where(col_tap == 1, 0, 1)
    shift = jnp.where(row_tap == 0, 6, 3) + jnp.where(col_tap == 0, 2, 1)
    return kind, shift


def conv_kernel(count, kinds, stride):
    def body(*refs):
        z_ref = refs[0]
        parts = refs[1 : 1 + count]
        affine_ref, recip_ref, mask_ref, shift_ref, w_ref, act_ref, out_ref, stat_ref = refs[
            1 + count :
        ]
        tap = pl.program_id(0)

        @pl.when(tap == 0)
        def _():
            mean, inv = moments(parts, recip_ref[...])
            for kind in range(kinds):
                pre = affine_ref[0:1] * ((z_ref[kind] - mean) * inv) + affine_ref[1:2]
                act_ref[kind] = (pre * sigmoid(pre)).astype(BF16)

        kind, shift = tap_forward(tap, stride)
        patch = dot_nn(shift_ref[shift], act_ref[kind]).astype(BF16)
        term = dot_nn(patch, w_ref[...])

        @pl.when(tap == 0)
        def _():
            out_ref[...] = term

        @pl.when(tap > 0)
        def _():
            out_ref[...] += term

        @pl.when(tap == 8)
        def _():
            stat_ref[...] = stat_rows(out_ref[...], mask_ref[...])

    return body


def widen_kernel(count, carry):
    def body(*refs):
        z_ref = refs[0]
        parts = refs[1 : 1 + count]
        rest = refs[1 + count :]
        if carry:
            affine_ref, recip_ref, mask_ref, w_ref, side_ref, act_ref, out_ref, stat_ref = rest
        else:
            affine_ref, recip_ref, mask_ref, w_ref, act_ref, out_ref, stat_ref = rest

        @pl.when(pl.program_id(0) == 0)
        def _():
            mean, inv = moments(parts, recip_ref[...])
            pre = affine_ref[0:1] * ((z_ref[...] - mean) * inv) + affine_ref[1:2]
            act_ref[...] = (pre * sigmoid(pre)).astype(BF16)

        z = dot_nn(act_ref[...], w_ref[...])
        out_ref[...] = z
        if carry:
            stat_ref[...] = jnp.concatenate([stat_rows(z, mask_ref[...]), side_ref[...]], 0)
        else:
            stat_ref[...] = stat_rows(z, mask_ref[...])

    return body


def pair_moments(parts, recip):
    total = tree_sum([part[...] for part in parts]) * recip
    mean, mean_side = total[0:1], total[2:3]
    inv = lax.rsqrt(total[1:2] - mean * mean + EPS_NORM)
    inv_side = lax.rsqrt(total[3:4] - mean_side * mean_side + EPS_NORM)
    return mean, inv, mean_side, inv_side


def mix_kernel(count):
    def body(*refs):
        z_ref, side_ref = refs[:2]
        parts = refs[2 : 2 + count]
        (affine_ref, affine_side_ref, recip_ref, mask_ref, w_ref) = refs[2 + count : 7 + count]
        hidden_ref, low_ref, out_ref, stat_ref = refs[7 + count :]
        mean, inv, mean_side, inv_side = pair_moments(parts, recip_ref[...])
        pre = (
            affine_ref[0:1] * ((z_ref[...] - mean) * inv)
            + affine_ref[1:2]
            + affine_side_ref[0:1] * ((side_ref[...] - mean_side) * inv_side)
            + affine_side_ref[1:2]
        )
        hidden = pre * sigmoid(pre)
        hidden_ref[...] = hidden
        low = hidden.astype(BF16)
        low_ref[...] = low
        term = dot_nn(low, w_ref[...])

        @pl.when(pl.program_id(0) == 0)
        def _():
            out_ref[...] = term

        @pl.when(pl.program_id(0) > 0)
        def _():
            out_ref[...] += term

        @pl.when(pl.program_id(0) == pl.num_programs(0) - 1)
        def _():
            stat_ref[...] = stat_rows(out_ref[...], mask_ref[...])

    return body


def output_kernel(count):
    def body(*refs):
        z_ref = refs[0]
        parts = refs[1 : 1 + count]
        affine_ref, recip_ref, mask_ref, hidden_ref, cot_ref, y_ref, grad_ref, stat_ref = refs[
            1 + count :
        ]
        mean, inv = moments(parts, recip_ref[...])
        normed = (z_ref[...] - mean) * inv
        pre = affine_ref[0:1] * normed + affine_ref[1:2] + hidden_ref[...]
        gate = sigmoid(pre)
        y_ref[...] = (pre * gate).astype(BF16)
        grad = cot_ref[...].astype(F32) * mask_ref[...] * (gate * (1.0 + pre * (1.0 - gate)))
        grad_ref[...] = grad
        stat_ref[...] = jnp.concatenate([column_sum(grad), column_sum(grad * normed)], 0)

    return body


def norm_back(grad, normed, sums, recip, mask, scale):
    return scale * (grad - mask * (sums[0:1] * recip + normed * (sums[1:2] * recip)))


def back_linear_kernel(count):
    def body(*refs):
        grad_ref, z_ref = refs[:2]
        parts = refs[2 : 2 + count]
        sums = refs[2 + count : 2 + 2 * count]
        affine_ref, recip_ref, mask_ref, w_ref, below_ref = refs[2 + 2 * count : 7 + 2 * count]
        below_parts = refs[7 + 2 * count : 7 + 3 * count]
        below_affine_ref, dz_ref, out_ref, stat_ref = refs[7 + 3 * count :]
        recip = recip_ref[...]
        mean, inv = moments(parts, recip)
        total = tree_sum([part[...] for part in sums])
        normed = (z_ref[...] - mean) * inv
        dz = norm_back(grad_ref[...], normed, total, recip, mask_ref[...], affine_ref[0:1] * inv)
        dz = dz.astype(BF16)
        dz_ref[...] = dz
        term = dot_nt(dz, w_ref[...])

        @pl.when(pl.program_id(0) == 0)
        def _():
            out_ref[...] = term

        @pl.when(pl.program_id(0) > 0)
        def _():
            out_ref[...] += term

        @pl.when(pl.program_id(0) == pl.num_programs(0) - 1)
        def _():
            finish_below(out_ref, below_ref, below_parts, below_affine_ref, recip, stat_ref)

    return body


def finish_below(out_ref, below_ref, below_parts, below_affine_ref, recip, stat_ref):
    mean, inv = moments(below_parts, recip)
    normed = (below_ref[...] - mean) * inv
    pre = below_affine_ref[0:1] * normed + below_affine_ref[1:2]
    grad = out_ref[...] * slope(pre)
    out_ref[...] = grad
    stat_ref[...] = jnp.concatenate([column_sum(grad), column_sum(grad * normed)], 0)


def back_conv_kernel(count, kinds, stride):
    def body(*refs):
        grad_ref, z_ref = refs[:2]
        parts = refs[2 : 2 + count]
        sums = refs[2 + count : 2 + 2 * count]
        affine_ref, recip_ref, mask_ref, shift_ref, w_ref, below_ref = refs[
            2 + 2 * count : 8 + 2 * count
        ]
        below_parts = refs[8 + 2 * count : 8 + 3 * count]
        below_affine_ref, below_recip_ref, dz_ref, out_ref, stat_ref = refs[8 + 3 * count :]
        tap = pl.program_id(0)

        @pl.when(tap == 0)
        def _():
            recip = recip_ref[...]
            mean, inv = moments(parts, recip)
            total = tree_sum([part[...] for part in sums])
            normed = (z_ref[...] - mean) * inv
            dz = norm_back(
                grad_ref[...], normed, total, recip, mask_ref[...], affine_ref[0:1] * inv
            )
            dz_ref[...] = dz.astype(BF16)
            out_ref[...] = jnp.zeros_like(out_ref)

        kind, shift = tap_backward(tap, stride)
        patch = dot_nn(shift_ref[shift], dz_ref[...]).astype(BF16)
        out_ref[kind] += dot_nt(patch, w_ref[...])

        @pl.when(tap == 8)
        def _():
            mean, inv = moments(below_parts, below_recip_ref[...])
            rows = None
            for which in range(kinds):
                normed = (below_ref[which] - mean) * inv
                pre = below_affine_ref[0:1] * normed + below_affine_ref[1:2]
                grad = out_ref[which] * slope(pre)
                out_ref[which] = grad
                part = jnp.concatenate([column_sum(grad), column_sum(grad * normed)], 0)
                rows = part if rows is None else rows + part
            stat_ref[...] = rows

    return body


def back_mix_kernel(count):
    def body(*refs):
        grad_ref, z_ref = refs[:2]
        parts = refs[2 : 2 + count]
        sums = refs[2 + count : 2 + 2 * count]
        affine_ref, recip_ref, mask_ref, w_ref, above_ref, mid_ref, side_ref = refs[
            2 + 2 * count : 9 + 2 * count
        ]
        pair_parts = refs[9 + 2 * count : 9 + 3 * count]
        affine_mid_ref, affine_side_ref, dz_ref, out_ref, stat_ref = refs[9 + 3 * count :]
        recip = recip_ref[...]

        @pl.when(pl.program_id(0) == 0)
        def _():
            mean, inv = moments(parts, recip)
            total = tree_sum([part[...] for part in sums])
            normed = (z_ref[...] - mean) * inv
            dz = norm_back(
                grad_ref[...], normed, total, recip, mask_ref[...], affine_ref[0:1] * inv
            )
            dz_ref[...] = dz.astype(BF16)

        mean, inv, mean_side, inv_side = pair_moments(pair_parts, recip)
        normed = (mid_ref[...] - mean) * inv
        normed_side = (side_ref[...] - mean_side) * inv_side
        pre = (
            affine_mid_ref[0:1] * normed
            + affine_mid_ref[1:2]
            + affine_side_ref[0:1] * normed_side
            + affine_side_ref[1:2]
        )
        grad = (above_ref[...] + dot_nt(dz_ref[...], w_ref[...])) * slope(pre)
        out_ref[...] = grad
        stat_ref[...] = jnp.concatenate(
            [column_sum(grad), column_sum(grad * normed), column_sum(grad * normed_side)], 0
        )

    return body


def back_pair_kernel(count):
    def body(*refs):
        grad_ref, mid_ref, side_ref = refs[:3]
        pair_parts = refs[3 : 3 + count]
        sums = refs[3 + count : 3 + 2 * count]
        affine_mid_ref, affine_side_ref, recip_ref, mask_ref, w_ref, below_ref = refs[
            3 + 2 * count : 9 + 2 * count
        ]
        below_parts = refs[9 + 2 * count : 9 + 3 * count]
        below_affine_ref, dz_ref, dz_side_ref, out_ref, stat_ref = refs[9 + 3 * count :]
        recip = recip_ref[...]
        mean, inv, mean_side, inv_side = pair_moments(pair_parts, recip)
        total = tree_sum([part[...] for part in sums])
        normed = (mid_ref[...] - mean) * inv
        normed_side = (side_ref[...] - mean_side) * inv_side
        grad = grad_ref[...]
        mask = mask_ref[...]
        dz = norm_back(grad, normed, total[0:2], recip, mask, affine_mid_ref[0:1] * inv)
        dz = dz.astype(BF16)
        dz_ref[...] = dz
        total_side = jnp.concatenate([total[0:1], total[2:3]], 0)
        dz_side_ref[...] = norm_back(
            grad, normed_side, total_side, recip, mask, affine_side_ref[0:1] * inv_side
        ).astype(BF16)
        term = dot_nt(dz, w_ref[...])

        @pl.when(pl.program_id(0) == 0)
        def _():
            out_ref[...] = term

        @pl.when(pl.program_id(0) > 0)
        def _():
            out_ref[...] += term

        @pl.when(pl.program_id(0) == pl.num_programs(0) - 1)
        def _():
            finish_below(out_ref, below_ref, below_parts, below_affine_ref, recip, stat_ref)

    return body


def back_first_kernel(count):
    def body(*refs):
        grad_ref, z_ref = refs[:2]
        parts = refs[2 : 2 + count]
        sums = refs[2 + count : 2 + 2 * count]
        affine_ref, recip_ref, mask_ref, x_ref, _, dz_ref, grad_w_ref, total_ref = refs[
            2 + 2 * count :
        ]
        recip = recip_ref[...]
        mean, inv = moments(parts, recip)
        total = tree_sum([part[...] for part in sums])
        normed = (z_ref[0] - mean) * inv
        dz = norm_back(grad_ref[0], normed, total, recip, mask_ref[...], affine_ref[0:1] * inv)
        dz = dz.astype(BF16)
        dz_ref[0] = dz
        term = dot_tn(x_ref[0], dz)

        @pl.when(pl.program_id(0) == 0)
        def _():
            total_ref[...] = term

        @pl.when(pl.program_id(0) > 0)
        def _():
            total_ref[...] += term

        @pl.when(pl.program_id(0) == pl.num_programs(0) - 1)
        def _():
            grad_w_ref[...] = total_ref[...].astype(BF16)

    return body


def weight_grad_kernel(act_ref, dz_ref, *rest):
    rest[-1][...] = dot_tn(act_ref[...], dz_ref[...]).astype(BF16)


def conv_grad_kernel(stride):
    def body(act_ref, shift_ref, dz_ref, *rest):
        kind, shift = tap_forward(pl.program_id(0), stride)
        patch = dot_nn(shift_ref[shift], act_ref[kind]).astype(BF16)
        rest[-1][...] = dot_tn(patch, dz_ref[...]).astype(BF16)

    return body


def level_masks(first_row, rows, bounds):
    index = first_row + lax.broadcasted_iota(jnp.int32, (rows, 1), 0)
    return [
        ((index >= bounds[level]) & (index < bounds[level + 1])).astype(F32)
        for level in range(len(bounds) - 1)
    ]


def tally_kernel(bounds):
    levels = len(bounds) - 1

    def body(first_ref, grad_ref, master_ref, old_ref, rows_ref, sums_ref):
        grad = grad_ref[...]
        master = master_ref[...]
        square = grad * grad
        raised = square + EPS_ONE
        rows_new = DECAY * old_ref[...] + (1.0 - DECAY) * jnp.mean(raised, 1, keepdims=True)
        rows_ref[...] = rows_new
        ratio = square / rows_new
        weight = jnp.sum(master * master, 1, keepdims=True)
        masks = level_masks(first_ref[0], grad.shape[0], bounds)
        spread = jnp.zeros((1, grad.shape[1]), F32)
        for level in range(levels):
            mask = masks[level]
            sums_ref[level : level + 1] = column_sum(raised * mask)
            sums_ref[levels + level : levels + level + 1] = column_sum(ratio * mask)
            low = 2 * levels + level
            sums_ref[low : low + 1] = spread + column_sum(rows_new * mask)
            low = 3 * levels + level
            sums_ref[low : low + 1] = spread + column_sum(weight * mask)

    return body


def renew_kernel(bounds):
    levels = len(bounds) - 1

    def body(first_ref, grad_ref, master_ref, rows_ref, sums_ref, old_ref, cols_ref, new_ref, low_ref):
        grad = grad_ref[...]
        columns = grad.shape[1]
        masks = level_masks(first_ref[0], grad.shape[0], bounds)
        factor = None
        for level in range(levels):
            height = float(bounds[level + 1] - bounds[level])
            cells = height * columns
            col_sum = sums_ref[level : level + 1]
            ratio_sum = sums_ref[levels + level : levels + level + 1]
            row_mean = sums_ref[2 * levels + level : 2 * levels + level + 1] / height
            weight_sum = sums_ref[3 * levels + level : 3 * levels + level + 1]
            cols_new = DECAY * old_ref[level : level + 1] + (1.0 - DECAY) * (col_sum / height)
            cols_ref[level : level + 1] = cols_new
            relative = cols_new / row_mean
            update_sq = jnp.sum(ratio_sum / relative, axis=1, keepdims=True)
            update_rms = jnp.sqrt(update_sq / cells)
            weight_rms = jnp.sqrt(weight_sum / cells)
            step = STEP_RATE * jnp.maximum(EPS_TWO, weight_rms) / jnp.maximum(1.0, update_rms)
            part = masks[level] * (step * lax.rsqrt(relative))
            factor = part if factor is None else factor + part
        new = master_ref[...] - grad * lax.rsqrt(rows_ref[...]) * factor
        new_ref[...] = new
        low_ref[...] = new.astype(BF16)

    return body


class Exchange:
    def __init__(self, n_wide, n_narrow):
        self.n_narrow = n_narrow
        self.total = n_wide * n_narrow
        self.bits = self.total.bit_length() - 1
        self.narrow_bits = n_narrow.bit_length() - 1
        self.index = lax.axis_index(AXES)

    def bit(self, level):
        return (self.index >> level) & 1

    def swap(self, value, level):
        pairs = [(device, device ^ (1 << level)) for device in range(self.total)]
        return lax.ppermute(value, AXES, pairs)

    def group_parts(self, value):
        return [value] + [
            lax.ppermute(value, "narrow", [(i, i ^ k) for i in range(self.n_narrow)])
            for k in range(1, self.n_narrow)
        ]

    def total_sum(self, value, first=0):
        for level in range(first, self.bits):
            value = value + self.swap(value, level)
        return value

    def scatter(self, part, prefix):
        open_bits = self.bits - len(prefix)
        rows = part.shape[0] >> open_bits
        current = part
        for level in range(open_bits):
            view = current.reshape((1 << (open_bits - level - 1), 2, rows, part.shape[1]))
            mine = self.bit(level)
            sent = lax.dynamic_index_in_dim(view, 1 - mine, 1, keepdims=False)
            kept = lax.dynamic_index_in_dim(view, mine, 1, keepdims=False)
            came = self.swap(sent, level)
            current = self.add(kept, came, level)
        current = current.reshape(rows, part.shape[1])
        for level in range(open_bits, self.bits):
            want = prefix[level - open_bits]
            pairs = []
            for device in range(self.total):
                settled = all(
                    (device >> other) & 1 == prefix[other - open_bits]
                    for other in range(open_bits, level)
                )
                if settled and (device >> level) & 1 != want:
                    pairs.append((device, device ^ (1 << level)))
            came = lax.ppermute(current, AXES, pairs)
            current = self.add(current, came, level)
        return current

    def add(self, kept, came, level):
        total = kept.astype(F32) + came.astype(F32)
        return total if level == self.bits - 1 else total.astype(BF16)


def make_body(mesh):
    n_wide, n_narrow = mesh.shape["wide"], mesh.shape["narrow"]

    def body(
        x_lo,
        x_mid,
        x_hi,
        cot_lo,
        cot_mid,
        cot_hi,
        live_counts,
        slim_master,
        broad_master,
        slim_rowstat,
        broad_rowstat,
        slim_colstat,
        broad_colstat,
        norm_params,
        norm_moments,
    ):
        link = Exchange(n_wide, n_narrow)
        count = n_narrow
        images = x_lo.shape[0]
        sides = tuple(value.shape[1] // 2 for value in (x_lo, x_mid, x_hi))
        c_in, mid, c_out = x_lo.shape[3], slim_master.shape[1], broad_master.shape[1]
        cells = grid_rows(images, sides)
        cells_in = 4 * cells
        rows = -(-cells // 16) * 16
        chunks = c_out // mid
        bounds_slim = (0, c_in, c_in + 9 * mid, c_in + 9 * mid + c_out, c_in + 18 * mid + c_out)
        bounds_broad = (0, mid, mid + c_in, 2 * mid + c_in)
        at_two, at_four, at_five = (bounds_slim[level] // mid for level in (1, 2, 3))
        at_six = bounds_broad[2] // mid
        widths = (mid, mid, c_out, c_out, mid, mid, c_out)
        norm_at = [sum(widths[:level]) // mid for level in range(7)]

        slim = lax.all_gather(slim_master.astype(BF16), AXES, axis=0, tiled=True)
        broad = lax.all_gather(broad_master.astype(BF16), AXES, axis=0, tiled=True)

        kinds = class_table(images, sides, rows)
        shifts = one_hot(shift_table(images, sides, rows), rows)
        x_flat = jnp.concatenate([value.reshape(-1, c_in) for value in (x_lo, x_mid, x_hi)], 0)
        x_kinds = jnp.dot(one_hot(kinds.reshape(-1), cells_in), x_flat, preferred_element_type=F32)
        x_kinds = x_kinds.astype(BF16).reshape(4, rows, c_in)
        cot = jnp.concatenate(
            [value.reshape(-1, c_out) for value in (cot_lo, cot_mid, cot_hi)]
            + [jnp.zeros((rows - cells, c_out), BF16)],
            0,
        )
        alive = [
            (jnp.arange(images) < live_counts[0, level]).astype(F32) for level in range(3)
        ]
        mask = jnp.concatenate(
            [jnp.repeat(alive[level], side * side) for level, side in enumerate(sides)]
            + [jnp.zeros((rows - cells,), F32)]
        )
        cell_count = lax.psum(jnp.sum(mask), "narrow")
        mask = mask[:, None]
        recip = (1.0 / cell_count).reshape(1, 1)
        recip_in = (0.25 / cell_count).reshape(1, 1)

        narrow_all = whole((rows, mid))
        kinds_all = whole((4, rows, mid))
        stat_all = whole((2, mid))
        mask_all = whole((rows, 1))
        one_all = whole((1, 1))
        shifts_all = whole((9, rows, rows))
        chunk = block((rows, mid), lambda j: (0, j))

        def stat_chunk(height):
            return block((height, mid), lambda j: (0, j))

        def affine(level):
            return block((2, mid), lambda j: (0, norm_at[level]))

        def affine_chunk(level):
            return block((2, mid), lambda j: (0, norm_at[level] + j))

        def slim_block(at):
            return block((mid, mid), lambda j: (at + j, 0))

        def broad_block(at):
            return block((mid, mid), lambda j: (at, j))

        narrow_f32 = shape_of((rows, mid), F32)
        wide_f32 = shape_of((rows, c_out), F32)
        narrow_low = shape_of((rows, mid), BF16)
        wide_low = shape_of((rows, c_out), BF16)
        stat_narrow = shape_of((2, mid), F32)
        stat_wide = shape_of((2, c_out), F32)
        flops_conv = 2 * rows * 9 * mid * (mid + rows)
        flops_wide = 2 * rows * mid * c_out

        z_one, stat = kernel_call(
            first_kernel,
            "first",
            (4,),
            [
                block((1, rows, c_in), lambda j: (j, 0, 0)),
                whole((c_in, mid)),
                mask_all,
            ],
            [block((1, rows, mid), lambda j: (j, 0, 0)), stat_all],
            [shape_of((4, rows, mid), F32), stat_narrow],
            2 * 4 * rows * c_in * mid,
        )(x_kinds, slim, mask)
        parts_one = link.group_parts(stat)
        z_side, stat_side = kernel_call(
            side_kernel,
            "side",
            (chunks,),
            [
                block((1, rows, c_in), lambda j: (0, 0, 0)),
                block((c_in, mid), lambda j: (0, j)),
                mask_all,
            ],
            [chunk, stat_chunk(2)],
            [wide_f32, stat_wide],
            2 * rows * c_in * c_out,
        )(x_kinds, broad[mid : mid + c_in], mask)
        act_one, z_two, stat = kernel_call(
            conv_kernel(count, 4, 2),
            "conv_two",
            (9,),
            [kinds_all]
            + [stat_all] * count
            + [affine(0), one_all, mask_all, shifts_all, slim_block(at_two)],
            [kinds_all, narrow_all, stat_all],
            [shape_of((4, rows, mid), BF16), narrow_f32, stat_narrow],
            flops_conv,
        )(z_one, *parts_one, norm_params, recip_in, mask, shifts, slim)
        parts_two = link.group_parts(stat)
        act_two, z_three, stat = kernel_call(
            widen_kernel(count, True),
            "widen_three",
            (chunks,),
            [narrow_all]
            + [stat_all] * count
            + [affine(1), one_all, mask_all, broad_block(0), stat_chunk(2)],
            [narrow_all, chunk, stat_chunk(4)],
            [narrow_low, wide_f32, shape_of((4, c_out), F32)],
            flops_wide,
        )(z_two, *parts_two, norm_params, recip, mask, broad, stat_side)
        parts_pair = link.group_parts(stat)
        hidden, hidden_low, z_four, stat = kernel_call(
            mix_kernel(count),
            "mix",
            (chunks,),
            [chunk, chunk]
            + [stat_chunk(4)] * count
            + [affine_chunk(2), affine_chunk(3), one_all, mask_all, slim_block(at_four)],
            [chunk, chunk, narrow_all, stat_all],
            [wide_f32, wide_low, narrow_f32, stat_narrow],
            flops_wide,
        )(z_three, z_side, *parts_pair, norm_params, norm_params, recip, mask, slim)
        parts_four = link.group_parts(stat)
        one_kind = whole((1, rows, mid))
        act_four, z_five, stat = kernel_call(
            conv_kernel(count, 1, 1),
            "conv_five",
            (9,),
            [one_kind]
            + [stat_all] * count
            + [affine(4), one_all, mask_all, shifts_all, slim_block(at_five)],
            [one_kind, narrow_all, stat_all],
            [shape_of((1, rows, mid), BF16), narrow_f32, stat_narrow],
            flops_conv,
        )(z_four[None], *parts_four, norm_params, recip, mask, shifts, slim)
        parts_five = link.group_parts(stat)
        act_five, z_six, stat = kernel_call(
            widen_kernel(count, False),
            "widen_six",
            (chunks,),
            [narrow_all]
            + [stat_all] * count
            + [affine(5), one_all, mask_all, broad_block(at_six)],
            [narrow_all, chunk, stat_chunk(2)],
            [narrow_low, wide_f32, stat_wide],
            flops_wide,
        )(z_five, *parts_five, norm_params, recip, mask, broad)
        parts_six = link.group_parts(stat)
        y, grad_out, stat = kernel_call(
            output_kernel(count),
            "output",
            (chunks,),
            [chunk]
            + [stat_chunk(2)] * count
            + [affine_chunk(6), one_all, mask_all, chunk, chunk],
            [chunk, chunk, stat_chunk(2)],
            [wide_low, wide_f32, stat_wide],
            flops_wide // 8,
        )(z_six, *parts_six, norm_params, recip, mask, hidden, cot)
        sums_six = link.group_parts(stat)

        dz_six, grad_five, stat = kernel_call(
            back_linear_kernel(count),
            "back_six",
            (chunks,),
            [chunk, chunk]
            + [stat_chunk(2)] * (2 * count)
            + [affine_chunk(6), one_all, mask_all, broad_block(at_six), narrow_all]
            + [stat_all] * count
            + [affine(5)],
            [chunk, narrow_all, stat_all],
            [wide_low, narrow_f32, stat_narrow],
            flops_wide,
        )(
            grad_out,
            z_six,
            *parts_six,
            *sums_six,
            norm_params,
            recip,
            mask,
            broad,
            z_five,
            *parts_five,
            norm_params,
        )
        sums_five = link.group_parts(stat)

        def weight_grad(act, dz, steps, act_at, out_shape, out_at, base, name):
            high, across = steps
            height = act.shape[0]
            specs = [
                block((height, mid), lambda i, j: (0, act_at + i)),
                block((height, mid), lambda i, j: (0, j)),
            ]
            args = [act, dz]
            if base is not None:
                specs.append(pl.BlockSpec(memory_space=pl.ANY))
                args.append(base)
            return kernel_call(
                weight_grad_kernel,
                name,
                (high, across),
                specs,
                block((mid, mid), lambda i, j: (out_at + i, j)),
                shape_of(out_shape, BF16),
                2 * height * mid * mid * high * across,
                aliases={2: 0} if base is not None else None,
            )(*args)

        def conv_grad(act, dz, stride, out_at, base, name):
            kinds_here = act.shape[0]
            return kernel_call(
                conv_grad_kernel(stride),
                name,
                (9,),
                [
                    whole((kinds_here, rows, mid)),
                    shifts_all,
                    narrow_all,
                    pl.BlockSpec(memory_space=pl.ANY),
                ],
                block((mid, mid), lambda t: (out_at + t, 0)),
                shape_of(base.shape, BF16),
                flops_conv,
                aliases={3: 0},
            )(act, shifts, dz, base)

        half = bounds_slim[-1] // 2
        quarter = bounds_broad[-1] // 4
        term_six = weight_grad(act_five, dz_six, (1, chunks), 0, (mid, c_out), 0, None, "grad_six")
        broad_three = link.scatter(term_six, (1, 1))

        dz_five, grad_four, stat = kernel_call(
            back_conv_kernel(count, 1, 1),
            "back_five",
            (9,),
            [narrow_all, narrow_all]
            + [stat_all] * (2 * count)
            + [affine(5), one_all, mask_all, shifts_all, slim_block(at_five), one_kind]
            + [stat_all] * count
            + [affine(4), one_all],
            [narrow_all, one_kind, stat_all],
            [narrow_low, shape_of((1, rows, mid), F32), stat_narrow],
            flops_conv,
        )(
            grad_five,
            z_five,
            *parts_five,
            *sums_five,
            norm_params,
            recip,
            mask,
            shifts,
            slim,
            z_four[None],
            *parts_four,
            norm_params,
            recip,
        )
        grad_four = grad_four[0]
        sums_four = link.group_parts(stat)
        dz_four, grad_mid, stat = kernel_call(
            back_mix_kernel(count),
            "back_four",
            (chunks,),
            [narrow_all, narrow_all]
            + [stat_all] * (2 * count)
            + [affine(4), one_all, mask_all, slim_block(at_four), chunk, chunk, chunk]
            + [stat_chunk(4)] * count
            + [affine_chunk(2), affine_chunk(3)],
            [narrow_all, chunk, stat_chunk(3)],
            [narrow_low, wide_f32, shape_of((3, c_out), F32)],
            flops_wide,
        )(
            grad_four,
            z_four,
            *parts_four,
            *sums_four,
            norm_params,
            recip,
            mask,
            slim,
            grad_out,
            z_three,
            z_side,
            *parts_pair,
            norm_params,
            norm_params,
        )
        sums_pair = link.group_parts(stat)
        low_four = half // mid - at_four
        slim_high = weight_grad(
            hidden_low,
            dz_four,
            (chunks - low_four, 1),
            low_four,
            (half, mid),
            0,
            None,
            "grad_four",
        )
        slim_high = conv_grad(
            act_four, dz_five, 1, at_five - half // mid, slim_high, "grad_five"
        )
        slim_high = link.scatter(slim_high, (1,))

        dz_three, dz_side, grad_two, stat = kernel_call(
            back_pair_kernel(count),
            "back_three",
            (chunks,),
            [chunk, chunk, chunk]
            + [stat_chunk(4)] * count
            + [stat_chunk(3)] * count
            + [affine_chunk(2), affine_chunk(3), one_all, mask_all, broad_block(0), narrow_all]
            + [stat_all] * count
            + [affine(1)],
            [chunk, chunk, narrow_all, stat_all],
            [wide_low, wide_low, narrow_f32, stat_narrow],
            flops_wide,
        )(
            grad_mid,
            z_three,
            z_side,
            *parts_pair,
            *sums_pair,
            norm_params,
            norm_params,
            recip,
            mask,
            broad,
            z_two,
            *parts_two,
            norm_params,
        )
        sums_two = link.group_parts(stat)
        x_sub = x_kinds[0]
        broad_low = weight_grad(
            act_two, dz_three, (1, chunks), 0, (2 * quarter, c_out), 0, None, "grad_three"
        )
        broad_low = weight_grad(
            x_sub, dz_side, (1, chunks), 0, (2 * quarter, c_out), 1, broad_low, "grad_side_low"
        )
        broad_low = link.scatter(broad_low, (0,))
        broad_two = weight_grad(
            x_sub, dz_side, (1, chunks), 1, (quarter, c_out), 0, None, "grad_side_high"
        )
        broad_two = link.scatter(broad_two, (0, 1))

        dz_two, grad_one, stat = kernel_call(
            back_conv_kernel(count, 4, 2),
            "back_two",
            (9,),
            [narrow_all, narrow_all]
            + [stat_all] * (2 * count)
            + [affine(1), one_all, mask_all, shifts_all, slim_block(at_two), kinds_all]
            + [stat_all] * count
            + [affine(0), one_all],
            [narrow_all, kinds_all, stat_all],
            [narrow_low, shape_of((4, rows, mid), F32), stat_narrow],
            flops_conv,
        )(
            grad_two,
            z_two,
            *parts_two,
            *sums_two,
            norm_params,
            recip,
            mask,
            shifts,
            slim,
            z_one,
            *parts_one,
            norm_params,
            recip_in,
        )
        sums_one = link.group_parts(stat)
        slim_low = weight_grad(
            hidden_low, dz_four, (low_four, 1), 0, (half, mid), at_four, None, "grad_four_low"
        )
        slim_low = conv_grad(act_one, dz_two, 2, at_two, slim_low, "grad_two")
        dz_one, slim_low = kernel_call(
            back_first_kernel(count),
            "back_one",
            (4,),
            [block((1, rows, mid), lambda j: (j, 0, 0))] * 2
            + [stat_all] * (2 * count)
            + [
                affine(0),
                one_all,
                mask_all,
                block((1, rows, c_in), lambda j: (j, 0, 0)),
                pl.BlockSpec(memory_space=pl.ANY),
            ],
            [block((1, rows, mid), lambda j: (j, 0, 0)), whole((c_in, mid))],
            [shape_of((4, rows, mid), BF16), shape_of((half, mid), BF16)],
            2 * 4 * rows * c_in * mid,
            scratch=[pltpu.VMEM((c_in, mid), F32)],
            aliases={2 + 2 * count + 4: 1},
        )(grad_one, z_one, *parts_one, *sums_one, norm_params, recip_in, mask, x_kinds, slim_low)
        slim_low = link.scatter(slim_low, (0,))

        back_rows = -np.ones((cells_in,), np.int32)
        side_rows = -np.ones((cells_in,), np.int32)
        for kind in range(4):
            for row in range(cells):
                back_rows[kinds[kind, row]] = kind * rows + row
        side_rows[kinds[0, :cells]] = np.arange(cells)
        dz_natural = jnp.dot(
            one_hot(back_rows, 4 * rows),
            dz_one.reshape(4 * rows, mid),
            preferred_element_type=F32,
        ).astype(BF16)
        side_natural = jnp.dot(
            one_hot(side_rows, rows), dz_side, preferred_element_type=F32
        ).astype(BF16)
        grad_x = dot_nt(dz_natural, slim[:c_in]) + dot_nt(side_natural, broad[mid : mid + c_in])

        def split(flat, extents):
            pieces = []
            offset = 0
            for extent in extents:
                length = images * extent * extent
                pieces.append(
                    flat[offset : offset + length].reshape(images, extent, extent, flat.shape[1])
                )
                offset += length
            return pieces

        y_parts = split(y, sides)
        dx_parts = split(grad_x, tuple(2 * side for side in sides))

        top = link.bit(link.bits - 1)
        second = link.bit(link.bits - 2)
        slim_grad = jnp.where(top == 1, slim_high, slim_low)
        broad_grad = jnp.where(
            top == 0, broad_low, jnp.where(second == 1, broad_three, broad_two)
        )

        def optimize(grad, master, rowstat, colstat, bounds, name):
            height, columns = grad.shape
            levels = len(bounds) - 1
            first = (link.index * height).astype(jnp.int32).reshape(1)
            scalar = pl.BlockSpec(memory_space=pltpu.SMEM)
            matrix, column = whole((height, columns)), whole((height, 1))
            sums_all, cols_all = whole((4 * levels, columns)), whole((levels, columns))
            rows_new, sums = kernel_call(
                tally_kernel(bounds),
                name + "_tally",
                (1,),
                [scalar, matrix, matrix, column],
                [column, sums_all],
                [shape_of((height, 1), F32), shape_of((4 * levels, columns), F32)],
                20 * height * columns,
            )(first, grad, master, rowstat.reshape(height, 1))
            sums = link.total_sum(sums)
            cols_new, new, low = kernel_call(
                renew_kernel(bounds),
                name + "_renew",
                (1,),
                [scalar, matrix, matrix, column, sums_all, cols_all],
                [cols_all, matrix, matrix],
                [
                    shape_of((levels, columns), F32),
                    shape_of((height, columns), F32),
                    shape_of((height, columns), BF16),
                ],
                20 * height * columns,
            )(first, grad, master, rows_new, sums, colstat)
            return rows_new.reshape(height), cols_new, new, low

        broad_rows_new, broad_cols_new, broad_new, broad_copy = optimize(
            broad_grad, broad_master, broad_rowstat, broad_colstat, bounds_broad, "broad"
        )
        slim_rows_new, slim_cols_new, slim_new, slim_copy = optimize(
            slim_grad, slim_master, slim_rowstat, slim_colstat, bounds_slim, "slim"
        )

        pair = tree_sum(sums_pair)
        norm_sums = [
            tree_sum(sums_one),
            tree_sum(sums_two),
            pair[0:2],
            pair[0:3:2],
            tree_sum(sums_four),
            tree_sum(sums_five),
            tree_sum(sums_six),
        ]
        norm_grad = jnp.concatenate(norm_sums, 1)[::-1]
        norm_grad = link.total_sum(norm_grad, link.narrow_bits)
        norm_moments_new = DECAY * norm_moments + (1.0 - DECAY) * (
            norm_grad * norm_grad + EPS_ONE
        )
        norm_update = norm_grad * lax.rsqrt(norm_moments_new)
        update_rms = jnp.sqrt(jnp.mean(norm_update * norm_update, 1))
        weight_rms = jnp.sqrt(jnp.mean(norm_params * norm_params, 1))
        step = STEP_RATE * jnp.maximum(EPS_TWO, weight_rms) / jnp.maximum(1.0, update_rms)
        norm_new = norm_params - step[:, None] * norm_update
        return (
            *y_parts,
            *dx_parts,
            slim_grad,
            broad_grad,
            slim_rows_new,
            broad_rows_new,
            slim_cols_new,
            broad_cols_new,
            slim_new,
            broad_new,
            slim_copy,
            broad_copy,
            norm_grad,
            norm_moments_new,
            norm_new,
        )

    return body


def solution(mesh):
    split = P(AXES)
    return jax.shard_map(
        make_body(mesh),
        mesh=mesh,
        in_specs=(split,) * 11 + (P(),) * 4,
        out_specs=(split,) * 10 + (P(),) * 2 + (split,) * 4 + (P(),) * 3,
        check_vma=False,
    )
```

time: 1400 us -> 722 us (0.52)
  waiting for transfers between devices: 599 us -> 325 us
  local copies, waits for them, and re-layouts: 360 us -> 109 us
  blocking collectives: 174 us -> 8.34 us
  Pallas kernels: 0 us -> 125 us
  other arithmetic: 138 us -> 29.5 us
  starting transfers between devices: 0.21 us -> 71.6 us
  matrix products: 92.5 us -> 26.4 us
    reduce_scatter x2 -> x0, waiting for transfers between devices: 434 us -> none  [the longest x1 251 us: body(): lax.psum_scatter(slim_term, ('wide', 'narrow'), scatter_dimension=0, tile...]
    ppermute x0 -> x74, waiting for transfers between devices: none -> 180 us  [the longest x31 151 us: swap(): return lax.ppermute(value, AXES, pairs)]
    psum x14 -> x1, blocking collectives: 174 us -> 8.34 us  [body(): cell_count = lax.psum(jnp.sum(mask), 'narrow')]
    slice x69 -> x10, local copies, waits for them, and re-layouts: 157 us -> 21.6 us  [the longest x6 14.1 us: split(): flat[offset:offset + length].reshape(images, extent, extent, flat.shape[1])]
    pallas_call x0 -> x26, Pallas kernels: none -> 125 us  [the longest x2 15.7 us: conv_grad(): kernel_call(conv_grad_kernel(stride), name, (9,), [whole((kinds_here, row...]
    ppermute x0 -> x74, starting transfers between devices: none -> 71.5 us  [the longest x31 35.3 us: swap(): return lax.ppermute(value, AXES, pairs)]
    dot_general x33 -> x3, matrix products: 92.5 us -> 26.4 us  [the longest x2 21.2 us: dot_nt(): lax.dot_general(first, second, (((1,), (1,)), ((), ())), preferred_elemen...]
    concatenate x37 -> x1, local copies, waits for them, and re-layouts: 45.6 us -> 0.08 us  [body(): jnp.concatenate([value.reshape(-1, c_out) for value in (cot_lo, cot_mid,...]
  transfers between devices with their start and end apart: 5 -> 76, of which waited for: 5 -> 29; matrix products, arithmetic and copies ran while one was open for 9% -> 19% of each run, Pallas kernels for 0% -> 10%
where the time goes in v1:
time: 722 us; the launch traced here: 714 us
  waiting for transfers between devices  325 us (45%)
  Pallas kernels  125 us (17%)
  local copies, waits for them, and re-layouts  109 us (15%)
  starting transfers between devices  71.6 us (10%)
  other arithmetic  29.5 us (4%)
  matrix products  26.4 us (4%)
  between operations  19.6 us (3%)
  blocking collectives  8.34 us (1%)
    ppermute x31, waiting for transfers between devices, swap(): return lax.ppermute(value, AXES, pairs)  151 us
    all_gather x1, waiting for transfers between devices, body(): slim = lax.all_gather(slim_master.astype(BF16), AXES, axis=0, tiled=True)  83 us
    all_gather x1, waiting for transfers between devices, body(): broad = lax.all_gather(broad_master.astype(BF16), AXES, axis=0, tiled=True)  62.2 us
    unnamed x222, local copies, waits for them, and re-layouts  50.6 us
    ppermute x31, starting transfers between devices, swap(): return lax.ppermute(value, AXES, pairs)  35.3 us
    ppermute x36, starting transfers between devices, group_parts(): lax.ppermute(value, 'narrow', [(i, i ^ k) for i in range(self.n_narrow)])  22.6 us
    dot_general x2, matrix products, dot_nt(): lax.dot_general(first, second, (((1,), (1,)), ((), ())), preferred_elemen...  21.2 us
    ppermute x7, waiting for transfers between devices, scatter(): came = lax.ppermute(current, AXES, pairs)  19.7 us
  transfers between devices with their start and end apart: 76, of which 29 were waited for; matrix products, arithmetic and copies ran while one was open for 19% of the time, Pallas kernels for 10%

profile of v1, /device:TPU:0, one launch (start us, length us, event | category | flops | bytes accessed | tf_op | source)
XLA Modules:
  0.0 714.3 jit_solution(6938804779038337884)
XLA Ops:
  27.2 83.0 %all-gather.3.cloned.1.call-done.w_ref.refs_9_.refs_10_.refs_14_.refs_13_ = bf16[12288,512]{1,0:T(8,128)(2,1)} async-done(((bf16[384,512]{1,0:T(8,128)(2,1)}), bf16[12288,512]{1,0:T(8,128)(2,1)}) %all-gather.3.cloned.1.call-update) | async-done | bytes 12582928 | tf_op jit(solution)/shard_map/all_gather | solution.py:665
  117.4 8.3 %psum.7 = f32[]{:T(128)} all-reduce(f32[]{:T(128)S(6)} %reduce_sum.48), channel_id=1, replica_groups=mesh['wide'=8,'narrow'=4] {'narrow'}, use_global_device_ids=true, to_apply=%region_3.4 | all-reduce | flops 1 | bytes 8 | tf_op jit(solution)/shard_map/psum | solution.py:685
  127.2 62.2 %all-gather.5.cloned.1.call-done.refs_8_.refs_13_.refs_15_ = bf16[2048,2048]{1,0:T(8,128)(2,1)} async-done(((bf16[64,2048]{1,0:T(8,128)(2,1)}), bf16[2048,2048]{1,0:T(8,128)(2,1)}) %all-gather.5.cloned.1.call-update) | async-done | bytes 8388624 | tf_op jit(solution)/shard_map/all_gather | solution.py:666
  194.3 10.9 %conv_two.1 = (bf16[4,320,512]{2,1,0:T(8,128)(2,1)S(1)}, f32[320,512]{1,0:T(8,128)S(1)}, f32[2,512]{1,0:T(2,128)S(1)}) custom-call(f32[4,320,512]{2,1,0:T(8,128)} %copy-done.5, f32[2,512]{1,0:T(2,128)S(1)} %get-tuple-element.71.refs_1_.refs_16_.refs_2_, f32[2,512]{1,0:T(2,128)S(1)} %collective-permute-done.refs_2_.refs_17_.refs_3_, ...), custom_call_target="tpu_custom_call" | custom-call | flops 2453667840 | bytes 12268339 | tf_op jit(solution)/shard_map/conv_two/pallas_call | solution.py:749
  236.1 9.0 %conv_five.1 = (bf16[1,320,512]{2,1,0:T(8,128)(2,1)S(1)}, f32[320,512]{1,0:T(8,128)S(1)}, f32[2,512]{1,0:T(2,128)S(1)}) custom-call(f32[1,320,512]{2,1,0:T(8,128)S(1)} %bitcast.131, f32[2,512]{1,0:T(2,128)S(1)} %get-tuple-element.79.refs_1_.refs_16_.refs_2_, f32[2,512]{1,0:T(2,128)S(1)} %collective-permute-done.9.refs_2_.refs_17_.refs_3_, ...), custom_call_target="tpu_custom_call" | custom-call | flops 2453667840 | bytes 12268339 | tf_op jit(solution)/shard_map/conv_five/pallas_call | solution.py:786
  317.0 9.5 %back_five.1 = (bf16[320,512]{1,0:T(8,128)(2,1)S(1)}, f32[1,320,512]{2,1,0:T(8,128)S(1)}, f32[2,512]{1,0:T(2,128)S(1)}) custom-call(f32[320,512]{1,0:T(8,128)S(1)} %get-tuple-element.88.refs_0_, f32[320,512]{1,0:T(8,128)S(1)} %copy-done.22, f32[2,512]{1,0:T(2,128)S(1)} %copy-done.71, f32[2,512]{1,0:T(2,128)S(1)} %copy-done.73, f32[2,512]{1,0:T(2,128)S(1)} %copy-done.75, ...), custom_call_target="tpu_custom_call" | custom-call | flops 2453667840 | bytes 12268339 | tf_op jit(solution)/shard_map/back_five/pallas_call | solution.py:895
  331.0 6.4 back_four.1
  343.4 7.8 %grad_five.1 = bf16[6144,512]{1,0:T(8,128)(2,1)} custom-call(bf16[1,320,512]{2,1,0:T(8,128)(2,1)S(1)} %copy-done.45, bf16[9,320,320]{2,1,0:T(8,128)(2,1)S(1)} %fusion.4.refs_8_.refs_13_.shift_ref, bf16[320,512]{1,0:T(8,128)(2,1)S(1)} %get-tuple-element.105.dz_ref, bf16[6144,512]{1,0:T(8,128)(2,1)} %grad_four.1.rest_0_), custom_call_target="tpu_custom_call", output_to_operand_aliasing={{}: (3, {})} | custom-call | flops 2453667840 | bytes 12268339 | tf_op jit(solution)/shard_map/grad_five/pallas_call | solution.py:874
  356.8 6.1 back_three.1
  378.0 13.5 %back_two.1 = (bf16[320,512]{1,0:T(8,128)(2,1)S(1)}, f32[4,320,512]{2,1,0:T(8,128)}, f32[2,512]{1,0:T(2,128)S(1)}) custom-call(f32[320,512]{1,0:T(8,128)S(1)} %copy-done.39, f32[320,512]{1,0:T(8,128)S(1)} %get-tuple-element.72.refs_0_.refs_16_.refs_1_, f32[2,512]{1,0:T(2,128)S(1)} %copy-done.55, f32[2,512]{1,0:T(2,128)S(1)} %copy-done.57, ...), custom_call_target="tpu_custom_call" | custom-call | flops 2453667840 | bytes 12268339 | tf_op jit(solution)/shard_map/back_two/pallas_call | solution.py:1011
  393.4 7.9 %grad_two.1.refs_14_ = bf16[6144,512]{1,0:T(8,128)(2,1)} custom-call(bf16[4,320,512]{2,1,0:T(8,128)(2,1)S(1)} %copy-done.37, bf16[9,320,320]{2,1,0:T(8,128)(2,1)S(1)} %fusion.4.refs_8_.refs_13_.shift_ref, bf16[320,512]{1,0:T(8,128)(2,1)S(1)} %get-tuple-element.99.dz_ref, bf16[6144,512]{1,0:T(8,128)(2,1)} %grad_four_low.1.rest_0_), custom_call_target="tpu_custom_call", output_to_operand_aliasing={{}: (3, {})} | custom-call | flops 2453667840 | bytes 12268339 | tf_op jit(solution)/shard_map/grad_two/pallas_call | solution.py:874
  407.5 7.1 back_one.1
  424.1 11.4 %collective-permute-done.52 = bf16[2,64,2048]{2,1,0:T(8,128)(2,1)S(1)} collective-permute-done((bf16[2,64,2048]{2,1,0:T(8,128)(2,1)S(1)}, bf16[2,64,2048]{2,1,0:T(8,128)(2,1)S(1)}, u32[]{:S(2)}, u32[]{:S(2)}) %collective-permute-start.52) | collective-permute-done | bytes 524320 | tf_op jit(solution)/shard_map/ppermute | solution.py:585
  436.5 12.0 %collective-permute-done.57 = bf16[2,64,2048]{2,1,0:T(8,128)(2,1)S(1)} collective-permute-done((bf16[2,64,2048]{2,1,0:T(8,128)(2,1)S(1)}, bf16[2,64,2048]{2,1,0:T(8,128)(2,1)S(1)}, u32[]{:S(2)}, u32[]{:S(2)}) %collective-permute-start.57) | collective-permute-done | bytes 524320 | tf_op jit(solution)/shard_map/ppermute | solution.py:585
  449.5 5.5 collective-permute-done.53
  478.5 18.4 %collective-permute-done.47 = bf16[4,64,2048]{2,1,0:T(8,128)(2,1)S(1)} collective-permute-done((bf16[4,64,2048]{2,1,0:T(8,128)(2,1)S(1)}, bf16[4,64,2048]{2,1,0:T(8,128)(2,1)S(1)}, u32[]{:S(2)}, u32[]{:S(2)}) %collective-permute-start.47) | collective-permute-done | bytes 1048608 | tf_op jit(solution)/shard_map/ppermute | solution.py:585
  501.2 29.4 %collective-permute-done.37 = bf16[4,384,512]{2,1,0:T(8,128)(2,1)S(1)} collective-permute-done((bf16[4,384,512]{2,1,0:T(8,128)(2,1)S(1)}, bf16[4,384,512]{2,1,0:T(8,128)(2,1)S(1)}, u32[]{:S(2)}, u32[]{:S(2)}) %collective-permute-start.37) | collective-permute-done | bytes 1572896 | tf_op jit(solution)/shard_map/ppermute | solution.py:585
  531.9 26.7 %collective-permute-done.42 = bf16[4,384,512]{2,1,0:T(8,128)(2,1)S(1)} collective-permute-done((bf16[4,384,512]{2,1,0:T(8,128)(2,1)S(1)}, bf16[4,384,512]{2,1,0:T(8,128)(2,1)S(1)}, u32[]{:S(2)}, u32[]{:S(2)}) %collective-permute-start.42) | collective-permute-done | bytes 1572896 | tf_op jit(solution)/shard_map/ppermute | solution.py:585
  561.4 17.7 %collective-permute-done.38 = bf16[2,384,512]{2,1,0:T(8,128)(2,1)S(1)} collective-permute-done((bf16[2,384,512]{2,1,0:T(8,128)(2,1)S(1)}, bf16[2,384,512]{2,1,0:T(8,128)(2,1)S(1)}, u32[]{:S(2)}, u32[]{:S(2)}) %collective-permute-start.38) | collective-permute-done | bytes 786464 | tf_op jit(solution)/shard_map/ppermute | solution.py:585
  594.6 9.6 %collective-permute-done.39 = bf16[1,384,512]{2,1,0:T(8,128)(2,1)S(1)} collective-permute-done((bf16[1,384,512]{2,1,0:T(8,128)(2,1)S(1)}, bf16[1,384,512]{2,1,0:T(8,128)(2,1)S(1)}, u32[]{:S(2)}, u32[]{:S(2)}) %collective-permute-start.39) | collective-permute-done | bytes 393248 | tf_op jit(solution)/shard_map/ppermute | solution.py:585
  612.9 11.5 %collective-permute-done.50 = bf16[64,2048]{1,0:T(8,128)(2,1)S(1)} collective-permute-done((bf16[64,2048]{1,0:T(8,128)(2,1)S(1)}, bf16[64,2048]{1,0:T(8,128)(2,1)S(1)}, u32[]{:S(2)}, u32[]{:S(2)}) %collective-permute-start.50) | collective-permute-done | bytes 262176 | tf_op jit(solution)/shard_map/ppermute | solution.py:620
  631.1 12.6 %fusion.22 = f32[1240,1024]{1,0:T(8,128)} fusion(bf16[320,2048]{1,0:T(8,128)(2,1)S(1)} %copy-done.25, s32[1240]{0:T(1024)S(1)} %copy-done.98, bf16[2048,2048]{1,0:T(8,128)(2,1)} %all-gather.5.cloned.1.call-done.refs_8_.refs_13_.refs_15_), kind=kOutput, calls=%fused_computation.44 | convolution fusion | flops 6829166080 | bytes 10589024 | tf_op jit(solution)/shard_map/dot_general | solution.py:53
  648.5 8.6 %convolution_add_fusion = f32[1240,1024]{1,0:T(8,128)} fusion(f32[1240,1024]{1,0:T(8,128)} %fusion.22, bf16[12288,512]{1,0:T(8,128)(2,1)} %all-gather.3.cloned.1.call-done.w_ref.refs_9_.refs_10_.refs_14_.refs_13_, bf16[1280,512]{1,0:T(8,128)(2,1)} %bitcast.134, s32[1240]{0:T(1024)S(1)} %copy-done.97), kind=kOutput, calls=%fused_computation.9 | convolution fusion | flops 2929018880 | bytes 12522336 | tf_op jit(solution)/shard_map/dot_general | solution.py:53
  678.6 5.6 copy.162
  (494 shorter events, 294.1 us)
Async XLA Ops:
  7.2 103.0 %all-gather.3.cloned.1.call-start = ((), (), s32[]{:S(2)}) async-start(), calls=%async_computation | async-start | bytes 12976128 | tf_op jit(solution)/shard_map/all_gather | solution.py:665
  9.3 180.0 %all-gather.5.cloned.1.call-start = ((), (), s32[]{:S(2)}) async-start(), calls=%async_computation.1 | async-start | bytes 8650752 | tf_op jit(solution)/shard_map/all_gather | solution.py:666
  115.0 79.2 %collective-permute-start = (f32[2,512]{1,0:T(2,128)S(1)}, f32[2,512]{1,0:T(2,128)S(1)}, u32[]{:S(2)}, u32[]{:S(2)}) collective-permute-start(f32[2,512]{1,0:T(2,128)S(1)} %get-tuple-element.71.refs_1_.refs_16_.refs_2_), channel_id=1, source_target_pairs={{0,1},{1,0},{2,3},{3,2},{4,5},{5,4},{6,7},{7,6},{8,9},{9,8},{10,11... | collective-permute-start | bytes 12296 | tf_op jit(solution)/shard_map/ppermute | solution.py:589
  115.3 78.9 %collective-permute-start.1 = (f32[2,512]{1,0:T(2,128)S(1)}, f32[2,512]{1,0:T(2,128)S(1)}, u32[]{:S(2)}, u32[]{:S(2)}) collective-permute-start(f32[2,512]{1,0:T(2,128)S(1)} %get-tuple-element.71.refs_1_.refs_16_.refs_2_), channel_id=1, source_target_pairs={{0,2},{1,3},{2,0},{3,1},{4,6},{5,7},{6,4},{7,5},{8,10},{9,11},{10,... | collective-permute-start | bytes 12296 | tf_op jit(solution)/shard_map/ppermute | solution.py:589
  116.7 77.5 %collective-permute-start.2 = (f32[2,512]{1,0:T(2,128)S(1)}, f32[2,512]{1,0:T(2,128)S(1)}, u32[]{:S(2)}, u32[]{:S(2)}) collective-permute-start(f32[2,512]{1,0:T(2,128)S(1)} %get-tuple-element.71.refs_1_.refs_16_.refs_2_), channel_id=1, source_target_pairs={{0,3},{1,2},{2,1},{3,0},{4,7},{5,6},{6,5},{7,4},{8,11},{9,10},{10,... | collective-permute-start | bytes 12296 | tf_op jit(solution)/shard_map/ppermute | solution.py:589
  277.6 24.4 %collective-permute-start.18 = (f32[2,2048]{1,0:T(2,128)S(1)}, f32[2,2048]{1,0:T(2,128)S(1)}, u32[]{:S(2)}, u32[]{:S(2)}) collective-permute-start(f32[2,2048]{1,0:T(2,128)S(1)} %get-tuple-element.87.refs_6_), channel_id=1, source_target_pairs={{0,1},{1,0},{2,3},{3,2},{4,5},{5,4},{6,7},{7,6},{8,9},{9,8},{10,11... | collective-permute-start | bytes 49160 | tf_op jit(solution)/shard_map/ppermute | solution.py:589
  277.7 24.3 %collective-permute-start.19 = (f32[2,2048]{1,0:T(2,128)S(1)}, f32[2,2048]{1,0:T(2,128)}, u32[]{:S(2)}, u32[]{:S(2)}) collective-permute-start(f32[2,2048]{1,0:T(2,128)S(1)} %get-tuple-element.87.refs_6_), channel_id=1, source_target_pairs={{0,2},{1,3},{2,0},{3,1},{4,6},{5,7},{6,4},{7,5},{8,10},{9,11},{10,... | collective-permute-start | bytes 49160 | tf_op jit(solution)/shard_map/ppermute | solution.py:589
  278.5 23.5 %collective-permute-start.20 = (f32[2,2048]{1,0:T(2,128)S(1)}, f32[2,2048]{1,0:T(2,128)}, u32[]{:S(2)}, u32[]{:S(2)}) collective-permute-start(f32[2,2048]{1,0:T(2,128)S(1)} %get-tuple-element.87.refs_6_), channel_id=1, source_target_pairs={{0,3},{1,2},{2,1},{3,0},{4,7},{5,6},{6,5},{7,4},{8,11},{9,10},{10,... | collective-permute-start | bytes 49160 | tf_op jit(solution)/shard_map/ppermute | solution.py:589
  329.5 88.6 %collective-permute-start.51 = (bf16[4,64,2048]{2,1,0:T(8,128)(2,1)}, bf16[4,64,2048]{2,1,0:T(8,128)(2,1)}, u32[]{:S(2)}, u32[]{:S(2)}) collective-permute-start(bf16[4,64,2048]{2,1,0:T(8,128)(2,1)} %dynamic-slice_bitcast_fusion.6), channel_id=1, source_target_pairs={{0,1},{1,0},{2,3},{3,2},{4,5},{5,4},{6,7},{7,6},{8,9},{9,8},{10,11... | collective-permute-start | bytes 3145736 | tf_op jit(solution)/shard_map/ppermute | solution.py:585
  355.0 115.7 %collective-permute-start.36 = (bf16[8,384,512]{2,1,0:T(8,128)(2,1)}, bf16[8,384,512]{2,1,0:T(8,128)(2,1)}, u32[]{:S(2)}, u32[]{:S(2)}) collective-permute-start(bf16[8,384,512]{2,1,0:T(8,128)(2,1)} %dynamic-slice_bitcast_fusion.1), channel_id=1, source_target_pairs={{0,1},{1,0},{2,3},{3,2},{4,5},{5,4},{6,7},{7,6},{8,9},{9,8},{10,11... | collective-permute-start | bytes 9437192 | tf_op jit(solution)/shard_map/ppermute | solution.py:585
  402.0 67.0 %collective-permute-start.46 = (bf16[8,64,2048]{2,1,0:T(8,128)(2,1)}, bf16[8,64,2048]{2,1,0:T(8,128)(2,1)S(1)}, u32[]{:S(2)}, u32[]{:S(2)}) collective-permute-start(bf16[8,64,2048]{2,1,0:T(8,128)(2,1)} %dynamic-slice_bitcast_fusion.2), channel_id=1, source_target_pairs={{0,1},{1,0},{2,3},{3,2},{4,5},{5,4},{6,7},{7,6},{8,9},{9,8},{10,11... | collective-permute-start | bytes 6291464 | tf_op jit(solution)/shard_map/ppermute | solution.py:585
  417.3 57.9 %collective-permute-start.41 = (bf16[8,384,512]{2,1,0:T(8,128)(2,1)S(1)}, bf16[8,384,512]{2,1,0:T(8,128)(2,1)S(1)}, u32[]{:S(2)}, u32[]{:S(2)}) collective-permute-start(bf16[8,384,512]{2,1,0:T(8,128)(2,1)S(1)} %dynamic-slice_bitcast_fusion), channel_id=1, source_target_pairs={{0,1},{1,0},{2,3},{3,2},{4,5},{5,4},{6,7},{7,6},{8,9},{9,8},{10,11... | collective-permute-start | bytes 9437192 | tf_op jit(solution)/shard_map/ppermute | solution.py:585
  418.2 225.5 %collective-permute-start.72 = (f32[2,8192]{1,0:T(2,128)}, f32[2,8192]{1,0:T(2,128)}, u32[]{:S(2)}, u32[]{:S(2)}) collective-permute-start(f32[2,8192]{1,0:T(2,128)} %add.313), channel_id=1, source_target_pairs={{0,8},{1,9},{2,10},{3,11},{4,12},{5,13},{6,14},{7,15},{8,0},{9,1},... | collective-permute-start | bytes 196616 | tf_op jit(solution)/shard_map/ppermute | solution.py:585
  469.1 142.1 %collective-permute-start.55 = (bf16[64,2048]{1,0:T(8,128)(2,1)S(1)}, bf16[64,2048]{1,0:T(8,128)(2,1)S(1)}, u32[]{:S(2)}, u32[]{:S(2)}) collective-permute-start(bf16[64,2048]{1,0:T(8,128)(2,1)S(1)} %add_convert_fusion.4), channel_id=1, source_target_pairs={{8,24},{9,25},{10,26},{11,27},{12,28},{13,29},{14,30},{15,31}} | collective-permute-start | bytes 786440 | tf_op jit(solution)/shard_map/ppermute | solution.py:620
  470.7 26.2 %collective-permute-start.47 = (bf16[4,64,2048]{2,1,0:T(8,128)(2,1)S(1)}, bf16[4,64,2048]{2,1,0:T(8,128)(2,1)S(1)}, u32[]{:S(2)}, u32[]{:S(2)}) collective-permute-start(bf16[4,64,2048]{2,1,0:T(8,128)(2,1)S(1)} %dynamic-slice_bitcast_fusion.7), channel_id=1, source_target_pairs={{0,2},{1,3},{2,0},{3,1},{4,6},{5,7},{6,4},{7,5},{8,10},{9,11},{10,... | collective-permute-start | bytes 3145736 | tf_op jit(solution)/shard_map/ppermute | solution.py:585
  475.1 55.4 %collective-permute-start.37 = (bf16[4,384,512]{2,1,0:T(8,128)(2,1)S(1)}, bf16[4,384,512]{2,1,0:T(8,128)(2,1)S(1)}, u32[]{:S(2)}, u32[]{:S(2)}) collective-permute-start(bf16[4,384,512]{2,1,0:T(8,128)(2,1)S(1)} %dynamic-slice_bitcast_fusion.4), channel_id=1, source_target_pairs={{0,2},{1,3},{2,0},{3,1},{4,6},{5,7},{6,4},{7,5},{8,10},{9,11},{10,... | collective-permute-start | bytes 4718600 | tf_op jit(solution)/shard_map/ppermute | solution.py:585
  477.5 81.1 %collective-permute-start.42 = (bf16[4,384,512]{2,1,0:T(8,128)(2,1)S(1)}, bf16[4,384,512]{2,1,0:T(8,128)(2,1)S(1)}, u32[]{:S(2)}, u32[]{:S(2)}) collective-permute-start(bf16[4,384,512]{2,1,0:T(8,128)(2,1)S(1)} %dynamic-slice_bitcast_fusion.3), channel_id=1, source_target_pairs={{0,2},{1,3},{2,0},{3,1},{4,6},{5,7},{6,4},{7,5},{8,10},{9,11},{10,... | collective-permute-start | bytes 4718600 | tf_op jit(solution)/shard_map/ppermute | solution.py:585
  496.8 116.0 %collective-permute-start.60 = (bf16[64,2048]{1,0:T(8,128)(2,1)S(1)}, bf16[64,2048]{1,0:T(8,128)(2,1)S(1)}, u32[]{:S(2)}, u32[]{:S(2)}) collective-permute-start(bf16[64,2048]{1,0:T(8,128)(2,1)S(1)} %add_convert_fusion.2), channel_id=1, source_target_pairs={{0,16},{1,17},{2,18},{3,19},{4,20},{5,21},{6,22},{7,23}} | collective-permute-start | bytes 786440 | tf_op jit(solution)/shard_map/ppermute | solution.py:620
  530.6 29.4 %collective-permute-start.48 = (bf16[2,64,2048]{2,1,0:T(8,128)(2,1)S(1)}, bf16[2,64,2048]{2,1,0:T(8,128)(2,1)S(1)}, u32[]{:S(2)}, u32[]{:S(2)}) collective-permute-start(bf16[2,64,2048]{2,1,0:T(8,128)(2,1)S(1)} %dynamic-slice_bitcast_fusion.12), channel_id=1, source_target_pairs={{0,4},{1,5},{2,6},{3,7},{4,0},{5,1},{6,2},{7,3},{8,12},{9,13},{10,... | collective-permute-start | bytes 1572872 | tf_op jit(solution)/shard_map/ppermute | solution.py:585
  558.6 20.5 %collective-permute-start.38 = (bf16[2,384,512]{2,1,0:T(8,128)(2,1)S(1)}, bf16[2,384,512]{2,1,0:T(8,128)(2,1)S(1)}, u32[]{:S(2)}, u32[]{:S(2)}) collective-permute-start(bf16[2,384,512]{2,1,0:T(8,128)(2,1)S(1)} %dynamic-slice_bitcast_fusion.9), channel_id=1, source_target_pairs={{0,4},{1,5},{2,6},{3,7},{4,0},{5,1},{6,2},{7,3},{8,12},{9,13},{10,... | collective-permute-start | bytes 2359304 | tf_op jit(solution)/shard_map/ppermute | solution.py:585
  560.0 29.4 %collective-permute-start.43 = (bf16[2,384,512]{2,1,0:T(8,128)(2,1)S(1)}, bf16[2,384,512]{2,1,0:T(8,128)(2,1)S(1)}, u32[]{:S(2)}, u32[]{:S(2)}) collective-permute-start(bf16[2,384,512]{2,1,0:T(8,128)(2,1)S(1)} %dynamic-slice_bitcast_fusion.8), channel_id=1, source_target_pairs={{0,4},{1,5},{2,6},{3,7},{4,0},{5,1},{6,2},{7,3},{8,12},{9,13},{10,... | collective-permute-start | bytes 2359304 | tf_op jit(solution)/shard_map/ppermute | solution.py:585
  644.6 42.8 %collective-permute-start.73 = (f32[2,8192]{1,0:T(2,128)S(1)}, f32[2,8192]{1,0:T(2,128)}, u32[]{:S(2)}, u32[]{:S(2)}) collective-permute-start(f32[2,8192]{1,0:T(2,128)S(1)} %add.314), channel_id=1, source_target_pairs={{0,16},{1,17},{2,18},{3,19},{4,20},{5,21},{6,22},{7,23},{8,24},{9,... | collective-permute-start | bytes 196616 | tf_op jit(solution)/shard_map/ppermute | solution.py:585
  645.6 38.6 %collective-permute-start.67 = (f32[12,2048]{1,0:T(8,128)S(1)}, f32[12,2048]{1,0:T(8,128)}, u32[]{:S(2)}, u32[]{:S(2)}) collective-permute-start(f32[12,2048]{1,0:T(8,128)S(1)} %add.290), channel_id=1, source_target_pairs={{0,2},{1,3},{2,0},{3,1},{4,6},{5,7},{6,4},{7,5},{8,10},{9,11},{10,... | collective-permute-start | bytes 294920 | tf_op jit(solution)/shard_map/ppermute | solution.py:585
  647.3 38.8 %collective-permute-start.62 = (f32[16,512]{1,0:T(8,128)S(1)}, f32[16,512]{1,0:T(8,128)S(1)}, u32[]{:S(2)}, u32[]{:S(2)}) collective-permute-start(f32[16,512]{1,0:T(8,128)S(1)} %add.285), channel_id=1, source_target_pairs={{0,2},{1,3},{2,0},{3,1},{4,6},{5,7},{6,4},{7,5},{8,10},{9,11},{10,... | collective-permute-start | bytes 98312 | tf_op jit(solution)/shard_map/ppermute | solution.py:585
  (156 other events, 1593.0 us)
Sparse Core Ops, SparseCore 0:
  11.5 98.6 all-gather.2
  113.6 75.6 all-gather.4

commit v2 on v1

--- a/solution.py
+++ b/solution.py
@@ -30,19 +30,54 @@
     return pl.BlockSpec(dims, place)
 
 
-def kernel_call(body, name, grid, in_specs, out_specs, out_shape, flops, scratch=(), aliases=None):
-    return pl.pallas_call(
+class Kernels:
+    def __init__(self):
+        self.last = None
+
+    def __call__(
+        self,
         body,
-        grid=grid,
-        in_specs=in_specs,
-        out_specs=out_specs,
-        out_shape=out_shape,
-        scratch_shapes=list(scratch),
-        input_output_aliases=aliases or {},
-        cost_estimate=pl.CostEstimate(flops=flops, bytes_accessed=flops // 200, transcendentals=0),
-        compiler_params=pltpu.CompilerParams(vmem_limit_bytes=VMEM_LIMIT),
-        name=name,
-    )
+        name,
+        grid,
+        in_specs,
+        out_specs,
+        out_shape,
+        flops,
+        scratch=(),
+        aliases=None,
+        after=(),
+        scalars=0,
+    ):
+        after = [value for value in (*after, self.last) if value is not None]
+        taken = scalars + len(in_specs)
+
+        def trimmed(*refs):
+            body(*refs[:taken], *refs[taken + len(after) :])
+
+        call = pl.pallas_call(
+            trimmed,
+            grid_spec=pltpu.PrefetchScalarGridSpec(
+                num_scalar_prefetch=scalars,
+                grid=grid,
+                in_specs=list(in_specs) + [pl.BlockSpec(memory_space=pl.ANY)] * len(after),
+                out_specs=out_specs,
+                scratch_shapes=list(scratch),
+            ),
+            out_shape=out_shape,
+            input_output_aliases=aliases or {},
+            cost_estimate=pl.CostEstimate(
+                flops=flops, bytes_accessed=flops // 200, transcendentals=0
+            ),
+            compiler_params=pltpu.CompilerParams(vmem_limit_bytes=VMEM_LIMIT),
+            name=name,
+        )
+
+        def run(*args):
+            out = call(*args, *after)
+            self.last = out[0] if isinstance(out, (list, tuple)) else out
+            return out
+
+        return run
 
 
 def dot_nn(first, second):
@@ -97,16 +132,16 @@
     base_in, base_out = 0, 0
     for side in sides_out:
         extent = 2 * side
-        for image in range(images):
-            for row in range(side):
-                for col in range(side):
+        for row in range(side):
+            for col in range(side):
+                for image in range(images):
                     for kind in range(4):
-                        row_in, col_in = 2 * row + kind // 2, 2 * col + kind % 2
-                        table[kind, base_out + row * side + col] = (
-                            base_in + row_in * extent + col_in
+                        cell = (2 * row + kind // 2) * extent + 2 * col + kind % 2
+                        table[kind, base_out + (row * side + col) * images + image] = (
+                            base_in + cell * images + image
                         )
-            base_in += extent * extent
-            base_out += side * side
+        base_in += images * extent * extent
+        base_out += images * side * side
     return table
 
 
@@ -114,14 +149,16 @@
     table = -np.ones((9, padded), np.int32)
     base = 0
     for side in sides_out:
-        for _ in range(images):
-            for row in range(side):
-                for col in range(side):
-                    for which in range(9):
-                        row_to, col_to = row + which // 3 - 1, col + which % 3 - 1
-                        if 0 <= row_to < side and 0 <= col_to < side:
-                            table[which, base + row * side + col] = base + row_to * side + col_to
-            base += side * side
+        for row in range(side):
+            for col in range(side):
+                for which in range(9):
+                    row_to, col_to = row + which // 3 - 1, col + which % 3 - 1
+                    if 0 <= row_to < side and 0 <= col_to < side:
+                        for image in range(images):
+                            table[which, base + (row * side + col) * images + image] = (
+                                base + (row_to * side + col_to) * images + image
+                            )
+        base += images * side * side
     return table
 
 
@@ -144,9 +181,19 @@
 
 
 def side_kernel(x_ref, w_ref, mask_ref, z_ref, stat_ref):
-    z = dot_nn(x_ref[0], w_ref[...])
-    z_ref[...] = z
-    stat_ref[...] = stat_rows(z, mask_ref[...])
+    term = dot_nn(x_ref[0], w_ref[...])
+
+    @pl.when(pl.program_id(1) == 0)
+    def _():
+        z_ref[...] = term
+
+    @pl.when(pl.program_id(1) > 0)
+    def _():
+        z_ref[...] += term
+
+    @pl.when(pl.program_id(1) == pl.num_programs(1) - 1)
+    def _():
+        stat_ref[...] = stat_rows(z_ref[...], mask_ref[...])
 
 
 def tap_forward(tap, stride):
@@ -270,27 +317,60 @@
     return body
 
 
-def output_kernel(count):
+def cell_rows(images, sides):
+    base = 0
+    for level, side in enumerate(sides):
+        for row in range(side):
+            for col in range(side):
+                yield level, row, col, base + (row * side + col) * images
+        base += images * side * side
+
+
+def output_kernel(count, images, sides):
     def body(*refs):
         z_ref = refs[0]
         parts = refs[1 : 1 + count]
-        affine_ref, recip_ref, mask_ref, hidden_ref, cot_ref, y_ref, grad_ref, stat_ref = refs[
-            1 + count :
-        ]
+        affine_ref, recip_ref, mask_ref, hidden_ref = refs[1 + count : 5 + count]
+        cot_refs = refs[5 + count : 8 + count]
+        y_refs = refs[8 + count : 11 + count]
+        grad_ref, stat_ref, flat_ref = refs[11 + count :]
+        used = grid_rows(images, sides)
+        if flat_ref.shape[0] > used:
+            flat_ref[used:] = jnp.zeros((flat_ref.shape[0] - used, flat_ref.shape[1]), F32)
+        for level, row, col, at in cell_rows(images, sides):
+            flat_ref[at : at + images] = cot_refs[level][row, col].astype(F32)
         mean, inv = moments(parts, recip_ref[...])
         normed = (z_ref[...] - mean) * inv
         pre = affine_ref[0:1] * normed + affine_ref[1:2] + hidden_ref[...]
         gate = sigmoid(pre)
-        y_ref[...] = (pre * gate).astype(BF16)
-        grad = cot_ref[...].astype(F32) * mask_ref[...] * (gate * (1.0 + pre * (1.0 - gate)))
+        grad = flat_ref[...] * mask_ref[...] * (gate * (1.0 + pre * (1.0 - gate)))
         grad_ref[...] = grad
-        stat_ref[...] = jnp.concatenate([column_sum(grad), column_sum(grad * normed)], 0)
+        stat_ref[...] = jnp.concatenate([column_sum(grad * normed), column_sum(grad)], 0)
+        flat_ref[...] = pre * gate
+        for level, row, col, at in cell_rows(images, sides):
+            y_refs[level][row, col] = flat_ref[at : at + images].astype(BF16)
+
+    return body
+
+
+def input_grad_kernel(images, sides):
+    def body(dz_ref, w_ref, side_ref, w_side_ref, *rest):
+        out_refs, flat_ref = rest[:3], rest[3]
+        for kind in range(4):
+            value = dot_nt(dz_ref[kind], w_ref[...])
+            if kind == 0:
+                value += dot_nt(side_ref[...], w_side_ref[...])
+            flat_ref[...] = value
+            for level, row, col, at in cell_rows(images, sides):
+                out_refs[level][2 * row + kind // 2, 2 * col + kind % 2] = flat_ref[
+                    at : at + images
+                ]
 
     return body
 
 
 def norm_back(grad, normed, sums, recip, mask, scale):
-    return scale * (grad - mask * (sums[0:1] * recip + normed * (sums[1:2] * recip)))
+    return scale * (grad - mask * (sums[1:2] * recip + normed * (sums[0:1] * recip)))
 
 
 def back_linear_kernel(count):
@@ -331,7 +411,7 @@
     pre = below_affine_ref[0:1] * normed + below_affine_ref[1:2]
     grad = out_ref[...] * slope(pre)
     out_ref[...] = grad
-    stat_ref[...] = jnp.concatenate([column_sum(grad), column_sum(grad * normed)], 0)
+    stat_ref[...] = jnp.concatenate([column_sum(grad * normed), column_sum(grad)], 0)
 
 
 def back_conv_kernel(count, kinds, stride):
@@ -371,7 +451,7 @@
                 pre = below_affine_ref[0:1] * normed + below_affine_ref[1:2]
                 grad = out_ref[which] * slope(pre)
                 out_ref[which] = grad
-                part = jnp.concatenate([column_sum(grad), column_sum(grad * normed)], 0)
+                part = jnp.concatenate([column_sum(grad * normed), column_sum(grad)], 0)
                 rows = part if rows is None else rows + part
             stat_ref[...] = rows
 
@@ -412,7 +492,7 @@
         grad = (above_ref[...] + dot_nt(dz_ref[...], w_ref[...])) * slope(pre)
         out_ref[...] = grad
         stat_ref[...] = jnp.concatenate(
-            [column_sum(grad), column_sum(grad * normed), column_sum(grad * normed_side)], 0
+            [column_sum(grad * normed), column_sum(grad), column_sum(grad * normed_side)], 0
         )
 
     return body
@@ -438,7 +518,7 @@
         dz = norm_back(grad, normed, total[0:2], recip, mask, affine_mid_ref[0:1] * inv)
         dz = dz.astype(BF16)
         dz_ref[...] = dz
-        total_side = jnp.concatenate([total[0:1], total[2:3]], 0)
+        total_side = jnp.concatenate([total[2:3], total[1:2]], 0)
         dz_side_ref[...] = norm_back(
             grad, normed_side, total_side, recip, mask, affine_side_ref[0:1] * inv_side
         ).astype(BF16)
@@ -495,11 +575,40 @@
     rest[-1][...] = dot_tn(act_ref[...], dz_ref[...]).astype(BF16)
 
 
-def conv_grad_kernel(stride):
+def conv_grad_kernel(stride, first):
     def body(act_ref, shift_ref, dz_ref, *rest):
-        kind, shift = tap_forward(pl.program_id(0), stride)
+        kind, shift = tap_forward(pl.program_id(0) + first, stride)
         patch = dot_nn(shift_ref[shift], act_ref[kind]).astype(BF16)
         rest[-1][...] = dot_tn(patch, dz_ref[...]).astype(BF16)
+
+    return body
+
+
+def pack_kernel(count, spans):
+    def body(*refs):
+        out_ref = refs[-1]
+        for which, (start, stop, rows) in enumerate(spans):
+            parts = refs[which * count : (which + 1) * count]
+            total = tree_sum([part[...] for part in parts])
+            for slot, row in enumerate(rows):
+                out_ref[slot : slot + 1, start:stop] = total[row : row + 1]
+
+    return body
+
+
+def merge_kernel(split, has_kept, last):
+    def add(kept_ref, came_ref):
+        total = kept_ref[...].astype(F32) + came_ref[...].astype(F32)
+        return total if last else total.astype(BF16)
+
+    def body(index_ref, *refs):
+        if not has_kept:
+            refs[1][...] = refs[0][...]
+        elif split:
+            refs[4][...] = add(refs[0], refs[1])
+            refs[5][...] = add(refs[2], refs[3])
+        else:
+            refs[2][...] = add(refs[0], refs[1])
 
     return body
 
@@ -595,35 +704,129 @@
             value = value + self.swap(value, level)
         return value
 
-    def scatter(self, part, prefix):
-        open_bits = self.bits - len(prefix)
-        rows = part.shape[0] >> open_bits
-        current = part
-        for level in range(open_bits):
-            view = current.reshape((1 << (open_bits - level - 1), 2, rows, part.shape[1]))
-            mine = self.bit(level)
-            sent = lax.dynamic_index_in_dim(view, 1 - mine, 1, keepdims=False)
-            kept = lax.dynamic_index_in_dim(view, mine, 1, keepdims=False)
-            came = self.swap(sent, level)
-            current = self.add(kept, came, level)
-        current = current.reshape(rows, part.shape[1])
-        for level in range(open_bits, self.bits):
-            want = prefix[level - open_bits]
+
+def insert_bit(unit, place, bit):
+    return ((unit >> place) << (place + 1)) | (bit << place) | (unit & ((1 << place) - 1))
+
+
+class Scatter:
+    def __init__(self, link, kernels, part, name, prefix=(), swap=False):
+        self.link = link
+        self.kernels = kernels
+        self.name = name
+        self.prefix = prefix
+        self.open_bits = link.bits - len(prefix)
+        units = 1 << self.open_bits
+        self.kept = part.reshape(units, part.shape[0] // units, part.shape[1])
+        self.left = list(range(self.open_bits))
+        self.levels = list(range(self.open_bits))
+        if swap:
+            self.levels[1], self.levels[2] = self.levels[2], self.levels[1]
+        self.levels += list(range(self.open_bits, link.bits))
+        self.at = 0
+        self.came = None
+        self.chosen = None
+        self.send_half(None)
+
+    def place(self, level):
+        return self.left.index(level)
+
+    def unit_spec(self, source):
+        dims = (1,) + self.kept.shape[1:]
+        return block(dims, lambda unit, index: (source(unit, index[0]), 0, 0))
+
+    def kept_source(self, source):
+        if self.chosen is None:
+            return source
+        place, level = self.chosen
+        return lambda unit, index: insert_bit(
+            source(unit, index), place, (index >> level) & 1
+        )
+
+    def run(self, body, specs, outs, number, args, dtype):
+        spec = self.unit_spec(lambda unit, index: unit)
+        shape = shape_of((number,) + self.kept.shape[1:], dtype)
+        out = self.kernels(
+            body,
+            self.name + "_" + str(self.at),
+            (number,),
+            specs,
+            [spec] * outs,
+            [shape] * outs,
+            4 * number * self.kept.shape[1] * self.kept.shape[2] * 200,
+            scalars=1,
+        )(self.link.index.astype(jnp.int32).reshape(1), *args)
+        return out
+
+    def send_half(self, came):
+        level = self.levels[self.at] if self.at < len(self.levels) else None
+        total_units = 1 << len(self.left)
+        if level is not None and level < self.open_bits:
+            place = self.place(level)
+
+            def keep(unit, index):
+                return insert_bit(unit, place, (index >> level) & 1)
+
+            def send(unit, index):
+                return insert_bit(unit, place, 1 - ((index >> level) & 1))
+
+            half = total_units // 2
+            if came is None:
+                (sent,) = self.run(
+                    merge_kernel(True, False, False),
+                    [self.unit_spec(send)],
+                    1,
+                    half,
+                    [self.kept],
+                    BF16,
+                )
+                self.chosen = (place, level)
+            else:
+                kept_keep = self.unit_spec(self.kept_source(keep))
+                kept_send = self.unit_spec(self.kept_source(send))
+                kept, sent = self.run(
+                    merge_kernel(True, True, False),
+                    [kept_keep, self.unit_spec(keep), kept_send, self.unit_spec(send)],
+                    2,
+                    half,
+                    [self.kept, came, self.kept, came],
+                    BF16,
+                )
+                self.kept, self.chosen = kept, None
+            self.left.remove(level)
+            self.came = self.link.swap(sent, level)
+        else:
+            same = lambda unit, index: unit
+            (self.kept,) = self.run(
+                merge_kernel(False, True, level is None),
+                [self.unit_spec(self.kept_source(same)), self.unit_spec(same)],
+                1,
+                total_units,
+                [self.kept, came],
+                F32 if level is None else BF16,
+            )
+            self.chosen = None
+            if level is None:
+                return
             pairs = []
-            for device in range(self.total):
+            for device in range(self.link.total):
                 settled = all(
-                    (device >> other) & 1 == prefix[other - open_bits]
-                    for other in range(open_bits, level)
+                    (device >> other) & 1 == self.prefix[other - self.open_bits]
+                    for other in range(self.open_bits, level)
                 )
-                if settled and (device >> level) & 1 != want:
+                if settled and (device >> level) & 1 != self.prefix[level - self.open_bits]:
                     pairs.append((device, device ^ (1 << level)))
-            came = lax.ppermute(current, AXES, pairs)
-            current = self.add(current, came, level)
-        return current
-
-    def add(self, kept, came, level):
-        total = kept.astype(F32) + came.astype(F32)
-        return total if level == self.bits - 1 else total.astype(BF16)
+            self.came = lax.ppermute(self.kept, AXES, pairs)
+
+    def step(self, number=1):
+        for _ in range(number):
+            if self.at < len(self.levels):
+                self.at += 1
+                self.send_half(self.came)
+
+    def finish(self):
+        self.step(len(self.levels))
+        return self.kept.reshape(self.kept.shape[1:])
 
 
 def make_body(mesh):
@@ -647,6 +850,7 @@
         norm_moments,
     ):
         link = Exchange(n_wide, n_narrow)
+        kernel_call = Kernels()
         count = n_narrow
         images = x_lo.shape[0]
         sides = tuple(value.shape[1] // 2 for value in (x_lo, x_mid, x_hi))
@@ -667,25 +871,26 @@
 
         kinds = class_table(images, sides, rows)
         shifts = one_hot(shift_table(images, sides, rows), rows)
-        x_flat = jnp.concatenate([value.reshape(-1, c_in) for value in (x_lo, x_mid, x_hi)], 0)
+
+        def by_cell(value):
+            return jnp.transpose(value, (1, 2, 0, 3))
+
+        x_flat = jnp.concatenate(
+            [by_cell(value).reshape(-1, c_in) for value in (x_lo, x_mid, x_hi)], 0
+        )
         x_kinds = jnp.dot(one_hot(kinds.reshape(-1), cells_in), x_flat, preferred_element_type=F32)
         x_kinds = x_kinds.astype(BF16).reshape(4, rows, c_in)
-        cot = jnp.concatenate(
-            [value.reshape(-1, c_out) for value in (cot_lo, cot_mid, cot_hi)]
-            + [jnp.zeros((rows - cells, c_out), BF16)],
-            0,
-        )
         alive = [
             (jnp.arange(images) < live_counts[0, level]).astype(F32) for level in range(3)
         ]
         mask = jnp.concatenate(
-            [jnp.repeat(alive[level], side * side) for level, side in enumerate(sides)]
+            [jnp.tile(alive[level], side * side) for level, side in enumerate(sides)]
             + [jnp.zeros((rows - cells,), F32)]
         )
-        cell_count = lax.psum(jnp.sum(mask), "narrow")
+        cell_count = tree_sum(link.group_parts(jnp.sum(mask).reshape(1, 1)))
         mask = mask[:, None]
-        recip = (1.0 / cell_count).reshape(1, 1)
-        recip_in = (0.25 / cell_count).reshape(1, 1)
+        recip = 1.0 / cell_count
+        recip_in = 0.25 / cell_count
 
         narrow_all = whole((rows, mid))
         kinds_all = whole((4, rows, mid))
@@ -731,21 +936,9 @@
             [block((1, rows, mid), lambda j: (j, 0, 0)), stat_all],
             [shape_of((4, rows, mid), F32), stat_narrow],
             2 * 4 * rows * c_in * mid,
+            after=[recip],
         )(x_kinds, slim, mask)
         parts_one = link.group_parts(stat)
-        z_side, stat_side = kernel_call(
-            side_kernel,
-            "side",
-            (chunks,),
-            [
-                block((1, rows, c_in), lambda j: (0, 0, 0)),
-                block((c_in, mid), lambda j: (0, j)),
-                mask_all,
-            ],
-            [chunk, stat_chunk(2)],
-            [wide_f32, stat_wide],
-            2 * rows * c_in * c_out,
-        )(x_kinds, broad[mid : mid + c_in], mask)
         act_one, z_two, stat = kernel_call(
             conv_kernel(count, 4, 2),
             "conv_two",
@@ -758,6 +951,22 @@
             flops_conv,
         )(z_one, *parts_one, norm_params, recip_in, mask, shifts, slim)
         parts_two = link.group_parts(stat)
+        z_side, stat_side = kernel_call(
+            side_kernel,
+            "side",
+            (chunks, c_in // mid),
+            [
+                block((1, rows, mid), lambda j, k: (0, 0, k)),
+                block((mid, mid), lambda j, k: (1 + k, j)),
+                whole((rows, 1)),
+            ],
+            [
+                block((rows, mid), lambda j, k: (0, j)),
+                block((2, mid), lambda j, k: (0, j)),
+            ],
+            [wide_f32, stat_wide],
+            2 * rows * c_in * c_out,
+        )(x_kinds, broad, mask)
         act_two, z_three, stat = kernel_call(
             widen_kernel(count, True),
             "widen_three",
@@ -807,17 +1016,31 @@
             flops_wide,
         )(z_five, *parts_five, norm_params, recip, mask, broad)
         parts_six = link.group_parts(stat)
-        y, grad_out, stat = kernel_call(
-            output_kernel(count),
+        grids = [
+            block((side, side, images, mid), lambda j: (0, 0, 0, j)) for side in sides
+        ]
+        *y_grids, grad_out, stat = kernel_call(
+            output_kernel(count, images, sides),
             "output",
             (chunks,),
             [chunk]
             + [stat_chunk(2)] * count
-            + [affine_chunk(6), one_all, mask_all, chunk, chunk],
-            [chunk, chunk, stat_chunk(2)],
-            [wide_low, wide_f32, stat_wide],
+            + [affine_chunk(6), one_all, mask_all, chunk]
+            + grids,
+            grids + [chunk, stat_chunk(2)],
+            [shape_of((side, side, images, c_out), BF16) for side in sides]
+            + [wide_f32, stat_wide],
             flops_wide // 8,
-        )(z_six, *parts_six, norm_params, recip, mask, hidden, cot)
+            scratch=[pltpu.VMEM((rows, mid), F32)],
+        )(
+            z_six,
+            *parts_six,
+            norm_params,
+            recip,
+            mask,
+            hidden,
+            *[by_cell(value) for value in (cot_lo, cot_mid, cot_hi)],
+        )
         sums_six = link.group_parts(stat)
 
         dz_six, grad_five, stat = kernel_call(
@@ -869,28 +1092,30 @@
                 aliases={2: 0} if base is not None else None,
             )(*args)
 
-        def conv_grad(act, dz, stride, out_at, base, name):
+        def conv_grad(act, dz, stride, taps, out_shape, out_at, base, name):
+            first, number = taps
             kinds_here = act.shape[0]
+            specs = [whole((kinds_here, rows, mid)), shifts_all, narrow_all]
+            args = [act, shifts, dz]
+            if base is not None:
+                specs.append(pl.BlockSpec(memory_space=pl.ANY))
+                args.append(base)
             return kernel_call(
-                conv_grad_kernel(stride),
+                conv_grad_kernel(stride, first),
                 name,
-                (9,),
-                [
-                    whole((kinds_here, rows, mid)),
-                    shifts_all,
-                    narrow_all,
-                    pl.BlockSpec(memory_space=pl.ANY),
-                ],
+                (number,),
+                specs,
                 block((mid, mid), lambda t: (out_at + t, 0)),
-                shape_of(base.shape, BF16),
-                flops_conv,
-                aliases={3: 0},
-            )(act, shifts, dz, base)
-
-        half = bounds_slim[-1] // 2
-        quarter = bounds_broad[-1] // 4
-        term_six = weight_grad(act_five, dz_six, (1, chunks), 0, (mid, c_out), 0, None, "grad_six")
-        broad_three = link.scatter(term_six, (1, 1))
+                shape_of(out_shape, BF16),
+                flops_conv * number // 9,
+                aliases={3: 0} if base is not None else None,
+            )(*args)
+
+        slim_part = (bounds_slim[-1] // 4, mid)
+        broad_part = (bounds_broad[-1] // 4, c_out)
+        per_part = slim_part[0] // mid
+        term_six = weight_grad(act_five, dz_six, (1, chunks), 0, broad_part, 0, None, "grad_six")
+        chain_six = Scatter(link, kernel_call, term_six, "sum_six", (1, 1))
 
         dz_five, grad_four, stat = kernel_call(
             back_conv_kernel(count, 1, 1),
@@ -921,6 +1146,12 @@
         )
         grad_four = grad_four[0]
         sums_four = link.group_parts(stat)
+        low_four = 2 * per_part - at_four
+        upper_part = (2 * slim_part[0], mid)
+        term = conv_grad(
+            act_four, dz_five, 1, (0, 9), upper_part, chunks - low_four, None, "grad_five"
+        )
+        chain_six.step()
         dz_four, grad_mid, stat = kernel_call(
             back_mix_kernel(count),
             "back_four",
@@ -950,22 +1181,17 @@
             norm_params,
         )
         sums_pair = link.group_parts(stat)
-        low_four = half // mid - at_four
-        slim_high = weight_grad(
+        term = weight_grad(
             hidden_low,
             dz_four,
             (chunks - low_four, 1),
             low_four,
-            (half, mid),
+            upper_part,
             0,
-            None,
+            term,
             "grad_four",
         )
-        slim_high = conv_grad(
-            act_four, dz_five, 1, at_five - half // mid, slim_high, "grad_five"
-        )
-        slim_high = link.scatter(slim_high, (1,))
-
+        chain_upper = Scatter(link, kernel_call, term, "sum_upper", (1,), True)
         dz_three, dz_side, grad_two, stat = kernel_call(
             back_pair_kernel(count),
             "back_three",
@@ -995,18 +1221,22 @@
             norm_params,
         )
         sums_two = link.group_parts(stat)
+        chain_six.step()
+        chain_upper.step()
         x_sub = x_kinds[0]
-        broad_low = weight_grad(
-            act_two, dz_three, (1, chunks), 0, (2 * quarter, c_out), 0, None, "grad_three"
-        )
-        broad_low = weight_grad(
-            x_sub, dz_side, (1, chunks), 0, (2 * quarter, c_out), 1, broad_low, "grad_side_low"
-        )
-        broad_low = link.scatter(broad_low, (0,))
-        broad_two = weight_grad(
-            x_sub, dz_side, (1, chunks), 1, (quarter, c_out), 0, None, "grad_side_high"
-        )
-        broad_two = link.scatter(broad_two, (0, 1))
+        two_parts = (2 * broad_part[0], c_out)
+        term = weight_grad(
+            act_two, dz_three, (1, chunks), 0, two_parts, 0, None, "grad_three"
+        )
+        term = weight_grad(
+            x_sub, dz_side, (1, chunks), 0, two_parts, 1, term, "grad_side_low"
+        )
+        chain_three = Scatter(link, kernel_call, term, "sum_three", (0,))
+        term = weight_grad(
+            x_sub, dz_side, (1, chunks), 1, broad_part, 0, None, "grad_side_high"
+        )
+        chain_side = Scatter(link, kernel_call, term, "sum_side", (0, 1), True)
+        chain_six.step()
 
         dz_two, grad_one, stat = kernel_call(
             back_conv_kernel(count, 4, 2),
@@ -1036,10 +1266,28 @@
             recip_in,
         )
         sums_one = link.group_parts(stat)
-        slim_low = weight_grad(
-            hidden_low, dz_four, (low_four, 1), 0, (half, mid), at_four, None, "grad_four_low"
-        )
-        slim_low = conv_grad(act_one, dz_two, 2, at_two, slim_low, "grad_two")
+        chain_three.step()
+        chain_side.step()
+        chain_six.step()
+        term = conv_grad(
+            act_one, dz_two, 2, (per_part - at_two, 9 - per_part + at_two), slim_part, 0, None,
+            "grad_two_high",
+        )
+        term = weight_grad(
+            hidden_low, dz_four, (low_four, 1), 0, slim_part, per_part - low_four, term,
+            "grad_four_low",
+        )
+        chain_two = Scatter(link, kernel_call, term, "sum_two", (1, 0), True)
+        half_part = (slim_part[0] // 2, mid)
+        per_half = per_part // 2
+        taps_low = per_half - at_two
+        term = conv_grad(
+            act_one, dz_two, 2, (taps_low, per_half), half_part, 0, None, "grad_two_mid"
+        )
+        chain_mid = Scatter(link, kernel_call, term, "sum_mid", (1, 0, 0))
+        slim_low = conv_grad(
+            act_one, dz_two, 2, (0, taps_low), half_part, at_two, None, "grad_two_low"
+        )
         dz_one, slim_low = kernel_call(
             back_first_kernel(count),
             "back_one",
@@ -1054,51 +1302,96 @@
                 pl.BlockSpec(memory_space=pl.ANY),
             ],
             [block((1, rows, mid), lambda j: (j, 0, 0)), whole((c_in, mid))],
-            [shape_of((4, rows, mid), BF16), shape_of((half, mid), BF16)],
+            [shape_of((4, rows, mid), BF16), shape_of(half_part, BF16)],
             2 * 4 * rows * c_in * mid,
             scratch=[pltpu.VMEM((c_in, mid), F32)],
             aliases={2 + 2 * count + 4: 1},
         )(grad_one, z_one, *parts_one, *sums_one, norm_params, recip_in, mask, x_kinds, slim_low)
-        slim_low = link.scatter(slim_low, (0,))
-
-        back_rows = -np.ones((cells_in,), np.int32)
-        side_rows = -np.ones((cells_in,), np.int32)
-        for kind in range(4):
-            for row in range(cells):
-                back_rows[kinds[kind, row]] = kind * rows + row
-        side_rows[kinds[0, :cells]] = np.arange(cells)
-        dz_natural = jnp.dot(
-            one_hot(back_rows, 4 * rows),
-            dz_one.reshape(4 * rows, mid),
-            preferred_element_type=F32,
-        ).astype(BF16)
-        side_natural = jnp.dot(
-            one_hot(side_rows, rows), dz_side, preferred_element_type=F32
-        ).astype(BF16)
-        grad_x = dot_nt(dz_natural, slim[:c_in]) + dot_nt(side_natural, broad[mid : mid + c_in])
-
-        def split(flat, extents):
-            pieces = []
-            offset = 0
-            for extent in extents:
-                length = images * extent * extent
-                pieces.append(
-                    flat[offset : offset + length].reshape(images, extent, extent, flat.shape[1])
-                )
-                offset += length
-            return pieces
-
-        y_parts = split(y, sides)
-        dx_parts = split(grad_x, tuple(2 * side for side in sides))
+        chain_one = Scatter(link, kernel_call, slim_low, "sum_one", (0, 0, 0))
+        chain_six.step()
+        chain_upper.step()
+        chain_two.step()
+        chain_mid.step()
+        chain_one.step()
+
+        extents = tuple(2 * side for side in sides)
+        dx_grids = kernel_call(
+            input_grad_kernel(images, sides),
+            "input_grad",
+            (c_in // mid,),
+            [
+                kinds_all,
+                slim_block(0),
+                whole((rows, c_out)),
+                block((mid, c_out), lambda j: (1 + j, 0)),
+            ],
+            [
+                block((extent, extent, images, mid), lambda j: (0, 0, 0, j))
+                for extent in extents
+            ],
+            [shape_of((extent, extent, images, c_in), F32) for extent in extents],
+            2 * 4 * rows * c_in * mid + 2 * rows * c_in * c_out,
+            scratch=[pltpu.VMEM((rows, mid), F32)],
+        )(dz_one, slim, dz_side, broad)
+
+        def by_image(value):
+            return jnp.transpose(value, (2, 0, 1, 3))
+
+        y_parts = [by_image(value) for value in y_grids]
+        dx_parts = [by_image(value) for value in dx_grids]
 
         top = link.bit(link.bits - 1)
         second = link.bit(link.bits - 2)
-        slim_grad = jnp.where(top == 1, slim_high, slim_low)
-        broad_grad = jnp.where(
-            top == 0, broad_low, jnp.where(second == 1, broad_three, broad_two)
-        )
-
-        def optimize(grad, master, rowstat, colstat, bounds, name):
+        third = link.bit(link.bits - 3)
+
+        def choose(bit, upper, lower):
+            return jnp.where(bit == 1, upper, lower)
+
+        spans = [
+            (mid * at, mid * at + width, rows_of)
+            for at, width, rows_of in zip(
+                norm_at, widths, ((0, 1),) * 2 + ((0, 1), (2, 1)) + ((0, 1),) * 3
+            )
+        ]
+        sum_sets = [sums_one, sums_two, sums_pair, sums_pair, sums_four, sums_five, sums_six]
+        flat_sets = [part for parts in sum_sets for part in parts]
+        norm_grad = kernel_call(
+            pack_kernel(count, spans),
+            "pack",
+            (1,),
+            [whole(part.shape) for part in flat_sets],
+            whole(norm_params.shape),
+            shape_of(norm_params.shape, F32),
+            1000000,
+        )(*flat_sets)
+        norm_grad = link.total_sum(norm_grad, link.narrow_bits)
+
+        chain_side.step()
+        chain_three.step()
+        chain_upper.step()
+        chain_mid.step()
+        chain_one.step()
+        chain_two.step()
+        chain_side.step()
+        chain_three.step()
+        chain_mid.step()
+        chain_one.step()
+        chain_upper.step()
+        chain_two.step()
+        chain_side.step()
+        chain_three.step()
+        broad_six, broad_three, broad_side = (
+            chain_six.finish(),
+            chain_three.finish(),
+            chain_side.finish(),
+        )
+        broad_grad = choose(top, choose(second, broad_six, broad_side), broad_three)
+        slim_high = chain_upper.finish()
+        slim_mid = chain_two.finish()
+        slim_low = choose(third, chain_mid.finish(), chain_one.finish())
+        slim_grad = choose(top, slim_high, choose(second, slim_mid, slim_low))
+
+        def optimize(grad, master, rowstat, colstat, bounds, name, after):
             height, columns = grad.shape
             levels = len(bounds) - 1
             first = (link.index * height).astype(jnp.int32).reshape(1)
@@ -1113,6 +1406,7 @@
                 [column, sums_all],
                 [shape_of((height, 1), F32), shape_of((4 * levels, columns), F32)],
                 20 * height * columns,
+                after=after,
             )(first, grad, master, rowstat.reshape(height, 1))
             sums = link.total_sum(sums)
             cols_new, new, low = kernel_call(
@@ -1128,27 +1422,20 @@
                 ],
                 20 * height * columns,
             )(first, grad, master, rows_new, sums, colstat)
-            return rows_new.reshape(height), cols_new, new, low
-
-        broad_rows_new, broad_cols_new, broad_new, broad_copy = optimize(
-            broad_grad, broad_master, broad_rowstat, broad_colstat, bounds_broad, "broad"
-        )
-        slim_rows_new, slim_cols_new, slim_new, slim_copy = optimize(
-            slim_grad, slim_master, slim_rowstat, slim_colstat, bounds_slim, "slim"
-        )
-
-        pair = tree_sum(sums_pair)
-        norm_sums = [
-            tree_sum(sums_one),
-            tree_sum(sums_two),
-            pair[0:2],
-            pair[0:3:2],
-            tree_sum(sums_four),
-            tree_sum(sums_five),
-            tree_sum(sums_six),
-        ]
-        norm_grad = jnp.concatenate(norm_sums, 1)[::-1]
-        norm_grad = link.total_sum(norm_grad, link.narrow_bits)
+            return (rows_new.reshape(height), cols_new, new, low), sums
+
+        (broad_rows_new, broad_cols_new, broad_new, broad_copy), sums = optimize(
+            broad_grad, broad_master, broad_rowstat, broad_colstat, bounds_broad, "broad", []
+        )
+        (slim_rows_new, slim_cols_new, slim_new, slim_copy), _ = optimize(
+            slim_grad,
+            slim_master,
+            slim_rowstat,
+            slim_colstat,
+            bounds_slim,
+            "slim",
+            [sums, norm_grad, dx_grids[2]],
+        )
         norm_moments_new = DECAY * norm_moments + (1.0 - DECAY) * (
             norm_grad * norm_grad + EPS_ONE
         )

time: 722 us -> 621 us (0.86)
  local copies, waits for them, and re-layouts: 109 us -> 41.8 us
  Pallas kernels: 125 us -> 176 us
  waiting for transfers between devices: 325 us -> 282 us
  matrix products: 26.4 us -> 5.11 us
  other arithmetic: 29.5 us -> 12.5 us
  blocking collectives: 8.34 us -> 0 us
    ppermute x31 -> x34, waiting for transfers between devices: 151 us -> 78 us  [swap(): return lax.ppermute(value, AXES, pairs)]
    pallas_call x26 -> x72, Pallas kernels: 125 us -> 176 us  [run(): out = call(*args, *after)]
    ppermute x7 -> x14, waiting for transfers between devices: 19.7 us -> 43.4 us  [send_half(): self.came = lax.ppermute(self.kept, AXES, pairs)]
    dot_general x2 -> x0, matrix products: 21.2 us -> none  [dot_nt(): lax.dot_general(first, second, (((1,), (1,)), ((), ())), preferred_elemen...]
    ppermute x36 -> x39, waiting for transfers between devices: 9.24 us -> 30.3 us  [group_parts(): lax.ppermute(value, 'narrow', [(i, i ^ k) for i in range(self.n_narrow)])]
    reshape x15 -> x3, local copies, waits for them, and re-layouts: 22.7 us -> 1.96 us  [body(): by_cell(value).reshape(-1, c_in)]
    slice x8 -> x0, local copies, waits for them, and re-layouts: 19 us -> none  [the longest x6 14.1 us: split(): flat[offset:offset + length].reshape(images, extent, extent, flat.shape[1])]
    ppermute x31 -> x34, starting transfers between devices: 35.3 us -> 20.2 us  [swap(): return lax.ppermute(value, AXES, pairs)]
  transfers between devices with their start and end apart: 76 -> 89, of which waited for: 29 -> 49; matrix products, arithmetic and copies ran while one was open for 19% -> 4% of each run, Pallas kernels for 10% -> 17%
where the time goes in v2:
time: 621 us; the launch traced here: 614 us
  waiting for transfers between devices  282 us (45%)
  Pallas kernels  176 us (28%)
  starting transfers between devices  75.7 us (12%)
  local copies, waits for them, and re-layouts  41.8 us (7%)
  between operations  20.4 us (3%)
  other arithmetic  12.5 us (2%)
    pallas_call x72, Pallas kernels, run(): out = call(*args, *after)  176 us
    ppermute x34, waiting for transfers between devices, swap(): return lax.ppermute(value, AXES, pairs)  78 us
    all_gather x1, waiting for transfers between devices, body(): slim = lax.all_gather(slim_master.astype(BF16), AXES, axis=0, tiled=True)  76.8 us
    all_gather x1, waiting for transfers between devices, body(): broad = lax.all_gather(broad_master.astype(BF16), AXES, axis=0, tiled=True)  53.8 us
    ppermute x14, waiting for transfers between devices, send_half(): self.came = lax.ppermute(self.kept, AXES, pairs)  43.4 us
    unnamed x289, local copies, waits for them, and re-layouts  37.4 us
    ppermute x39, waiting for transfers between devices, group_parts(): lax.ppermute(value, 'narrow', [(i, i ^ k) for i in range(self.n_narrow)])  30.3 us
    ppermute x39, starting transfers between devices, group_parts(): lax.ppermute(value, 'narrow', [(i, i ^ k) for i in range(self.n_narrow)])  28.7 us
  transfers between devices with their start and end apart: 89, of which 49 were waited for; matrix products, arithmetic and copies ran while one was open for 4% of the time, Pallas kernels for 17%

profile of v2, /device:TPU:0, one launch (start us, length us, event | category | flops | bytes accessed | tf_op | source)
XLA Modules:
  0.0 614.0 jit_solution(3748369842492586220)
XLA Ops:
  26.6 5.1 fusion.2
  33.6 76.8 %all-gather.3.cloned.1.call-done.refs_1_.refs_9_.refs_10_.refs_14_.refs_13_ = bf16[12288,512]{1,0:T(8,128)(2,1)} async-done(((bf16[384,512]{1,0:T(8,128)(2,1)}), bf16[12288,512]{1,0:T(8,128)(2,1)}) %all-gather.3.cloned.1.call-update) | async-done | bytes 12582928 | tf_op jit(solution)/shard_map/all_gather | solution.py:869
  122.0 10.8 %conv_two.1 = (bf16[4,320,512]{2,1,0:T(8,128)(2,1)S(1)}, f32[320,512]{1,0:T(8,128)S(1)}, f32[2,512]{1,0:T(2,128)S(1)}) custom-call(f32[4,320,512]{2,1,0:T(8,128)} %copy-done.6, f32[2,512]{1,0:T(2,128)S(1)} %get-tuple-element.104.refs_1_.refs_16_.refs_2_, f32[2,512]{1,0:T(2,128)S(1)} %collective-permute-done.3.refs_2_.refs_17_.refs_3_, ...), custom_call_target="tpu_custom_call" | custom-call | flops 2453667840 | bytes 12268339 | tf_op jit(solution)/shard_map/conv_two/pallas_call | solution.py:76
  135.7 53.8 %all-gather.5.cloned.1.call-done.refs_1_.refs_8_.refs_13_.refs_15_.refs_3_ = bf16[2048,2048]{1,0:T(8,128)(2,1)} async-done(((bf16[64,2048]{1,0:T(8,128)(2,1)}), bf16[2048,2048]{1,0:T(8,128)(2,1)}) %all-gather.5.cloned.1.call-update) | async-done | bytes 8388624 | tf_op jit(solution)/shard_map/all_gather | solution.py:870
  190.9 7.6 %side.1 = (f32[320,2048]{1,0:T(8,128)S(1)}, f32[2,2048]{1,0:T(2,128)S(1)}) custom-call(bf16[4,320,1024]{2,1,0:T(8,128)(2,1)} %bitcast.52, bf16[2048,2048]{1,0:T(8,128)(2,1)} %all-gather.5.cloned.1.call-done.refs_1_.refs_8_.refs_13_.refs_15_.refs_3_, f32[320,1]{1,0:T(8,128)S(1)} %broadcast_in_dim.6.refs_2_.refs_7_.refs_9_.refs_12_.refs_14_, ...), custom_call_target="tpu_custom_call" | custom-call | flops 1342177280 | bytes 6710886 | tf_op jit(solution)/shard_map/side/pallas_call | solution.py:76
  210.6 5.3 mix.1
  222.5 9.0 %conv_five.1 = (bf16[1,320,512]{2,1,0:T(8,128)(2,1)S(1)}, f32[320,512]{1,0:T(8,128)S(1)}, f32[2,512]{1,0:T(2,128)S(1)}) custom-call(f32[1,320,512]{2,1,0:T(8,128)S(1)} %bitcast.55, f32[2,512]{1,0:T(2,128)S(1)} %get-tuple-element.114.refs_1_.refs_16_.refs_2_, f32[2,512]{1,0:T(2,128)S(1)} %collective-permute-done.12.refs_2_.refs_17_.refs_3_, ...), custom_call_target="tpu_custom_call" | custom-call | flops 2453667840 | bytes 12268339 | tf_op jit(solution)/shard_map/conv_five/pallas_call | solution.py:76
  245.6 6.9 %output.1 = (bf16[5,5,2,2048]{3,2,1,0:T(2,128)(2,1)}, bf16[7,7,2,2048]{3,2,1,0:T(2,128)(2,1)}, bf16[9,9,2,2048]{3,2,1,0:T(2,128)(2,1)}, f32[320,2048]{1,0:T(8,128)S(1)}, f32[2,2048]{1,0:T(2,128)S(1)}) custom-call(f32[320,2048]{1,0:T(8,128)} %copy-done.18, f32[2,2048]{1,0:T(2,128)S(1)} %get-tuple-element.120.refs_1_.refs_2_, ...), custom_call_target="tpu_custom_call" | custom-call | flops 83886080 | bytes 419430 | tf_op jit(solution)/shard_map/output/pallas_call | solution.py:76
  280.0 10.5 %back_five.1 = (bf16[320,512]{1,0:T(8,128)(2,1)S(1)}, f32[1,320,512]{2,1,0:T(8,128)S(1)}, f32[2,512]{1,0:T(2,128)S(1)}) custom-call(f32[320,512]{1,0:T(8,128)S(1)} %get-tuple-element.127.refs_0_, f32[320,512]{1,0:T(8,128)S(1)} %copy-done.27, f32[2,512]{1,0:T(2,128)S(1)} %copy-done.82, f32[2,512]{1,0:T(2,128)S(1)} %collective-permute-done.15.refs_2_.refs_16_.refs_3_, ...), custom_call_target="tpu_custom_call" | custom-call | flops 2453667840 | bytes 12268339 | tf_op jit(solution)/shard_map/back_five/pallas_call | solution.py:76
  292.5 7.8 %grad_five.1.refs_5_.refs_2_ = bf16[6144,512]{1,0:T(8,128)(2,1)} custom-call(bf16[1,320,512]{2,1,0:T(8,128)(2,1)S(1)} %get-tuple-element.118.refs_9_.refs_0_, bf16[9,320,320]{2,1,0:T(8,128)(2,1)S(1)} %copy-done.1, bf16[320,512]{1,0:T(8,128)(2,1)S(1)} %get-tuple-element.132.refs_2_.refs_3_, bf16[320,512]{1,0:T(8,128)(2,1)S(1)} %get-tuple-element.132.refs_2_.refs_3_), custom_call_target="tpu_custom_call" | custom-call | flops 2453667840 | bytes 12268339 | tf_op jit(solution)/shard_map/grad_five/pallas_call | solution.py:76
  300.7 6.4 %back_four.1 = (bf16[320,512]{1,0:T(8,128)(2,1)S(1)}, f32[320,2048]{1,0:T(8,128)S(1)}, f32[3,2048]{1,0:T(4,128)S(1)}) custom-call(f32[320,512]{1,0:T(8,128)S(1)} %bitcast.60, f32[320,512]{1,0:T(8,128)S(1)} %copy-done.29, f32[2,512]{1,0:T(2,128)S(1)} %copy-done.106, f32[2,512]{1,0:T(2,128)S(1)} %copy-done.108, f32[2,512]{1,0:T(2,128)S(1)} %copy-done.110, ...), custom_call_target="tpu_custom_call" | custom-call | flops 671088640 | bytes 3355443 | tf_op jit(solution)/shard_map/back_four/pallas_call | solution.py:76
  320.4 9.7 %collective-permute-done.32.refs_9_.refs_10_.refs_14_ = f32[3,2048]{1,0:T(4,128)S(1)} collective-permute-done((f32[3,2048]{1,0:T(4,128)S(1)}, f32[3,2048]{1,0:T(4,128)S(1)}, u32[]{:S(2)}, u32[]{:S(2)}) %collective-permute-start.32) | collective-permute-done | bytes 24608 | tf_op jit(solution)/shard_map/ppermute | solution.py:698
  330.2 6.0 back_three.1
  351.1 5.7 sum_three_0.1.refs_2_
  361.8 6.3 %collective-permute-done.38.refs_2_ = bf16[1,64,2048]{2,1,0:T(8,128)(2,1)S(1)} collective-permute-done((bf16[1,64,2048]{2,1,0:T(8,128)(2,1)S(1)}, bf16[1,64,2048]{2,1,0:T(8,128)(2,1)S(1)}, u32[]{:S(2)}, u32[]{:S(2)}) %collective-permute-start.38) | collective-permute-done | bytes 262176 | tf_op jit(solution)/shard_map/ppermute | solution.py:694
  372.7 13.4 %back_two.1 = (bf16[320,512]{1,0:T(8,128)(2,1)S(1)}, f32[4,320,512]{2,1,0:T(8,128)}, f32[2,512]{1,0:T(2,128)S(1)}) custom-call(f32[320,512]{1,0:T(8,128)S(1)} %copy-done.58, f32[320,512]{1,0:T(8,128)S(1)} %copy-done.25, f32[2,512]{1,0:T(2,128)S(1)} %copy-done.98, f32[2,512]{1,0:T(2,128)S(1)} %copy-done.100, f32[2,512]{1,0:T(2,128)S(1)} %copy-done.102, ...), custom_call_target="tpu_custom_call" | custom-call | flops 2453667840 | bytes 12268339 | tf_op jit(solution)/shard_map/back_two/pallas_call | solution.py:76
  411.2 6.6 %back_one.1 = (bf16[4,320,512]{2,1,0:T(8,128)(2,1)S(1)}, bf16[1536,512]{1,0:T(8,128)(2,1)S(1)}) custom-call(f32[4,320,512]{2,1,0:T(8,128)} %get-tuple-element.146.refs_0_, f32[4,320,512]{2,1,0:T(8,128)} %copy-done.6, f32[2,512]{1,0:T(2,128)S(1)} %copy-done.90, f32[2,512]{1,0:T(2,128)S(1)} %copy-done.92, ...), custom_call_target="tpu_custom_call", output_to_operand_aliasing={{1}: (14, {})} | custom-call | flops 1342177280 | bytes 6710886 | tf_op jit(solution)/shard_map/back_one/pallas_call | solution.py:76
  437.5 6.8 %input_grad.1 = (f32[10,10,2,1024]{3,2,1,0:T(2,128)}, f32[14,14,2,1024]{3,2,1,0:T(2,128)}, f32[18,18,2,1024]{3,2,1,0:T(2,128)}) custom-call(bf16[4,320,512]{2,1,0:T(8,128)(2,1)S(1)} %copy-done.33, bf16[12288,512]{1,0:T(8,128)(2,1)} %all-gather.3.cloned.1.call-done.refs_1_.refs_9_.refs_10_.refs_14_.refs_13_, bf16[320,2048]{1,0:T(8,128)(2,1)S(1)} %copy-done.15, ...), custom_call_target="tpu_custom_call" | custom-call | flops 2684354560 | bytes 13421772 | tf_op jit(solution)/shard_map/input_grad/pallas_call | solution.py:76
  448.1 14.2 %collective-permute-done.51.refs_2_.refs_4_ = bf16[2,384,512]{2,1,0:T(8,128)(2,1)S(1)} collective-permute-done((bf16[2,384,512]{2,1,0:T(8,128)(2,1)S(1)}, bf16[2,384,512]{2,1,0:T(8,128)(2,1)S(1)}, u32[]{:S(2)}, u32[]{:S(2)}) %collective-permute-start.51) | collective-permute-done | bytes 786464 | tf_op jit(solution)/shard_map/ppermute | solution.py:694
  463.7 15.5 %collective-permute-done.56.refs_2_ = bf16[1,384,512]{2,1,0:T(8,128)(2,1)S(1)} collective-permute-done((bf16[1,384,512]{2,1,0:T(8,128)(2,1)}, bf16[1,384,512]{2,1,0:T(8,128)(2,1)S(1)}, u32[]{:S(2)}, u32[]{:S(2)}) %collective-permute-start.56) | collective-permute-done | bytes 393248 | tf_op jit(solution)/shard_map/ppermute | solution.py:694
  505.9 5.5 collective-permute-start.65
  511.4 6.6 %collective-permute-done.67.refs_2_ = bf16[1,64,2048]{2,1,0:T(8,128)(2,1)S(1)} collective-permute-done((bf16[1,64,2048]{2,1,0:T(8,128)(2,1)S(1)}, bf16[1,64,2048]{2,1,0:T(8,128)(2,1)S(1)}, u32[]{:S(2)}, u32[]{:S(2)}) %collective-permute-start.67) | collective-permute-done | bytes 262176 | tf_op jit(solution)/shard_map/ppermute | solution.py:819
  525.9 19.1 %collective-permute-done.72.refs_2_ = bf16[1,384,512]{2,1,0:T(8,128)(2,1)} collective-permute-done((bf16[1,384,512]{2,1,0:T(8,128)(2,1)}, bf16[1,384,512]{2,1,0:T(8,128)(2,1)}, u32[]{:S(2)}, u32[]{:S(2)}) %collective-permute-start.72) | collective-permute-done | bytes 393248 | tf_op jit(solution)/shard_map/ppermute | solution.py:819
  548.5 9.1 %collective-permute-done.73.refs_2_ = bf16[1,384,512]{2,1,0:T(8,128)(2,1)S(1)} collective-permute-done((bf16[1,384,512]{2,1,0:T(8,128)(2,1)S(1)}, bf16[1,384,512]{2,1,0:T(8,128)(2,1)S(1)}, u32[]{:S(2)}, u32[]{:S(2)}) %collective-permute-start.73) | collective-permute-done | bytes 393248 | tf_op jit(solution)/shard_map/ppermute | solution.py:819
  (563 shorter events, 269.1 us)
Async XLA Ops:
  7.2 103.2 %all-gather.3.cloned.1.call-start = ((), (), s32[]{:S(2)}) async-start(), calls=%async_computation | async-start | bytes 12976128 | tf_op jit(solution)/shard_map/all_gather | solution.py:869
  9.4 180.2 %all-gather.5.cloned.1.call-start = ((), (), s32[]{:S(2)}) async-start(), calls=%async_computation.1 | async-start | bytes 8650752 | tf_op jit(solution)/shard_map/all_gather | solution.py:870
  133.8 66.2 %collective-permute-start.6 = (f32[2,512]{1,0:T(2,128)S(1)}, f32[2,512]{1,0:T(2,128)S(1)}, u32[]{:S(2)}, u32[]{:S(2)}) collective-permute-start(f32[2,512]{1,0:T(2,128)S(1)} %get-tuple-element.106.refs_1_.refs_17_.refs_2_), channel_id=1, source_target_pairs={{0,1},{1,0},{2,3},{3,2},{4,5},{5,4},{6,7},{7,6},{8,9},{9,8},{10,11... | collective-permute-start | bytes 12296 | tf_op jit(solution)/shard_map/ppermute | solution.py:698
  134.0 66.1 %collective-permute-start.7 = (f32[2,512]{1,0:T(2,128)S(1)}, f32[2,512]{1,0:T(2,128)S(1)}, u32[]{:S(2)}, u32[]{:S(2)}) collective-permute-start(f32[2,512]{1,0:T(2,128)S(1)} %get-tuple-element.106.refs_1_.refs_17_.refs_2_), channel_id=1, source_target_pairs={{0,2},{1,3},{2,0},{3,1},{4,6},{5,7},{6,4},{7,5},{8,10},{9,11},{10,... | collective-permute-start | bytes 12296 | tf_op jit(solution)/shard_map/ppermute | solution.py:698
  134.7 65.4 %collective-permute-start.8 = (f32[2,512]{1,0:T(2,128)S(1)}, f32[2,512]{1,0:T(2,128)S(1)}, u32[]{:S(2)}, u32[]{:S(2)}) collective-permute-start(f32[2,512]{1,0:T(2,128)S(1)} %get-tuple-element.106.refs_1_.refs_17_.refs_2_), channel_id=1, source_target_pairs={{0,3},{1,2},{2,1},{3,0},{4,7},{5,6},{6,5},{7,4},{8,11},{9,10},{10,... | collective-permute-start | bytes 12296 | tf_op jit(solution)/shard_map/ppermute | solution.py:698
  275.1 25.2 %collective-permute-start.30 = (bf16[4,64,2048]{2,1,0:T(8,128)(2,1)S(1)}, bf16[4,64,2048]{2,1,0:T(8,128)(2,1)S(1)}, u32[]{:S(2)}, u32[]{:S(2)}) collective-permute-start(bf16[4,64,2048]{2,1,0:T(8,128)(2,1)S(1)} %sum_six_0.1.refs_22_), channel_id=1, source_target_pairs={{0,1},{1,0},{2,3},{3,2},{4,5},{5,4},{6,7},{7,6},{8,9},{9,8},{10,11... | collective-permute-start | bytes 3145736 | tf_op jit(solution)/shard_map/ppermute | solution.py:694
  314.7 21.7 %collective-permute-start.39 = (bf16[8,384,512]{2,1,0:T(8,128)(2,1)S(1)}, bf16[8,384,512]{2,1,0:T(8,128)(2,1)}, u32[]{:S(2)}, u32[]{:S(2)}) collective-permute-start(bf16[8,384,512]{2,1,0:T(8,128)(2,1)S(1)} %sum_upper_0.1.refs_22_), channel_id=1, source_target_pairs={{0,1},{1,0},{2,3},{3,2},{4,5},{5,4},{6,7},{7,6},{8,9},{9,8},{10,11... | collective-permute-start | bytes 9437192 | tf_op jit(solution)/shard_map/ppermute | solution.py:694
  315.1 21.2 %collective-permute-start.37 = (bf16[2,64,2048]{2,1,0:T(8,128)(2,1)S(1)}, bf16[2,64,2048]{2,1,0:T(8,128)(2,1)S(1)}, u32[]{:S(2)}, u32[]{:S(2)}) collective-permute-start(bf16[2,64,2048]{2,1,0:T(8,128)(2,1)S(1)} %get-tuple-element.140), channel_id=1, source_target_pairs={{0,2},{1,3},{2,0},{3,1},{4,6},{5,7},{6,4},{7,5},{8,10},{9,11},{10,... | collective-permute-start | bytes 1572872 | tf_op jit(solution)/shard_map/ppermute | solution.py:694
  356.8 29.4 %collective-permute-start.45 = (bf16[8,64,2048]{2,1,0:T(8,128)(2,1)}, bf16[8,64,2048]{2,1,0:T(8,128)(2,1)S(1)}, u32[]{:S(2)}, u32[]{:S(2)}) collective-permute-start(bf16[8,64,2048]{2,1,0:T(8,128)(2,1)} %sum_three_0.1.refs_2_), channel_id=1, source_target_pairs={{0,1},{1,0},{2,3},{3,2},{4,5},{5,4},{6,7},{7,6},{8,9},{9,8},{10,11... | collective-permute-start | bytes 6291464 | tf_op jit(solution)/shard_map/ppermute | solution.py:694
  359.3 29.5 %collective-permute-start.44 = (bf16[4,64,2048]{2,1,0:T(8,128)(2,1)S(1)}, bf16[4,64,2048]{2,1,0:T(8,128)(2,1)S(1)}, u32[]{:S(2)}, u32[]{:S(2)}) collective-permute-start(bf16[4,64,2048]{2,1,0:T(8,128)(2,1)S(1)} %sum_side_0.1.refs_3_), channel_id=1, source_target_pairs={{0,1},{1,0},{2,3},{3,2},{4,5},{5,4},{6,7},{7,6},{8,9},{9,8},{10,11... | collective-permute-start | bytes 3145736 | tf_op jit(solution)/shard_map/ppermute | solution.py:694
  368.2 21.8 %collective-permute-start.43 = (bf16[1,64,2048]{2,1,0:T(8,128)(2,1)S(1)}, bf16[1,64,2048]{2,1,0:T(8,128)(2,1)S(1)}, u32[]{:S(2)}, u32[]{:S(2)}) collective-permute-start(bf16[1,64,2048]{2,1,0:T(8,128)(2,1)S(1)} %sum_six_3.1.refs_22_.refs_1_), channel_id=1, source_target_pairs={{0,8},{1,9},{2,10},{3,11},{4,12},{5,13},{6,14},{7,15},{16,24},{17,... | collective-permute-start | bytes 786440 | tf_op jit(solution)/shard_map/ppermute | solution.py:819
  371.6 49.0 %collective-permute-start.49 = (bf16[4,384,512]{2,1,0:T(8,128)(2,1)}, bf16[4,384,512]{2,1,0:T(8,128)(2,1)S(1)}, u32[]{:S(2)}, u32[]{:S(2)}) collective-permute-start(bf16[4,384,512]{2,1,0:T(8,128)(2,1)} %get-tuple-element.153), channel_id=1, source_target_pairs={{0,4},{1,5},{2,6},{3,7},{4,0},{5,1},{6,2},{7,3},{8,12},{9,13},{10,... | collective-permute-start | bytes 4718600 | tf_op jit(solution)/shard_map/ppermute | solution.py:694
  400.6 22.5 %collective-permute-start.48 = (bf16[4,384,512]{2,1,0:T(8,128)(2,1)}, bf16[4,384,512]{2,1,0:T(8,128)(2,1)S(1)}, u32[]{:S(2)}, u32[]{:S(2)}) collective-permute-start(bf16[4,384,512]{2,1,0:T(8,128)(2,1)} %sum_two_0.1.refs_3_), channel_id=1, source_target_pairs={{0,1},{1,0},{2,3},{3,2},{4,5},{5,4},{6,7},{7,6},{8,9},{9,8},{10,11... | collective-permute-start | bytes 4718600 | tf_op jit(solution)/shard_map/ppermute | solution.py:694
  406.2 19.5 %collective-permute-start.47 = (bf16[2,384,512]{2,1,0:T(8,128)(2,1)}, bf16[2,384,512]{2,1,0:T(8,128)(2,1)}, u32[]{:S(2)}, u32[]{:S(2)}) collective-permute-start(bf16[2,384,512]{2,1,0:T(8,128)(2,1)} %sum_mid_0.1.refs_3_), channel_id=1, source_target_pairs={{0,1},{1,0},{2,3},{3,2},{4,5},{5,4},{6,7},{7,6},{8,9},{9,8},{10,11... | collective-permute-start | bytes 2359304 | tf_op jit(solution)/shard_map/ppermute | solution.py:694
  419.5 27.3 %collective-permute-start.52 = (bf16[4,64,2048]{2,1,0:T(8,128)(2,1)S(1)}, bf16[4,64,2048]{2,1,0:T(8,128)(2,1)S(1)}, u32[]{:S(2)}, u32[]{:S(2)}) collective-permute-start(bf16[4,64,2048]{2,1,0:T(8,128)(2,1)S(1)} %copy-done.133), channel_id=1, source_target_pairs={{0,2},{1,3},{2,0},{3,1},{4,6},{5,7},{6,4},{7,5},{8,10},{9,11},{10,... | collective-permute-start | bytes 3145736 | tf_op jit(solution)/shard_map/ppermute | solution.py:694
  423.1 39.2 %collective-permute-start.51 = (bf16[2,384,512]{2,1,0:T(8,128)(2,1)S(1)}, bf16[2,384,512]{2,1,0:T(8,128)(2,1)S(1)}, u32[]{:S(2)}, u32[]{:S(2)}) collective-permute-start(bf16[2,384,512]{2,1,0:T(8,128)(2,1)S(1)} %get-tuple-element.161), channel_id=1, source_target_pairs={{0,2},{1,3},{2,0},{3,1},{4,6},{5,7},{6,4},{7,5},{8,10},{9,11},{10,... | collective-permute-start | bytes 2359304 | tf_op jit(solution)/shard_map/ppermute | solution.py:694
  425.7 57.9 %collective-permute-start.61 = (bf16[2,384,512]{2,1,0:T(8,128)(2,1)S(1)}, bf16[2,384,512]{2,1,0:T(8,128)(2,1)S(1)}, u32[]{:S(2)}, u32[]{:S(2)}) collective-permute-start(bf16[2,384,512]{2,1,0:T(8,128)(2,1)S(1)} %get-tuple-element.172), channel_id=1, source_target_pairs={{0,4},{1,5},{2,6},{3,7},{4,0},{5,1},{6,2},{7,3},{8,12},{9,13},{10,... | collective-permute-start | bytes 2359304 | tf_op jit(solution)/shard_map/ppermute | solution.py:694
  430.9 51.2 %collective-permute-start.55 = (bf16[1,384,512]{2,1,0:T(8,128)(2,1)}, bf16[1,384,512]{2,1,0:T(8,128)(2,1)S(1)}, u32[]{:S(2)}, u32[]{:S(2)}) collective-permute-start(bf16[1,384,512]{2,1,0:T(8,128)(2,1)} %get-tuple-element.168), channel_id=1, source_target_pairs={{0,2},{1,3},{2,0},{3,1},{4,6},{5,7},{6,4},{7,5},{8,10},{9,11},{10,... | collective-permute-start | bytes 1179656 | tf_op jit(solution)/shard_map/ppermute | solution.py:694
  436.6 42.6 %collective-permute-start.56 = (bf16[1,384,512]{2,1,0:T(8,128)(2,1)}, bf16[1,384,512]{2,1,0:T(8,128)(2,1)S(1)}, u32[]{:S(2)}, u32[]{:S(2)}) collective-permute-start(bf16[1,384,512]{2,1,0:T(8,128)(2,1)} %get-tuple-element.169), channel_id=1, source_target_pairs={{0,2},{1,3},{2,0},{3,1},{4,6},{5,7},{6,4},{7,5},{8,10},{9,11},{10,... | collective-permute-start | bytes 1179656 | tf_op jit(solution)/shard_map/ppermute | solution.py:694
  447.1 38.1 %collective-permute-start.59 = (bf16[2,64,2048]{2,1,0:T(8,128)(2,1)S(1)}, bf16[2,64,2048]{2,1,0:T(8,128)(2,1)S(1)}, u32[]{:S(2)}, u32[]{:S(2)}) collective-permute-start(bf16[2,64,2048]{2,1,0:T(8,128)(2,1)S(1)} %get-tuple-element.170), channel_id=1, source_target_pairs={{0,4},{1,5},{2,6},{3,7},{4,0},{5,1},{6,2},{7,3},{8,12},{9,13},{10,... | collective-permute-start | bytes 1572872 | tf_op jit(solution)/shard_map/ppermute | solution.py:694
  462.3 21.9 %collective-permute-start.60 = (bf16[1,64,2048]{2,1,0:T(8,128)(2,1)S(1)}, bf16[1,64,2048]{2,1,0:T(8,128)(2,1)S(1)}, u32[]{:S(2)}, u32[]{:S(2)}) collective-permute-start(bf16[1,64,2048]{2,1,0:T(8,128)(2,1)S(1)} %get-tuple-element.171), channel_id=1, source_target_pairs={{0,2},{1,3},{2,0},{3,1},{4,6},{5,7},{6,4},{7,5},{8,10},{9,11},{10,... | collective-permute-start | bytes 786440 | tf_op jit(solution)/shard_map/ppermute | solution.py:694
  495.8 23.6 %collective-permute-start.62 = (bf16[1,384,512]{2,1,0:T(8,128)(2,1)S(1)}, bf16[1,384,512]{2,1,0:T(8,128)(2,1)S(1)}, u32[]{:S(2)}, u32[]{:S(2)}) collective-permute-start(bf16[1,384,512]{2,1,0:T(8,128)(2,1)S(1)} %sum_upper_4.1.refs_3_.refs_1_), channel_id=1, source_target_pairs={{0,16},{1,17},{2,18},{3,19},{4,20},{5,21},{6,22},{7,23},{8,24},{9,... | collective-permute-start | bytes 1179656 | tf_op jit(solution)/shard_map/ppermute | solution.py:819
  499.0 20.4 %collective-permute-start.68 = (bf16[1,384,512]{2,1,0:T(8,128)(2,1)S(1)}, bf16[1,384,512]{2,1,0:T(8,128)(2,1)S(1)}, u32[]{:S(2)}, u32[]{:S(2)}) collective-permute-start(bf16[1,384,512]{2,1,0:T(8,128)(2,1)S(1)} %sum_two_3.1.refs_3_.refs_1_), channel_id=1, source_target_pairs={{0,8},{1,9},{2,10},{3,11},{4,12},{5,13},{6,14},{7,15},{16,24},{17,... | collective-permute-start | bytes 1179656 | tf_op jit(solution)/shard_map/ppermute | solution.py:819
  523.3 21.7 %collective-permute-start.72 = (bf16[1,384,512]{2,1,0:T(8,128)(2,1)}, bf16[1,384,512]{2,1,0:T(8,128)(2,1)}, u32[]{:S(2)}, u32[]{:S(2)}) collective-permute-start(bf16[1,384,512]{2,1,0:T(8,128)(2,1)} %sum_one_3.1.refs_3_.refs_1_), channel_id=1, source_target_pairs={{8,0},{9,1},{10,2},{11,3},{24,16},{25,17},{26,18},{27,19}} | collective-permute-start | bytes 1179656 | tf_op jit(solution)/shard_map/ppermute | solution.py:819
  (208 other events, 1904.4 us)
Sparse Core Ops, SparseCore 0:
  11.5 98.8 all-gather.2
  113.8 75.7 all-gather.4

commit v3 on v2

--- a/solution.py
+++ b/solution.py
@@ -28,6 +28,51 @@
 
 def block(dims, place):
     return pl.BlockSpec(dims, place)
+
+
+LENGTHS = dict(
+    first=3.9,
+    conv_two=10.8,
+    side=7.2,
+    widen_three=3.8,
+    mix=5.3,
+    conv_five=8.9,
+    widen_six=3.9,
+    output=6.8,
+    back_six=5.1,
+    grad_six=2.1,
+    back_five=10,
+    grad_five_high=5.5,
+    grad_five_low=3.2,
+    back_four=6.5,
+    grad_four=1.5,
+    back_three=6,
+    grad_three=3,
+    grad_side_low=2.1,
+    grad_side_high=2.1,
+    back_two=13.7,
+    grad_two_high=4.8,
+    grad_four_low=0.5,
+    grad_two_low=4.8,
+    back_one=6.3,
+    input_grad=6.7,
+    sum_six_0=1,
+    sum_five_0=1.8,
+    sum_four_0=2.1,
+    sum_three_0=4.5,
+    sum_side_0=1.5,
+    sum_two_0=2.2,
+    sum_one_0=2,
+    sum_five_1=2.2,
+    sum_four_1=2.7,
+    sum_three_1=3.6,
+    sum_side_1=2,
+    sum_two_1=2.2,
+)
+
+
+def length(name):
+    return LENGTHS.get(name, 1)
 
 
 class Kernels:
@@ -49,6 +94,8 @@
         scalars=0,
     ):
         after = [value for value in (*after, self.last) if value is not None]
+        if aliases:
+            after = []
         taken = scalars + len(in_specs)
 
         def trimmed(*refs):
@@ -66,7 +113,9 @@
             out_shape=out_shape,
             input_output_aliases=aliases or {},
             cost_estimate=pl.CostEstimate(
-                flops=flops, bytes_accessed=flops // 200, transcendentals=0
+                flops=int(length(name) * 1.15e9),
+                bytes_accessed=int(length(name) * 3.6e6),
+                transcendentals=0,
             ),
             compiler_params=pltpu.CompilerParams(vmem_limit_bytes=VMEM_LIMIT),
             name=name,
@@ -584,14 +633,21 @@
     return body
 
 
-def pack_kernel(count, spans):
+def pack_kernel(count, spans, piece):
     def body(*refs):
         out_ref = refs[-1]
-        for which, (start, stop, rows) in enumerate(spans):
+        columns = out_ref.shape[1]
+        high = out_ref.shape[0] // 2
+        for which, (start, width, rows) in enumerate(spans):
             parts = refs[which * count : (which + 1) * count]
             total = tree_sum([part[...] for part in parts])
-            for slot, row in enumerate(rows):
-                out_ref[slot : slot + 1, start:stop] = total[row : row + 1]
+            for offset in range(0, width, piece):
+                line, at = (start + offset) // columns, (start + offset) % columns
+                for slot, row in enumerate(rows):
+                    here = slot * high + line
+                    out_ref[here : here + 1, at : at + piece] = total[
+                        row : row + 1, offset : offset + piece
+                    ]
 
     return body
 
@@ -621,10 +677,13 @@
     ]
 
 
-def tally_kernel(bounds):
+def tally_kernel(bounds, extra):
     levels = len(bounds) - 1
 
-    def body(first_ref, grad_ref, master_ref, old_ref, rows_ref, sums_ref):
+    def body(first_ref, grad_ref, master_ref, old_ref, *rest):
+        rows_ref, sums_ref = rest[-2:]
+        if extra:
+            sums_ref[4 * levels :] = rest[0][...]
         grad = grad_ref[...]
         master = master_ref[...]
         square = grad * grad
@@ -699,10 +758,12 @@
             for k in range(1, self.n_narrow)
         ]
 
-    def total_sum(self, value, first=0):
+    def total_sums(self, value, first=0):
+        sums = []
         for level in range(first, self.bits):
             value = value + self.swap(value, level)
-        return value
+            sums.append(value)
+        return sums
 
 
 def insert_bit(unit, place, bit):
@@ -710,7 +771,7 @@
 
 
 class Scatter:
-    def __init__(self, link, kernels, part, name, prefix=(), swap=False):
+    def __init__(self, link, kernels, part, name, prefix=(), first="narrow"):
         self.link = link
         self.kernels = kernels
         self.name = name
@@ -719,13 +780,18 @@
         units = 1 << self.open_bits
         self.kept = part.reshape(units, part.shape[0] // units, part.shape[1])
         self.left = list(range(self.open_bits))
-        self.levels = list(range(self.open_bits))
-        if swap:
-            self.levels[1], self.levels[2] = self.levels[2], self.levels[1]
-        self.levels += list(range(self.open_bits, link.bits))
+        inner = list(range(1, link.narrow_bits))
+        outer = list(range(link.narrow_bits, link.bits))
+        orders = {
+            "narrow": inner + outer,
+            "wide": outer[:1] + inner + outer[1:],
+            "all_wide": outer + inner,
+        }
+        self.levels = [0] + orders[first]
         self.at = 0
         self.came = None
         self.chosen = None
+        self.after = []
         self.send_half(None)
 
     def place(self, level):
@@ -755,6 +821,7 @@
             [shape] * outs,
             4 * number * self.kept.shape[1] * self.kept.shape[2] * 200,
             scalars=1,
+            after=self.after,
         )(self.link.index.astype(jnp.int32).reshape(1), *args)
         return out
 
@@ -794,7 +861,8 @@
                 )
                 self.kept, self.chosen = kept, None
             self.left.remove(level)
-            self.came = self.link.swap(sent, level)
+            with jax.named_scope(self.name + "_bit" + str(level)):
+                self.came = self.link.swap(sent, level)
         else:
             same = lambda unit, index: unit
             (self.kept,) = self.run(
@@ -816,16 +884,18 @@
                 )
                 if settled and (device >> level) & 1 != self.prefix[level - self.open_bits]:
                     pairs.append((device, device ^ (1 << level)))
-            self.came = lax.ppermute(self.kept, AXES, pairs)
-
-    def step(self, number=1):
-        for _ in range(number):
-            if self.at < len(self.levels):
-                self.at += 1
-                self.send_half(self.came)
+            with jax.named_scope(self.name + "_bit" + str(level)):
+                self.came = lax.ppermute(self.kept, AXES, pairs)
+
+    def step(self, after=()):
+        if self.at < len(self.levels):
+            self.at += 1
+            self.after = list(after)
+            self.send_half(self.came)
 
     def finish(self):
-        self.step(len(self.levels))
+        while self.at < len(self.levels):
+            self.step()
         return self.kept.reshape(self.kept.shape[1:])
 
 
@@ -1115,7 +1185,7 @@
         broad_part = (bounds_broad[-1] // 4, c_out)
         per_part = slim_part[0] // mid
         term_six = weight_grad(act_five, dz_six, (1, chunks), 0, broad_part, 0, None, "grad_six")
-        chain_six = Scatter(link, kernel_call, term_six, "sum_six", (1, 1))
+        chain_six = Scatter(link, kernel_call, term_six, "sum_six", (1, 1), "all_wide")
 
         dz_five, grad_four, stat = kernel_call(
             back_conv_kernel(count, 1, 1),
@@ -1147,11 +1217,15 @@
         grad_four = grad_four[0]
         sums_four = link.group_parts(stat)
         low_four = 2 * per_part - at_four
-        upper_part = (2 * slim_part[0], mid)
+        low_five = 3 * per_part - at_five
+        chain_six.step()
         term = conv_grad(
-            act_four, dz_five, 1, (0, 9), upper_part, chunks - low_four, None, "grad_five"
-        )
-        chain_six.step()
+            act_four, dz_five, 1, (low_five, 9 - low_five), slim_part, 0, None, "grad_five_high"
+        )
+        chain_five = Scatter(link, kernel_call, term, "sum_five", (1, 1), "all_wide")
+        term_four = conv_grad(
+            act_four, dz_five, 1, (0, low_five), slim_part, chunks - low_four, None, "grad_five_low"
+        )
         dz_four, grad_mid, stat = kernel_call(
             back_mix_kernel(count),
             "back_four",
@@ -1181,17 +1255,19 @@
             norm_params,
         )
         sums_pair = link.group_parts(stat)
-        term = weight_grad(
+        chain_five.step()
+        chain_six.step()
+        term_four = weight_grad(
             hidden_low,
             dz_four,
             (chunks - low_four, 1),
             low_four,
-            upper_part,
+            slim_part,
             0,
-            term,
+            term_four,
             "grad_four",
         )
-        chain_upper = Scatter(link, kernel_call, term, "sum_upper", (1,), True)
+        chain_four = Scatter(link, kernel_call, term_four, "sum_four", (0, 1), "all_wide")
         dz_three, dz_side, grad_two, stat = kernel_call(
             back_pair_kernel(count),
             "back_three",
@@ -1221,22 +1297,22 @@
             norm_params,
         )
         sums_two = link.group_parts(stat)
-        chain_six.step()
-        chain_upper.step()
+        chain_four.step()
         x_sub = x_kinds[0]
         two_parts = (2 * broad_part[0], c_out)
+        term_three = weight_grad(
+            act_two, dz_three, (1, chunks), 0, two_parts, 0, None, "grad_three"
+        )
         term = weight_grad(
-            act_two, dz_three, (1, chunks), 0, two_parts, 0, None, "grad_three"
-        )
-        term = weight_grad(
-            x_sub, dz_side, (1, chunks), 0, two_parts, 1, term, "grad_side_low"
-        )
-        chain_three = Scatter(link, kernel_call, term, "sum_three", (0,))
+            x_sub, dz_side, (1, chunks), 0, two_parts, 1, term_three, "grad_side_low"
+        )
+        chain_six.step()
+        chain_three = Scatter(link, kernel_call, term, "sum_three", (0,), "all_wide")
+        chain_five.step()
         term = weight_grad(
             x_sub, dz_side, (1, chunks), 1, broad_part, 0, None, "grad_side_high"
         )
-        chain_side = Scatter(link, kernel_call, term, "sum_side", (0, 1), True)
-        chain_six.step()
+        chain_side = Scatter(link, kernel_call, term, "sum_side", (0, 1), "narrow")
 
         dz_two, grad_one, stat = kernel_call(
             back_conv_kernel(count, 4, 2),
@@ -1267,8 +1343,8 @@
         )
         sums_one = link.group_parts(stat)
         chain_three.step()
-        chain_side.step()
-        chain_six.step()
+        chain_four.step()
+        chain_five.step()
         term = conv_grad(
             act_one, dz_two, 2, (per_part - at_two, 9 - per_part + at_two), slim_part, 0, None,
             "grad_two_high",
@@ -1277,16 +1353,9 @@
             hidden_low, dz_four, (low_four, 1), 0, slim_part, per_part - low_four, term,
             "grad_four_low",
         )
-        chain_two = Scatter(link, kernel_call, term, "sum_two", (1, 0), True)
-        half_part = (slim_part[0] // 2, mid)
-        per_half = per_part // 2
-        taps_low = per_half - at_two
-        term = conv_grad(
-            act_one, dz_two, 2, (taps_low, per_half), half_part, 0, None, "grad_two_mid"
-        )
-        chain_mid = Scatter(link, kernel_call, term, "sum_mid", (1, 0, 0))
+        chain_two = Scatter(link, kernel_call, term, "sum_two", (1, 0), "narrow")
         slim_low = conv_grad(
-            act_one, dz_two, 2, (0, taps_low), half_part, at_two, None, "grad_two_low"
+            act_one, dz_two, 2, (0, per_part - at_two), slim_part, at_two, None, "grad_two_low"
         )
         dz_one, slim_low = kernel_call(
             back_first_kernel(count),
@@ -1302,17 +1371,15 @@
                 pl.BlockSpec(memory_space=pl.ANY),
             ],
             [block((1, rows, mid), lambda j: (j, 0, 0)), whole((c_in, mid))],
-            [shape_of((4, rows, mid), BF16), shape_of(half_part, BF16)],
+            [shape_of((4, rows, mid), BF16), shape_of(slim_part, BF16)],
             2 * 4 * rows * c_in * mid,
             scratch=[pltpu.VMEM((c_in, mid), F32)],
             aliases={2 + 2 * count + 4: 1},
         )(grad_one, z_one, *parts_one, *sums_one, norm_params, recip_in, mask, x_kinds, slim_low)
-        chain_one = Scatter(link, kernel_call, slim_low, "sum_one", (0, 0, 0))
+        chain_one = Scatter(link, kernel_call, slim_low, "sum_one", (0, 0), "wide")
+        chain_side.step()
+        chain_two.step()
         chain_six.step()
-        chain_upper.step()
-        chain_two.step()
-        chain_mid.step()
-        chain_one.step()
 
         extents = tuple(2 * side for side in sides)
         dx_grids = kernel_call(
@@ -1342,78 +1409,48 @@
 
         top = link.bit(link.bits - 1)
         second = link.bit(link.bits - 2)
-        third = link.bit(link.bits - 3)
 
         def choose(bit, upper, lower):
             return jnp.where(bit == 1, upper, lower)
 
-        spans = [
-            (mid * at, mid * at + width, rows_of)
-            for at, width, rows_of in zip(
-                norm_at, widths, ((0, 1),) * 2 + ((0, 1), (2, 1)) + ((0, 1),) * 3
-            )
-        ]
-        sum_sets = [sums_one, sums_two, sums_pair, sums_pair, sums_four, sums_five, sums_six]
-        flat_sets = [part for parts in sum_sets for part in parts]
-        norm_grad = kernel_call(
-            pack_kernel(count, spans),
-            "pack",
-            (1,),
-            [whole(part.shape) for part in flat_sets],
-            whole(norm_params.shape),
-            shape_of(norm_params.shape, F32),
-            1000000,
-        )(*flat_sets)
-        norm_grad = link.total_sum(norm_grad, link.narrow_bits)
-
-        chain_side.step()
-        chain_three.step()
-        chain_upper.step()
-        chain_mid.step()
-        chain_one.step()
-        chain_two.step()
-        chain_side.step()
-        chain_three.step()
-        chain_mid.step()
-        chain_one.step()
-        chain_upper.step()
-        chain_two.step()
-        chain_side.step()
-        chain_three.step()
-        broad_six, broad_three, broad_side = (
-            chain_six.finish(),
-            chain_three.finish(),
-            chain_side.finish(),
-        )
-        broad_grad = choose(top, choose(second, broad_six, broad_side), broad_three)
-        slim_high = chain_upper.finish()
-        slim_mid = chain_two.finish()
-        slim_low = choose(third, chain_mid.finish(), chain_one.finish())
-        slim_grad = choose(top, slim_high, choose(second, slim_mid, slim_low))
-
-        def optimize(grad, master, rowstat, colstat, bounds, name, after):
+        def tally(grad, master, rowstat, bounds, name, after, extra=None):
             height, columns = grad.shape
             levels = len(bounds) - 1
             first = (link.index * height).astype(jnp.int32).reshape(1)
-            scalar = pl.BlockSpec(memory_space=pltpu.SMEM)
+            matrix, column = whole((height, columns)), whole((height, 1))
+            extras = [] if extra is None else [extra]
+            sum_dims = (4 * levels + sum(value.shape[0] for value in extras), columns)
+            rows_new, sums = kernel_call(
+                tally_kernel(bounds, bool(extras)),
+                name,
+                (1,),
+                [pl.BlockSpec(memory_space=pltpu.SMEM), matrix, matrix, column]
+                + [whole(value.shape) for value in extras],
+                [column, whole(sum_dims)],
+                [shape_of((height, 1), F32), shape_of(sum_dims, F32)],
+                20 * height * columns,
+                after=after,
+            )(first, grad, master, rowstat.reshape(height, 1), *extras)
+            return rows_new, link.total_sums(sums)
+
+        def renew(grad, master, rows_new, sums, colstat, bounds, name):
+            height, columns = grad.shape
+            levels = len(bounds) - 1
+            first = (link.index * height).astype(jnp.int32).reshape(1)
             matrix, column = whole((height, columns)), whole((height, 1))
             sums_all, cols_all = whole((4 * levels, columns)), whole((levels, columns))
-            rows_new, sums = kernel_call(
-                tally_kernel(bounds),
-                name + "_tally",
+            return kernel_call(
+                renew_kernel(bounds),
+                name,
                 (1,),
-                [scalar, matrix, matrix, column],
-                [column, sums_all],
-                [shape_of((height, 1), F32), shape_of((4 * levels, columns), F32)],
-                20 * height * columns,
-                after=after,
-            )(first, grad, master, rowstat.reshape(height, 1))
-            sums = link.total_sum(sums)
-            cols_new, new, low = kernel_call(
-                renew_kernel(bounds),
-                name + "_renew",
-                (1,),
-                [scalar, matrix, matrix, column, sums_all, cols_all],
+                [
+                    pl.BlockSpec(memory_space=pltpu.SMEM),
+                    matrix,
+                    matrix,
+                    column,
+                    sums_all,
+                    cols_all,
+                ],
                 [cols_all, matrix, matrix],
                 [
                     shape_of((levels, columns), F32),
@@ -1422,20 +1459,79 @@
                 ],
                 20 * height * columns,
             )(first, grad, master, rows_new, sums, colstat)
-            return (rows_new.reshape(height), cols_new, new, low), sums
-
-        (broad_rows_new, broad_cols_new, broad_new, broad_copy), sums = optimize(
-            broad_grad, broad_master, broad_rowstat, broad_colstat, bounds_broad, "broad", []
-        )
-        (slim_rows_new, slim_cols_new, slim_new, slim_copy), _ = optimize(
+
+        spans = [
+            (mid * at, width, rows_of)
+            for at, width, rows_of in zip(
+                norm_at, widths, ((0, 1),) * 2 + ((0, 1), (2, 1)) + ((0, 1),) * 3
+            )
+        ]
+        sum_sets = [sums_one, sums_two, sums_pair, sums_pair, sums_four, sums_five, sums_six]
+        flat_sets = [part for parts in sum_sets for part in parts]
+        norm_rows = norm_params.size // c_out
+        norm_sums = kernel_call(
+            pack_kernel(count, spans, mid),
+            "pack",
+            (1,),
+            [whole(part.shape) for part in flat_sets],
+            whole((norm_rows, c_out)),
+            shape_of((norm_rows, c_out), F32),
+            1000000,
+        )(*flat_sets)
+
+        chain_one.step()
+        chain_three.step()
+        chain_four.step()
+        chain_five.step()
+        chain_side.step()
+        chain_two.step()
+        chain_one.step()
+        chain_three.step()
+        chain_side.step()
+        chain_four.step()
+        broad_six = chain_six.finish()
+        chain_two.step()
+        chain_one.step()
+        chain_side.step()
+        slim_five = chain_five.finish()
+        chain_three.step()
+        chain_two.step()
+        chain_one.step()
+        broad_side = chain_side.finish()
+        broad_three = chain_three.finish()
+        broad_grad = choose(top, choose(second, broad_six, broad_side), broad_three)
+        broad_rows_new, broad_sums = tally(
+            broad_grad, broad_master, broad_rowstat, bounds_broad, "broad_tally", [], norm_sums
+        )
+        slim_four = chain_four.finish()
+        slim_two = chain_two.finish()
+        slim_one = chain_one.finish()
+        slim_high = choose(second, slim_five, slim_four)
+        slim_low = choose(second, slim_two, slim_one)
+        slim_grad = choose(top, slim_high, slim_low)
+
+        slim_rows_new, slim_sums = tally(
+            slim_grad, slim_master, slim_rowstat, bounds_slim, "slim_tally", []
+        )
+        broad_cols_new, broad_new, broad_copy = renew(
+            broad_grad,
+            broad_master,
+            broad_rows_new,
+            broad_sums[-1][:-norm_rows],
+            broad_colstat,
+            bounds_broad,
+            "broad_renew",
+        )
+        slim_cols_new, slim_new, slim_copy = renew(
             slim_grad,
             slim_master,
-            slim_rowstat,
+            slim_rows_new,
+            slim_sums[-1],
             slim_colstat,
             bounds_slim,
-            "slim",
-            [sums, norm_grad, dx_grids[2]],
-        )
+            "slim_renew",
+        )
+        norm_grad = broad_sums[-1][-norm_rows:].reshape(norm_params.shape) * (1.0 / n_narrow)
         norm_moments_new = DECAY * norm_moments + (1.0 - DECAY) * (
             norm_grad * norm_grad + EPS_ONE
         )
@@ -1449,8 +1545,8 @@
             *dx_parts,
             slim_grad,
             broad_grad,
-            slim_rows_new,
-            broad_rows_new,
+            slim_rows_new.reshape(-1),
+            broad_rows_new.reshape(-1),
             slim_cols_new,
             broad_cols_new,
             slim_new,

time: 621 us -> 581 us (0.936)
  waiting for transfers between devices: 282 us -> 214 us
  starting transfers between devices: 75.7 us -> 86.6 us
  local copies, waits for them, and re-layouts: 41.8 us -> 50.8 us
    ppermute x34 -> x32, waiting for transfers between devices: 78 us -> 48.3 us  [swap(): return lax.ppermute(value, AXES, pairs)]
    ppermute x14 -> x13, waiting for transfers between devices: 43.4 us -> 20.1 us  [send_half(): self.came = lax.ppermute(self.kept, AXES, pairs)]
    ppermute x39, waiting for transfers between devices: 30.3 us -> 15.8 us  [group_parts(): lax.ppermute(value, 'narrow', [(i, i ^ k) for i in range(self.n_narrow)])]
    ppermute x34 -> x32, starting transfers between devices: 20.2 us -> 32.5 us  [swap(): return lax.ppermute(value, AXES, pairs)]
    unnamed x289 -> x322, local copies, waits for them, and re-layouts: 37.4 us -> 45.5 us
    ppermute x14 -> x13, starting transfers between devices: 26.7 us -> 24.6 us  [send_half(): self.came = lax.ppermute(self.kept, AXES, pairs)]
  transfers between devices with their start and end apart: 89 -> 86, of which waited for: 49 -> 32; matrix products, arithmetic and copies ran while one was open for 4% -> 4% of each run, Pallas kernels for 17% -> 25%
where the time goes in v3:
time: 581 us; the launch traced here: 574 us
  waiting for transfers between devices  214 us (37%)
  Pallas kernels  182 us (31%)
  starting transfers between devices  86.6 us (15%)
  local copies, waits for them, and re-layouts  50.8 us (9%)
  between operations  20.6 us (4%)
  other arithmetic  14 us (2%)
    pallas_call x72, Pallas kernels, run(): out = call(*args, *after)  182 us
    all_gather x1, waiting for transfers between devices, body(): slim = lax.all_gather(slim_master.astype(BF16), AXES, axis=0, tiled=True)  75.3 us
    all_gather x1, waiting for transfers between devices, body(): broad = lax.all_gather(broad_master.astype(BF16), AXES, axis=0, tiled=True)  54.8 us
    ppermute x32, waiting for transfers between devices, swap(): return lax.ppermute(value, AXES, pairs)  48.3 us
    unnamed x322, local copies, waits for them, and re-layouts  45.5 us
    ppermute x32, starting transfers between devices, swap(): return lax.ppermute(value, AXES, pairs)  32.5 us
    ppermute x39, starting transfers between devices, group_parts(): lax.ppermute(value, 'narrow', [(i, i ^ k) for i in range(self.n_narrow)])  29.5 us
    ppermute x13, starting transfers between devices, send_half(): self.came = lax.ppermute(self.kept, AXES, pairs)  24.6 us
  transfers between devices with their start and end apart: 86, of which 32 were waited for; matrix products, arithmetic and copies ran while one was open for 4% of the time, Pallas kernels for 25%

profile of v3, /device:TPU:0, one launch (start us, length us, event | category | flops | bytes accessed | tf_op | source)
XLA Modules:
  0.0 573.9 jit_solution(236532335569543126)
XLA Ops:
  17.6 4.3 collective-permute-start.1
  27.7 5.2 fusion.2
  34.8 75.3 %all-gather.3.cloned.1.call-done.refs_1_.refs_9_.refs_10_.refs_14_.refs_13_ = bf16[12288,512]{1,0:T(8,128)(2,1)} async-done(((bf16[384,512]{1,0:T(8,128)(2,1)}), bf16[12288,512]{1,0:T(8,128)(2,1)}) %all-gather.3.cloned.1.call-update) | async-done | bytes 12582928 | tf_op jit(solution)/shard_map/all_gather | solution.py:939
  120.9 10.8 %conv_two.1 = (bf16[4,320,512]{2,1,0:T(8,128)(2,1)S(1)}, f32[320,512]{1,0:T(8,128)S(1)}, f32[2,512]{1,0:T(2,128)S(1)}) custom-call(f32[4,320,512]{2,1,0:T(8,128)} %copy-done.119, f32[2,512]{1,0:T(2,128)S(1)} %get-tuple-element.106.refs_1_.refs_16_.refs_2_, f32[2,512]{1,0:T(2,128)S(1)} %collective-permute-done.3.refs_2_.refs_17_.refs_3_, ...), custom_call_target="tpu_custom_call" | custom-call | flops 12419999744 | bytes 38880000 | tf_op jit(solution)/shard_map/conv_two/pallas_call | solution.py:125
  134.6 54.8 %all-gather.5.cloned.1.call-done.refs_1_.refs_8_.refs_13_.refs_15_.refs_3_ = bf16[2048,2048]{1,0:T(8,128)(2,1)} async-done(((bf16[64,2048]{1,0:T(8,128)(2,1)}), bf16[2048,2048]{1,0:T(8,128)(2,1)}) %all-gather.5.cloned.1.call-update) | async-done | bytes 8388624 | tf_op jit(solution)/shard_map/all_gather | solution.py:940
  190.8 7.6 %side.1 = (f32[320,2048]{1,0:T(8,128)S(1)}, f32[2,2048]{1,0:T(2,128)S(1)}) custom-call(bf16[4,320,1024]{2,1,0:T(8,128)(2,1)} %bitcast.53, bf16[2048,2048]{1,0:T(8,128)(2,1)} %all-gather.5.cloned.1.call-done.refs_1_.refs_8_.refs_13_.refs_15_.refs_3_, f32[320,1]{1,0:T(8,128)S(1)} %copy-done.24, bf16[4,320,512]{2,1,0:T(8,128)(2,1)S(1)} %copy-done.146), custom_call_target="tpu_custom_call" | custom-call | flops 8280000000 | bytes 25920000 | tf_op jit(solution)/shard_map/side/pallas_call | solution.py:125
  210.3 5.3 mix.1
  221.2 9.0 %conv_five.1 = (bf16[1,320,512]{2,1,0:T(8,128)(2,1)S(1)}, f32[320,512]{1,0:T(8,128)S(1)}, f32[2,512]{1,0:T(2,128)S(1)}) custom-call(f32[1,320,512]{2,1,0:T(8,128)S(1)} %bitcast.62, f32[2,512]{1,0:T(2,128)S(1)} %get-tuple-element.116.refs_1_.refs_16_.refs_2_, f32[2,512]{1,0:T(2,128)S(1)} %collective-permute-done.12.refs_2_.refs_17_.refs_3_, ...), custom_call_target="tpu_custom_call" | custom-call | flops 10234999808 | bytes 32040000 | tf_op jit(solution)/shard_map/conv_five/pallas_call | solution.py:125
  244.4 6.9 %output.1 = (bf16[5,5,2,2048]{3,2,1,0:T(2,128)(2,1)}, bf16[7,7,2,2048]{3,2,1,0:T(2,128)(2,1)}, bf16[9,9,2,2048]{3,2,1,0:T(2,128)(2,1)}, f32[320,2048]{1,0:T(8,128)S(1)}, f32[2,2048]{1,0:T(2,128)S(1)}) custom-call(f32[320,2048]{1,0:T(8,128)} %copy-done.134, f32[2,2048]{1,0:T(2,128)S(1)} %get-tuple-element.122.refs_1_.refs_2_, ...), custom_call_target="tpu_custom_call" | custom-call | flops 7820000256 | bytes 24480000 | tf_op jit(solution)/shard_map/output/pallas_call | solution.py:125
  261.2 5.0 back_six.1
  271.5 10.1 %back_five.1 = (bf16[320,512]{1,0:T(8,128)(2,1)S(1)}, f32[1,320,512]{2,1,0:T(8,128)S(1)}, f32[2,512]{1,0:T(2,128)S(1)}) custom-call(f32[320,512]{1,0:T(8,128)S(1)} %get-tuple-element.129.refs_0_, f32[320,512]{1,0:T(8,128)S(1)} %copy-done.143, f32[2,512]{1,0:T(2,128)S(1)} %copy-done.109, f32[2,512]{1,0:T(2,128)S(1)} %collective-permute-done.15.refs_2_.refs_16_.refs_3_, ...), custom_call_target="tpu_custom_call" | custom-call | flops 11500000256 | bytes 36000000 | tf_op jit(solution)/shard_map/back_five/pallas_call | solution.py:125
  285.3 5.5 grad_five_high.1.refs_2_
  298.3 6.4 %back_four.1 = (bf16[320,512]{1,0:T(8,128)(2,1)S(1)}, f32[320,2048]{1,0:T(8,128)S(1)}, f32[3,2048]{1,0:T(4,128)S(1)}) custom-call(f32[320,512]{1,0:T(8,128)S(1)} %bitcast.64, f32[320,512]{1,0:T(8,128)S(1)} %copy-done.114, f32[2,512]{1,0:T(2,128)S(1)} %copy-done.101, f32[2,512]{1,0:T(2,128)S(1)} %copy-done.103, f32[2,512]{1,0:T(2,128)S(1)} %copy-done.105, ...), custom_call_target="tpu_custom_call" | custom-call | flops 7474999808 | bytes 23400000 | tf_op jit(solution)/shard_map/back_four/pallas_call | solution.py:125
  313.6 6.1 %back_three.1 = (bf16[320,2048]{1,0:T(8,128)(2,1)S(1)}, bf16[320,2048]{1,0:T(8,128)(2,1)S(1)}, f32[320,512]{1,0:T(8,128)S(1)}, f32[2,512]{1,0:T(2,128)S(1)}) custom-call(f32[320,2048]{1,0:T(8,128)} %copy-done.128, f32[320,2048]{1,0:T(8,128)} %copy-done.125, f32[320,2048]{1,0:T(8,128)} %copy-done.124, ...), custom_call_target="tpu_custom_call" | custom-call | flops 6899999744 | bytes 21600000 | tf_op jit(solution)/shard_map/back_three/pallas_call | solution.py:125
  345.6 4.1 sum_three_0.1.refs_3_
  360.2 13.6 %back_two.1 = (bf16[320,512]{1,0:T(8,128)(2,1)S(1)}, f32[4,320,512]{2,1,0:T(8,128)}, f32[2,512]{1,0:T(2,128)S(1)}) custom-call(f32[320,512]{1,0:T(8,128)S(1)} %copy-done.141, f32[320,512]{1,0:T(8,128)S(1)} %copy-done.137, f32[2,512]{1,0:T(2,128)S(1)} %copy-done.73, f32[2,512]{1,0:T(2,128)S(1)} %copy-done.75, f32[2,512]{1,0:T(2,128)S(1)} %copy-done.78, ...), custom_call_target="tpu_custom_call" | custom-call | flops 15754999808 | bytes 49320000 | tf_op jit(solution)/shard_map/back_two/pallas_call | solution.py:125
  383.8 4.7 grad_two_high.1.refs_2_
  401.9 7.1 %back_one.1 = (bf16[4,320,512]{2,1,0:T(8,128)(2,1)S(1)}, bf16[3072,512]{1,0:T(8,128)(2,1)}) custom-call(f32[4,320,512]{2,1,0:T(8,128)S(1)} %copy-done.144, f32[4,320,512]{2,1,0:T(8,128)} %copy-done.119, f32[2,512]{1,0:T(2,128)S(1)} %copy-done.65, f32[2,512]{1,0:T(2,128)S(1)} %copy-done.67, ...), custom_call_target="tpu_custom_call", output_to_operand_aliasing={{1}: (14, {})} | custom-call | flops 7245000192 | bytes 22680000 | tf_op jit(solution)/shard_map/back_one/pallas_call | solution.py:125
  424.0 6.8 %input_grad.1 = (f32[10,10,2,1024]{3,2,1,0:T(2,128)}, f32[14,14,2,1024]{3,2,1,0:T(2,128)}, f32[18,18,2,1024]{3,2,1,0:T(2,128)}) custom-call(bf16[4,320,512]{2,1,0:T(8,128)(2,1)S(1)} %copy-done.130, bf16[12288,512]{1,0:T(8,128)(2,1)} %all-gather.3.cloned.1.call-done.refs_1_.refs_9_.refs_10_.refs_14_.refs_13_, ...), custom_call_target="tpu_custom_call" | custom-call | flops 7704999936 | bytes 24120000 | tf_op jit(solution)/shard_map/input_grad/pallas_call | solution.py:125
  435.7 9.0 %collective-permute-done.53.refs_2_.refs_4_ = bf16[4,64,2048]{2,1,0:T(8,128)(2,1)S(1)} collective-permute-done((bf16[4,64,2048]{2,1,0:T(8,128)(2,1)S(1)}, bf16[4,64,2048]{2,1,0:T(8,128)(2,1)S(1)}, u32[]{:S(2)}, u32[]{:S(2)}) %collective-permute-start.53) | collective-permute-done | bytes 1048608 | tf_op jit(solution)/shard_map/sum_three_bit2/ppermute | solution.py:753
  464.4 14.2 %collective-permute-done.58.refs_2_ = bf16[2,64,2048]{2,1,0:T(8,128)(2,1)} collective-permute-done((bf16[2,64,2048]{2,1,0:T(8,128)(2,1)}, bf16[2,64,2048]{2,1,0:T(8,128)(2,1)}, u32[]{:S(2)}, u32[]{:S(2)}) %collective-permute-start.58) | collective-permute-done | bytes 524320 | tf_op jit(solution)/shard_map/sum_three_bit3/ppermute | solution.py:753
  491.3 4.4 collective-permute-start.69
  498.6 18.2 %collective-permute-done.70.refs_2_.refs_4_ = bf16[2,64,2048]{2,1,0:T(8,128)(2,1)S(1)} collective-permute-done((bf16[2,64,2048]{2,1,0:T(8,128)(2,1)S(1)}, bf16[2,64,2048]{2,1,0:T(8,128)(2,1)S(1)}, u32[]{:S(2)}, u32[]{:S(2)}) %collective-permute-start.70) | collective-permute-done | bytes 524320 | tf_op jit(solution)/shard_map/sum_three_bit4/ppermute | solution.py:888
  528.4 5.5 collective-permute-done.80
  (591 shorter events, 253.5 us)
Async XLA Ops:
  7.2 103.0 %all-gather.3.cloned.1.call-start = ((), (), s32[]{:S(2)}) async-start(), calls=%async_computation | async-start | bytes 12976128 | tf_op jit(solution)/shard_map/all_gather | solution.py:939
  9.3 180.2 %all-gather.5.cloned.1.call-start = ((), (), s32[]{:S(2)}) async-start(), calls=%async_computation.1 | async-start | bytes 8650752 | tf_op jit(solution)/shard_map/all_gather | solution.py:940
  132.8 67.1 %collective-permute-start.6 = (f32[2,512]{1,0:T(2,128)S(1)}, f32[2,512]{1,0:T(2,128)S(1)}, u32[]{:S(2)}, u32[]{:S(2)}) collective-permute-start(f32[2,512]{1,0:T(2,128)S(1)} %get-tuple-element.108.refs_1_.refs_17_.refs_2_), channel_id=1, source_target_pairs={{0,1},{1,0},{2,3},{3,2},{4,5},{5,4},{6,7},{7,6},{8,9},{9,8},{10,11... | collective-permute-start | bytes 12296 | tf_op jit(solution)/shard_map/ppermute | solution.py:757
  132.9 66.9 %collective-permute-start.7 = (f32[2,512]{1,0:T(2,128)S(1)}, f32[2,512]{1,0:T(2,128)S(1)}, u32[]{:S(2)}, u32[]{:S(2)}) collective-permute-start(f32[2,512]{1,0:T(2,128)S(1)} %get-tuple-element.108.refs_1_.refs_17_.refs_2_), channel_id=1, source_target_pairs={{0,2},{1,3},{2,0},{3,1},{4,6},{5,7},{6,4},{7,5},{8,10},{9,11},{10,... | collective-permute-start | bytes 12296 | tf_op jit(solution)/shard_map/ppermute | solution.py:757
  133.6 66.3 %collective-permute-start.8 = (f32[2,512]{1,0:T(2,128)S(1)}, f32[2,512]{1,0:T(2,128)S(1)}, u32[]{:S(2)}, u32[]{:S(2)}) collective-permute-start(f32[2,512]{1,0:T(2,128)S(1)} %get-tuple-element.108.refs_1_.refs_17_.refs_2_), channel_id=1, source_target_pairs={{0,3},{1,2},{2,1},{3,0},{4,7},{5,6},{6,5},{7,4},{8,11},{9,10},{10,... | collective-permute-start | bytes 12296 | tf_op jit(solution)/shard_map/ppermute | solution.py:757
  349.7 25.6 %collective-permute-start.47 = (bf16[8,64,2048]{2,1,0:T(8,128)(2,1)S(1)}, bf16[8,64,2048]{2,1,0:T(8,128)(2,1)}, u32[]{:S(2)}, u32[]{:S(2)}) collective-permute-start(bf16[8,64,2048]{2,1,0:T(8,128)(2,1)S(1)} %sum_three_0.1.refs_3_), channel_id=1, source_target_pairs={{0,1},{1,0},{2,3},{3,2},{4,5},{5,4},{6,7},{7,6},{8,9},{9,8},{10,11... | collective-permute-start | bytes 6291464 | tf_op jit(solution)/shard_map/sum_three_bit0/ppermute | solution.py:753
  351.7 28.1 %collective-permute-start.46 = (bf16[2,384,512]{2,1,0:T(8,128)(2,1)}, bf16[2,384,512]{2,1,0:T(8,128)(2,1)}, u32[]{:S(2)}, u32[]{:S(2)}) collective-permute-start(bf16[2,384,512]{2,1,0:T(8,128)(2,1)} %get-tuple-element.151), channel_id=1, source_target_pairs={{0,4},{1,5},{2,6},{3,7},{4,0},{5,1},{6,2},{7,3},{8,12},{9,13},{10,... | collective-permute-start | bytes 2359304 | tf_op jit(solution)/shard_map/sum_four_bit2/ppermute | solution.py:753
  356.9 25.3 %collective-permute-start.45 = (bf16[2,384,512]{2,1,0:T(8,128)(2,1)S(1)}, bf16[2,384,512]{2,1,0:T(8,128)(2,1)S(1)}, u32[]{:S(2)}, u32[]{:S(2)}) collective-permute-start(bf16[2,384,512]{2,1,0:T(8,128)(2,1)S(1)} %sum_five_2.1.refs_2_.refs_1_), channel_id=1, source_target_pairs={{0,8},{1,9},{2,10},{3,11},{4,12},{5,13},{6,14},{7,15},{16,24},{17,... | collective-permute-start | bytes 2359304 | tf_op jit(solution)/shard_map/sum_five_bit3/ppermute | solution.py:888
  373.8 26.4 %collective-permute-start.42 = (f32[2,512]{1,0:T(2,128)S(1)}, f32[2,512]{1,0:T(2,128)S(1)}, u32[]{:S(2)}, u32[]{:S(2)}) collective-permute-start(f32[2,512]{1,0:T(2,128)S(1)} %get-tuple-element.149.refs_6_.refs_0_), channel_id=1, source_target_pairs={{0,1},{1,0},{2,3},{3,2},{4,5},{5,4},{6,7},{7,6},{8,9},{9,8},{10,11... | collective-permute-start | bytes 12296 | tf_op jit(solution)/shard_map/ppermute | solution.py:757
  374.0 26.2 %collective-permute-start.43 = (f32[2,512]{1,0:T(2,128)S(1)}, f32[2,512]{1,0:T(2,128)S(1)}, u32[]{:S(2)}, u32[]{:S(2)}) collective-permute-start(f32[2,512]{1,0:T(2,128)S(1)} %get-tuple-element.149.refs_6_.refs_0_), channel_id=1, source_target_pairs={{0,2},{1,3},{2,0},{3,1},{4,6},{5,7},{6,4},{7,5},{8,10},{9,11},{10,... | collective-permute-start | bytes 12296 | tf_op jit(solution)/shard_map/ppermute | solution.py:757
  375.2 25.0 %collective-permute-start.44 = (f32[2,512]{1,0:T(2,128)S(1)}, f32[2,512]{1,0:T(2,128)S(1)}, u32[]{:S(2)}, u32[]{:S(2)}) collective-permute-start(f32[2,512]{1,0:T(2,128)S(1)} %get-tuple-element.149.refs_6_.refs_0_), channel_id=1, source_target_pairs={{0,3},{1,2},{2,1},{3,0},{4,7},{5,6},{6,5},{7,4},{8,11},{9,10},{10,... | collective-permute-start | bytes 12296 | tf_op jit(solution)/shard_map/ppermute | solution.py:757
  379.8 34.3 %collective-permute-start.50 = (bf16[4,64,2048]{2,1,0:T(8,128)(2,1)}, bf16[4,64,2048]{2,1,0:T(8,128)(2,1)}, u32[]{:S(2)}, u32[]{:S(2)}) collective-permute-start(bf16[4,64,2048]{2,1,0:T(8,128)(2,1)} %sum_side_0.1.refs_22_), channel_id=1, source_target_pairs={{0,1},{1,0},{2,3},{3,2},{4,5},{5,4},{6,7},{7,6},{8,9},{9,8},{10,11... | collective-permute-start | bytes 3145736 | tf_op jit(solution)/shard_map/sum_side_bit0/ppermute | solution.py:753
  412.8 34.0 %collective-permute-start.52 = (bf16[2,384,512]{2,1,0:T(8,128)(2,1)}, bf16[2,384,512]{2,1,0:T(8,128)(2,1)}, u32[]{:S(2)}, u32[]{:S(2)}) collective-permute-start(bf16[2,384,512]{2,1,0:T(8,128)(2,1)} %sum_four_2.1.refs_3_.refs_1_), channel_id=1, source_target_pairs={{8,0},{9,1},{10,2},{11,3},{12,4},{13,5},{14,6},{15,7},{24,16},{25,... | collective-permute-start | bytes 2359304 | tf_op jit(solution)/shard_map/sum_four_bit3/ppermute | solution.py:888
  414.1 37.9 %collective-permute-start.51 = (bf16[2,384,512]{2,1,0:T(8,128)(2,1)}, bf16[2,384,512]{2,1,0:T(8,128)(2,1)}, u32[]{:S(2)}, u32[]{:S(2)}) collective-permute-start(bf16[2,384,512]{2,1,0:T(8,128)(2,1)} %sum_five_3.1.refs_3_.refs_1_), channel_id=1, source_target_pairs={{8,24},{9,25},{10,26},{11,27},{12,28},{13,29},{14,30},{15,31}} | collective-permute-start | bytes 2359304 | tf_op jit(solution)/shard_map/sum_five_bit4/ppermute | solution.py:888
  418.6 26.1 %collective-permute-start.53 = (bf16[4,64,2048]{2,1,0:T(8,128)(2,1)S(1)}, bf16[4,64,2048]{2,1,0:T(8,128)(2,1)S(1)}, u32[]{:S(2)}, u32[]{:S(2)}) collective-permute-start(bf16[4,64,2048]{2,1,0:T(8,128)(2,1)S(1)} %copy-done.30), channel_id=1, source_target_pairs={{0,4},{1,5},{2,6},{3,7},{4,0},{5,1},{6,2},{7,3},{8,12},{9,13},{10,... | collective-permute-start | bytes 3145736 | tf_op jit(solution)/shard_map/sum_three_bit2/ppermute | solution.py:753
  422.2 37.5 %collective-permute-start.60 = (bf16[2,384,512]{2,1,0:T(8,128)(2,1)}, bf16[2,384,512]{2,1,0:T(8,128)(2,1)}, u32[]{:S(2)}, u32[]{:S(2)}) collective-permute-start(bf16[2,384,512]{2,1,0:T(8,128)(2,1)} %get-tuple-element.171), channel_id=1, source_target_pairs={{0,2},{1,3},{2,0},{3,1},{4,6},{5,7},{6,4},{7,5},{8,10},{9,11},{10,... | collective-permute-start | bytes 2359304 | tf_op jit(solution)/shard_map/sum_two_bit1/ppermute | solution.py:753
  434.5 27.5 %collective-permute-start.59 = (bf16[2,384,512]{2,1,0:T(8,128)(2,1)}, bf16[2,384,512]{2,1,0:T(8,128)(2,1)}, u32[]{:S(2)}, u32[]{:S(2)}) collective-permute-start(bf16[2,384,512]{2,1,0:T(8,128)(2,1)} %get-tuple-element.170), channel_id=1, source_target_pairs={{0,4},{1,5},{2,6},{3,7},{4,0},{5,1},{6,2},{7,3},{8,12},{9,13},{10,... | collective-permute-start | bytes 2359304 | tf_op jit(solution)/shard_map/sum_one_bit2/ppermute | solution.py:753
  449.1 32.8 %collective-permute-start.65 = (bf16[2,384,512]{2,1,0:T(8,128)(2,1)S(1)}, bf16[2,384,512]{2,1,0:T(8,128)(2,1)S(1)}, u32[]{:S(2)}, u32[]{:S(2)}) collective-permute-start(bf16[2,384,512]{2,1,0:T(8,128)(2,1)S(1)} %sum_four_3.1.refs_5_.refs_1_.refs_3_), channel_id=1, source_target_pairs={{0,16},{1,17},{2,18},{3,19},{4,20},{5,21},{6,22},{7,23}} | collective-permute-start | bytes 2359304 | tf_op jit(solution)/shard_map/sum_four_bit4/ppermute | solution.py:888
  452.0 26.6 %collective-permute-start.58 = (bf16[2,64,2048]{2,1,0:T(8,128)(2,1)}, bf16[2,64,2048]{2,1,0:T(8,128)(2,1)}, u32[]{:S(2)}, u32[]{:S(2)}) collective-permute-start(bf16[2,64,2048]{2,1,0:T(8,128)(2,1)} %get-tuple-element.169), channel_id=1, source_target_pairs={{0,8},{1,9},{2,10},{3,11},{4,12},{5,13},{6,14},{7,15},{8,0},{9,1},... | collective-permute-start | bytes 1572872 | tf_op jit(solution)/shard_map/sum_three_bit3/ppermute | solution.py:753
  459.7 23.8 %collective-permute-start.64 = (bf16[1,64,2048]{2,1,0:T(8,128)(2,1)S(1)}, bf16[1,64,2048]{2,1,0:T(8,128)(2,1)S(1)}, u32[]{:S(2)}, u32[]{:S(2)}) collective-permute-start(bf16[1,64,2048]{2,1,0:T(8,128)(2,1)S(1)} %copy-done.40), channel_id=1, source_target_pairs={{0,2},{1,3},{2,0},{3,1},{4,6},{5,7},{6,4},{7,5},{8,10},{9,11},{10,... | collective-permute-start | bytes 786440 | tf_op jit(solution)/shard_map/sum_six_bit1/ppermute | solution.py:753
  462.0 35.2 %collective-permute-start.55 = (bf16[1,384,512]{2,1,0:T(8,128)(2,1)S(1)}, bf16[1,384,512]{2,1,0:T(8,128)(2,1)S(1)}, u32[]{:S(2)}, u32[]{:S(2)}) collective-permute-start(bf16[1,384,512]{2,1,0:T(8,128)(2,1)S(1)} %get-tuple-element.165), channel_id=1, source_target_pairs={{0,2},{1,3},{2,0},{3,1},{4,6},{5,7},{6,4},{7,5},{8,10},{9,11},{10,... | collective-permute-start | bytes 1179656 | tf_op jit(solution)/shard_map/sum_five_bit1/ppermute | solution.py:753
  483.6 33.2 %collective-permute-start.70 = (bf16[2,64,2048]{2,1,0:T(8,128)(2,1)S(1)}, bf16[2,64,2048]{2,1,0:T(8,128)(2,1)S(1)}, u32[]{:S(2)}, u32[]{:S(2)}) collective-permute-start(bf16[2,64,2048]{2,1,0:T(8,128)(2,1)S(1)} %sum_three_3.1.refs_3_.refs_1_), channel_id=1, source_target_pairs={{16,0},{17,1},{18,2},{19,3},{20,4},{21,5},{22,6},{23,7},{24,8},{25... | collective-permute-start | bytes 1572872 | tf_op jit(solution)/shard_map/sum_three_bit4/ppermute | solution.py:888
  487.1 40.2 %collective-permute-start.66 = (bf16[1,384,512]{2,1,0:T(8,128)(2,1)S(1)}, bf16[1,384,512]{2,1,0:T(8,128)(2,1)S(1)}, u32[]{:S(2)}, u32[]{:S(2)}) collective-permute-start(bf16[1,384,512]{2,1,0:T(8,128)(2,1)S(1)} %get-tuple-element.178), channel_id=1, source_target_pairs={{0,2},{1,3},{2,0},{3,1},{4,6},{5,7},{6,4},{7,5},{8,10},{9,11},{10,... | collective-permute-start | bytes 1179656 | tf_op jit(solution)/shard_map/sum_four_bit1/ppermute | solution.py:753
  491.3 26.5 %collective-permute-start.69 = (bf16[1,384,512]{2,1,0:T(8,128)(2,1)S(1)}, bf16[1,384,512]{2,1,0:T(8,128)(2,1)S(1)}, u32[]{:S(2)}, u32[]{:S(2)}) collective-permute-start(bf16[1,384,512]{2,1,0:T(8,128)(2,1)S(1)} %sum_two_3.1.refs_3_.refs_1_), channel_id=1, source_target_pairs={{0,8},{1,9},{2,10},{3,11},{4,12},{5,13},{6,14},{7,15},{16,24},{17,... | collective-permute-start | bytes 1179656 | tf_op jit(solution)/shard_map/sum_two_bit3/ppermute | solution.py:888
  (223 other events, 2047.4 us)
Sparse Core Ops, SparseCore 0:
  11.5 98.6 all-gather.2
  113.6 75.8 all-gather.4
